TPU v7x, 128 devices: a whole 4x4x4 slice. The times are simulated.
128 devices in a mesh: east: 4 (over y), north: 16 (over x, z), layer: 2 (over core).
Axes of the slice: x: 4, y: 4, z: 4, core: 2. Of those that a mesh axis runs over, the one named last changes fastest.
Arguments:
- head_old: float32 [8, 2048, 1024], P('layer', 'north', 'east'), may hold values from -6 to 6
- head_target: float32 [8, 2048, 1024], P('layer', 'north', 'east'), may hold values from -12 to 12
- conductivity_east: bfloat16 [8, 2048, 1024], P('layer', 'north', 'east'), may hold values from 0.05 to 6, as said below
- conductivity_north: bfloat16 [8, 2048, 1024], P('layer', 'north', 'east'), may hold values from 0.099609375 to 2
- conductivity_vertical: bfloat16 [8, 2048, 1024], P('layer', 'north', 'east'), may hold values from 0.019897461 to 0.5
- storage: bfloat16 [8, 2048, 1024], P('layer', 'north', 'east'), may hold values from 0.19921875 to 2
- well_east: int32 [3000], replicated, may hold values from 0 to 1023
- well_north: int32 [3000], replicated, may hold values from 0 to 2047
- screen_top: int32 [3000], replicated, may hold values from 0 to 3
- screen_bottom: int32 [3000], replicated, may hold values from 3 to 7
- tariff_band: int32 [3000], replicated, may hold values from 0 to 3
- pump_rates: float32 [3000], replicated, may hold values from 0.2 to 2
- ground_level: float32 [3000], replicated, may hold values from 2 to 6
- band_prices: float32 [4], replicated, may hold values from 0.5 to 4
Outputs:
- head_new: float32 [8, 2048, 1024], P('layer', 'north', 'east')
- adjoint_head: float32 [8, 2048, 1024], P('layer', 'north', 'east')
- rate_gradient: float32 [3000], replicated
- pumping_cost: float32 [], replicated
- misfit: float32 [], replicated
Inputs may be any that keep to these rules, and one draw needn't show every extreme that they name: Every screen spans at least one layer: screen_top <= screen_bottom for each well. `conductivity_east`: conductivity along x, positive.
All inputs are finite; a program needn't handle non-finite values.
Results may differ from a plain program's by a relative error of at most 0.0003.
Values may be sent and summed in bfloat16 or wider, within the bound.
A program may use at most 128 MiB of HBM per device.

v0:
```python
import jax
import jax.numpy as jnp
from jax import lax
from jax.sharding import PartitionSpec as P

SWEEPS = 3


CENTRE = 1.0
HALF_WIDTH = 0.95


def extended(value, sides, width):
    for axis, dim in sides:
        size, length = (lax.axis_size(axis), value.shape[dim])
        up = [(i, (i + 1) % size) for i in range(size - 1)]
        down = [(j, i) for i, j in up]
        last = lax.slice_in_dim(value, length - width, length, axis=dim)
        initial = lax.slice_in_dim(value, 0, width, axis=dim)
        before = lax.ppermute(last, axis, up)
        after = lax.ppermute(initial, axis, down)
        value = jnp.concatenate([before, value, after], axis=dim)
    return value


def harmonic(first, second):
    total = first + second
    return 2.0 * first * second / jnp.where(total > 0, total, 1.0)


def face_terms(east_pad, north_pad, up_pad, stored):
    face_east = harmonic(east_pad[:, :, :-1], east_pad[:, :, 1:])
    face_north = harmonic(north_pad[:, :-1], north_pad[:, 1:])
    face_up = harmonic(up_pad[:-1], up_pad[1:])
    diagonal = stored + face_east[:, :, :-1] + face_east[:, :, 1:]
    diagonal = diagonal + face_north[:, :-1] + face_north[:, 1:]
    diagonal = diagonal + face_up[:-1] + face_up[1:]
    positive = diagonal > 0
    inverse = jnp.where(positive, 1.0 / jnp.where(positive, diagonal, 1.0), 0.0)
    return (stored, face_east, face_north, face_up, inverse)


def coefficients(padded_coefs):
    stacked = padded_coefs.astype(jnp.float32)
    east_pad = stacked[0][1:-1, 1:-1, :]
    north_pad = stacked[1][1:-1, :, 1:-1]
    up_pad = stacked[2][:, 1:-1, 1:-1]
    stored = stacked[3][1:-1, 1:-1, 1:-1]
    return face_terms(east_pad, north_pad, up_pad, stored)


def apply_operator(padded, storage_part, face_east, face_north, face_up):
    center = padded[1:-1, 1:-1, 1:-1]
    step_east = padded[1:-1, 1:-1, 1:] - padded[1:-1, 1:-1, :-1]
    step_north = padded[1:-1, 1:, 1:-1] - padded[1:-1, :-1, 1:-1]
    step_up = padded[1:, 1:-1, 1:-1] - padded[:-1, 1:-1, 1:-1]
    flux_east = face_east * step_east
    flux_north = face_north * step_north
    flux_up = face_up * step_up
    total = storage_part * center + (flux_east[:, :, :-1] - flux_east[:, :, 1:])
    total = total + (flux_north[:, :-1] - flux_north[:, 1:])
    return total + (flux_up[:-1] - flux_up[1:])


def keep_whole(field):
    return field


def chebyshev(start, rhs, operate, trim, precondition):
    if start is None:
        residual = rhs
    else:
        residual = trim(rhs) - operate(start)
    direction = precondition(residual) / CENTRE
    if start is None:
        iterate = direction
    else:
        iterate = trim(start) + direction
    sigma = CENTRE / HALF_WIDTH
    factor = 1.0 / sigma
    for sweep_index in range(SWEEPS - 1):
        residual = trim(residual) - operate(direction)
        factor_next = 1.0 / (2.0 * sigma - factor)
        direction = factor_next * factor * trim(
            direction
        ) + 2.0 * factor_next / HALF_WIDTH * precondition(residual)
        iterate = trim(iterate) + direction
        factor = factor_next
    return iterate


def per_device(
    head_old,
    head_target,
    conductivity_east,
    conductivity_north,
    conductivity_vertical,
    storage,
    well_east,
    well_north,
    screen_top,
    screen_bottom,
    tariff_band,
    pump_rates,
    ground_level,
    band_prices,
):
    depth_cells, north_cells, east_cells = head_old.shape
    stacked_coefs = jnp.stack(
        (conductivity_east, conductivity_north, conductivity_vertical, storage)
    )
    padded_coefs = extended(stacked_coefs, (("east", 3), ("north", 2), ("layer", 1)), 1)
    margin = 0
    top_level = coefficients(padded_coefs)
    levels = [None] * (margin + 1)
    levels[margin] = top_level

    def margin_of(field):
        return (field.shape[0] - depth_cells) // 2

    def precondition(residual):
        return levels[margin_of(residual)][4] * residual

    def operate(field):
        padded = extended(field, (("east", 2), ("north", 1), ("layer", 0)), 1)
        level = levels[0]
        return apply_operator(padded, level[0], level[1], level[2], level[3])

    east_start = lax.axis_index("east") * east_cells
    north_start = lax.axis_index("north") * north_cells
    layer_start = lax.axis_index("layer") * depth_cells
    local_east = well_east - east_start
    local_north = well_north - north_start
    owning = (
        (local_east >= 0)
        & (local_east < east_cells)
        & (local_north >= 0)
        & (local_north < north_cells)
    ).astype(jnp.float32)
    cells = jnp.clip(local_north, 0, north_cells - 1) * east_cells + jnp.clip(
        local_east, 0, east_cells - 1
    )
    depth = layer_start + jnp.arange(depth_cells, dtype=jnp.int32)[:, None]
    screened = ((depth >= screen_top[None, :]) & (depth <= screen_bottom[None, :])).astype(
        jnp.float32
    ) * owning[None, :]
    weights = (
        conductivity_east.reshape(depth_cells, north_cells * east_cells)[:, cells].astype(
            jnp.float32
        )
        * screened
    )
    totals = lax.psum(jnp.sum(weights, axis=0), "layer")
    shares = weights / (totals + (1.0 - owning))[None, :]
    flat_shape = (depth_cells, north_cells * east_cells)
    source = (
        jnp.zeros(flat_shape, jnp.float32)
        .at[:, cells]
        .add(pump_rates[None, :] * shares)
        .reshape(head_old.shape)
    )
    stored = storage.astype(jnp.float32)
    rhs = stored * head_old - source
    head_new = chebyshev(head_old, rhs, operate, keep_whole, precondition)
    departure = head_new - head_target
    misfit_part = jnp.sum(departure * departure)
    all_cells = float(
        depth_cells
        * north_cells
        * east_cells
        * lax.axis_size("east")
        * lax.axis_size("north")
        * lax.axis_size("layer")
    )
    head_part = jnp.sum(shares * head_new.reshape(flat_shape)[:, cells], axis=0)
    head_screen, misfit_total = lax.psum((head_part, misfit_part), ("east", "north", "layer"))
    band_ids = jnp.arange(band_prices.shape[0], dtype=jnp.int32)
    prices = jnp.sum(
        jnp.where(tariff_band[:, None] == band_ids[None, :], band_prices[None, :], 0.0), axis=1
    )
    load = (
        departure.reshape(flat_shape)
        .at[:, cells]
        .add(-(prices * pump_rates)[None, :] * shares)
        .reshape(head_old.shape)
    )
    adjoint_head = chebyshev(None, load, operate, keep_whole, precondition)
    adjoint_part = jnp.sum(shares * adjoint_head.reshape(flat_shape)[:, cells], axis=0)
    adjoint_screen = lax.psum(adjoint_part, ("east", "north", "layer"))
    misfit = misfit_total / all_cells
    lift = ground_level - head_screen
    rate_gradient = prices * lift - adjoint_screen
    pumping_cost = jnp.sum(prices * pump_rates * lift)
    return (head_new, adjoint_head, rate_gradient, pumping_cost, misfit)


def solution(mesh):
    in_specs = (
        P("layer", "north", "east"),
        P("layer", "north", "east"),
        P("layer", "north", "east"),
        P("layer", "north", "east"),
        P("layer", "north", "east"),
        P("layer", "north", "east"),
        P(),
        P(),
        P(),
        P(),
        P(),
        P(),
        P(),
        P(),
    )
    out_specs = (P("layer", "north", "east"), P("layer", "north", "east"), P(), P(), P())
    return jax.shard_map(
        per_device, mesh=mesh, in_specs=in_specs, out_specs=out_specs, check_vma=False
    )
```

profile of v0, /device:TPU:0, one launch (start us, length us, event | category | flops | bytes accessed | tf_op | source)
XLA Modules:
  0.0 415.4 jit_solution(4808711370803003127)
XLA Ops:
  0.6 1.9 fusion.86
  2.5 3.6 collective-permute-start.7
  6.1 1.3 collective-permute-start.6
  7.5 1.4 pad_maximum_fusion.1
  10.0 4.6 %collective-permute-start = (bf16[4,4,128,1]{3,2,1,0:T(8,128)(2,1)}, bf16[4,4,128,1]{3,2,1,0:T(8,128)(2,1)S(1)}, u32[]{:S(2)}, u32[]{:S(2)}) collective-permute-start(bf16[4,4,128,1]{3,2,1,0:T(8,128)(2,1)} %get-tuple-element.52), channel_id=1, source_target_pairs={{0,32},{32,64},{64,96},{1,33},{33,65},{65,97},{2,34},{34,66},{66,9... | collective-permute-start | bytes 12296 | tf_op jit(solution)/shard_map/ppermute | solution.py:20
  14.6 1.3 collective-permute-start.1
  16.0 6.1 %copy.26 = bf16[4,128,256]{0,2,1:T(8,128)(2,1)} copy(bf16[4,128,256]{2,1,0:T(8,128)(2,1)S(1)} %copy-done.7) | data formatting | bytes 524288 | tf_op args[2]
  22.2 13.0 %gather_fusion = bf16[3000,4]{1,0:T(8,128)(2,1)S(1)} fusion(bf16[4,32768]{0,1:T(8,128)(2,1)} %bitcast.53, s32[3072]{0:T(1024)S(1)} %pad_clamp_fusion), kind=kCustom, calls=%fused_computation | custom fusion | bytes 60000 | tf_op jit(solution)/shard_map/gather | solution.py:148
  35.2 2.6 fusion.10
  37.9 3.3 psum.28
  42.2 3.8 collective-permute-start.2
  46.0 1.3 collective-permute-start.3
  47.4 4.5 %collective-permute-start.9 = (f32[4,1,258]{2,1,0:T(1,128)S(1)}, f32[4,1,258]{2,1,0:T(1,128)S(1)}, u32[]{:S(2)}, u32[]{:S(2)}) collective-permute-start(f32[4,1,258]{2,1,0:T(1,128)S(1)} %get-tuple-element.54), channel_id=1, source_target_pairs={{0,2},{2,4},{4,6},{6,8},{8,10},{10,12},{12,14},{14,16},{16,18},{18... | collective-permute-start | bytes 12392 | tf_op jit(solution)/shard_map/ppermute | solution.py:20
  52.0 1.3 collective-permute-start.8
  53.3 3.4 pad_maximum_fusion
  57.7 2.4 collective-permute-start.4
  61.4 26.2 %scatter_custom_fusion = f32[4,32768]{0,1:T(8,128)} fusion(s32[3000]{0:T(1024)S(1)} %compare_select_fusion.5, f32[]{:T(128)} %constant.20.clone.1, f32[3000]{0:T(1024)S(1)} %copy-done.20, bf16[3000,4]{1,0:T(8,128)(2,1)S(1)} %gather_fusion, f32[3000]{0:T(1024)S(1)} %subtract_add_fusion, f32[3000]{0:T(1024)S(1)} %and_convert_fusion, s32[4]{0:T(128)S(1)} %iota_add_fusion, ...), kind=kCustom, calls=%fused_computation.5 | custom fusion | flops 108000 | bytes 1354244 | tf_op jit(solution)/shard_map/scatter-add | solution.py:159
  87.5 10.7 %copy.27 = f32[4,128,256]{2,1,0:T(8,128)} copy(f32[4,128,256]{0,2,1:T(8,128)} %bitcast.50) | data formatting | bytes 1048576 | tf_op jit(solution)/shard_map/reshape | solution.py:160
  98.5 1.3 collective-permute-start.10
  99.8 4.0 collective-permute-start.11
  103.8 5.4 %maximum_convert_fusion = f32[4,6,130,258]{3,2,1,0:T(8,128)S(1)} fusion(bf16[4,1,130,258]{3,2,1,0:T(8,128)(2,1)} %collective-permute-done.5, bf16[4,4,1,258]{3,2,1,0:T(2,128)(2,1)S(1)} %collective-permute-done.3, bf16[4,4,128,1]{3,2,1,0:T(8,128)(2,1)} %collective-permute-done.1, bf16[1,4,128,256]{3,2,1,0:T(8,128)(2,1)S(1)} %bitcast.61, ...), kind=kLoop, calls=%fused_computation.7 | loop fusion | flops 16099200 | bytes 4829760 | tf_op jit(solution)/shard_map/convert_element_type | solution.py:44
  112.7 4.4 %collective-permute-start.13 = (f32[4,128,1]{2,1,0:T(8,128)S(1)}, f32[4,128,1]{2,1,0:T(8,128)S(1)}, u32[]{:S(2)}, u32[]{:S(2)}) collective-permute-start(f32[4,128,1]{2,1,0:T(8,128)S(1)} %get-tuple-element.62), channel_id=1, source_target_pairs={{0,32},{32,64},{64,96},{1,33},{33,65},{65,97},{2,34},{34,66},{66,9... | collective-permute-start | bytes 6152 | tf_op jit(solution)/shard_map/ppermute | solution.py:20
  117.1 1.3 collective-permute-start.12
  118.5 3.6 collective-permute-done.13
  122.1 4.1 collective-permute-done.12
  126.4 4.3 %collective-permute-start.15 = (f32[4,1,258]{2,1,0:T(1,128)S(1)}, f32[4,1,258]{2,1,0:T(1,128)S(1)}, u32[]{:S(2)}, u32[]{:S(2)}) collective-permute-start(f32[4,1,258]{2,1,0:T(1,128)S(1)} %get-tuple-element.50), channel_id=1, source_target_pairs={{0,2},{2,4},{4,6},{6,8},{8,10},{10,12},{12,14},{14,16},{16,18},{18... | collective-permute-start | bytes 12392 | tf_op jit(solution)/shard_map/ppermute | solution.py:20
  130.6 1.3 collective-permute-start.14
  132.3 3.9 collective-permute-done.14
  136.4 1.3 collective-permute-start.16
  137.7 3.1 collective-permute-start.17
  142.8 3.9 collective-permute-start.19
  146.6 1.3 collective-permute-start.18
  147.9 4.7 %collective-permute-done.19 = f32[4,128,1]{2,1,0:T(8,128)S(1)} collective-permute-done((f32[4,128,1]{2,1,0:T(8,128)S(1)}, f32[4,128,1]{2,1,0:T(8,128)S(1)}, u32[]{:S(2)}, u32[]{:S(2)}) %collective-permute-start.19) | collective-permute-done | bytes 2080 | tf_op jit(solution)/shard_map/ppermute | solution.py:20
  152.7 4.1 collective-permute-done.18
  156.9 3.9 collective-permute-start.21
  160.8 1.3 collective-permute-start.20
  162.4 5.7 %collective-permute-done.20 = f32[4,1,258]{2,1,0:T(1,128)S(1)} collective-permute-done((f32[4,1,258]{2,1,0:T(1,128)S(1)}, f32[4,1,258]{2,1,0:T(1,128)S(1)}, u32[]{:S(2)}, u32[]{:S(2)}) %collective-permute-start.20) | collective-permute-done | bytes 4160 | tf_op jit(solution)/shard_map/ppermute | solution.py:21
  168.4 1.3 collective-permute-start.22
  169.7 3.3 collective-permute-start.23
  174.2 2.2 multiply_reduce_fusion
  176.4 9.9 %copy.28 = f32[4,128,256]{0,2,1:T(8,128)} copy(f32[4,128,256]{2,1,0:T(8,128)} %get-tuple-element.11) | data formatting | bytes 1048576 | tf_op jit(solution)/shard_map/sub | solution.py:165
  186.3 31.2 %scatter_custom_fusion.1 = f32[4,32768]{0,1:T(8,128)} fusion(f32[4,32768]{0,1:T(8,128)} %bitcast.48, s32[3000]{0:T(1024)S(1)} %compare_select_fusion.5, f32[3000]{0:T(1024)S(1)} %multiply_negate_fusion, bf16[3000,4]{1,0:T(8,128)(2,1)} %copy-done.4, f32[3000]{0:T(1024)S(1)} %subtract_add_fusion, f32[3000]{0:T(1024)S(1)} %and_convert_fusion, ...), kind=kCustom, calls=%fused_computation.16 | custom fusion | flops 108000 | bytes 1354240 | tf_op jit(solution)/shard_map/scatter-add | solution.py:184
  217.5 10.7 %copy.29 = f32[4,128,256]{2,1,0:T(8,128)} copy(f32[4,128,256]{0,2,1:T(8,128)} %bitcast.49) | data formatting | bytes 1048576 | tf_op jit(solution)/shard_map/reshape | solution.py:185
  229.4 3.5 collective-permute-start.25
  232.9 1.3 collective-permute-start.24
  234.2 4.6 %collective-permute-done.25 = f32[4,128,1]{2,1,0:T(8,128)S(1)} collective-permute-done((f32[4,128,1]{2,1,0:T(8,128)S(1)}, f32[4,128,1]{2,1,0:T(8,128)S(1)}, u32[]{:S(2)}, u32[]{:S(2)}) %collective-permute-start.25) | collective-permute-done | bytes 2080 | tf_op jit(solution)/shard_map/ppermute | solution.py:20
  238.9 4.1 collective-permute-done.24
  243.1 6.0 %collective-permute-start.27 = (f32[4,1,258]{2,1,0:T(1,128)S(1)}, f32[4,1,258]{2,1,0:T(1,128)S(1)}, u32[]{:S(2)}, u32[]{:S(2)}) collective-permute-start(f32[4,1,258]{2,1,0:T(1,128)S(1)} %get-tuple-element.46), channel_id=1, source_target_pairs={{0,2},{2,4},{4,6},{6,8},{8,10},{10,12},{12,14},{14,16},{16,18},{18... | collective-permute-start | bytes 12392 | tf_op jit(solution)/shard_map/ppermute | solution.py:20
  249.2 1.3 collective-permute-start.26
  250.8 3.9 collective-permute-done.26
  256.2 3.1 collective-permute-start.29
  260.7 2.5 multiply_add_fusion
  264.0 2.2 collective-permute-start.31
  266.2 1.3 collective-permute-start.30
  267.5 9.7 %copy.31 = f32[4,128,256]{0,2,1:T(8,128)} copy(f32[4,128,256]{2,1,0:T(8,128)} %get-tuple-element.12) | data formatting | bytes 1048576 | tf_op jit(solution)/shard_map/add | solution.py:87
  277.2 16.6 %gather_fusion.1 = f32[3000,4]{1,0:T(8,128)} fusion(f32[4,32768]{0,1:T(8,128)} %bitcast.52, s32[3072]{0:T(1024)S(1)} %pad_clamp_fusion), kind=kCustom, calls=%fused_computation.1 | custom fusion | bytes 108000 | tf_op jit(solution)/shard_map/gather | solution.py:175
  294.6 4.0 collective-permute-start.33
  301.2 3.0 collective-permute-done.32
  306.6 3.1 collective-permute-start.35
  311.1 1.7 fusion.47
  312.8 8.8 %copy.32 = f32[4,128,256]{0,2,1:T(8,128)} copy(f32[4,128,256]{2,1,0:T(8,128)S(1)} %fusion.47) | data formatting | bytes 1048576 | tf_op jit(solution)/shard_map/add | solution.py:87
  321.6 16.7 %gather_fusion.2 = f32[3000,4]{1,0:T(8,128)} fusion(f32[4,32768]{0,1:T(8,128)} %bitcast.51, s32[3072]{0:T(1024)S(1)} %pad_clamp_fusion), kind=kCustom, calls=%fused_computation.2 | custom fusion | bytes 108000 | tf_op jit(solution)/shard_map/gather | solution.py:188
  338.2 5.9 %fusion.3 = (f32[3000]{0:T(1024)S(1)}, f32[3000]{0:T(1024)S(1)}) fusion(f32[3000,4]{1,0:T(8,128)S(1)} %copy-done.16, f32[3000]{0:T(1024)S(1)} %subtract_add_fusion, f32[3000]{0:T(1024)S(1)} %and_convert_fusion, s32[3000]{0:T(1024)S(1)} %copy-done.18, s32[3000]{0:T(1024)S(1)} %copy-done.19, s32[4]{0:T(128)S(1)} %iota_add_fusion, ...), kind=kLoop, calls=%fused_computation.15 | loop fusion | flops 126000 | bytes 192016 | tf_op jit(solution)/shard_map/reduce_sum | solution.py:175
  344.2 68.2 %all-reduce = (f32[3000]{0:T(1024)S(1)}, f32[3000]{0:T(1024)S(1)}, f32[]{:T(128)}) all-reduce(f32[3000]{0:T(1024)S(1)} %get-tuple-element.6, f32[3000]{0:T(1024)S(1)} %get-tuple-element.5, f32[]{:T(128)} %get-tuple-element.10), channel_id=1, replica_groups=mesh['east'=4,'north'=16,'layer'=2] {'east','north','layer'}, use_global_device_ids=true, to_apply=%region_8.9 | all-reduce | flops 6001 | bytes 48008 | tf_op jit(solution)/shard_map/psum | solution.py:189
  (126 shorter events, 26.6 us)
Async XLA Ops:
  2.5 44.8 %collective-permute-start.7 = (f32[4,128,1]{2,1,0:T(8,128)}, f32[4,128,1]{2,1,0:T(8,128)S(1)}, u32[]{:S(2)}, u32[]{:S(2)}) collective-permute-start(f32[4,128,1]{2,1,0:T(8,128)} %get-tuple-element.64), channel_id=1, source_target_pairs={{0,32},{32,64},{64,96},{1,33},{33,65},{65,97},{2,34},{34,66},{66,9... | collective-permute-start | bytes 6152 | tf_op jit(solution)/shard_map/ppermute | solution.py:20
  6.1 41.2 %collective-permute-start.6 = (f32[4,128,1]{2,1,0:T(8,128)}, f32[4,128,1]{2,1,0:T(8,128)S(1)}, u32[]{:S(2)}, u32[]{:S(2)}) collective-permute-start(f32[4,128,1]{2,1,0:T(8,128)} %get-tuple-element.65), channel_id=1, source_target_pairs={{32,0},{64,32},{96,64},{33,1},{65,33},{97,65},{34,2},{66,34},{98,6... | collective-permute-start | bytes 6152 | tf_op jit(solution)/shard_map/ppermute | solution.py:21
  7.4 8.5 %copy-start.21 = (s32[3000]{0:T(1024)S(1)}, s32[3000]{0:T(1024)}, u32[]{:S(2)}) copy-start(s32[3000]{0:T(1024)} %param.20) | copy-start | bytes 36004
  7.4 8.5 %copy-start.22 = (s32[3000]{0:T(1024)S(1)}, s32[3000]{0:T(1024)}, u32[]{:S(2)}) copy-start(s32[3000]{0:T(1024)} %param.21) | copy-start | bytes 36004
  7.4 8.5 %copy-start.7 = (bf16[4,128,256]{2,1,0:T(8,128)(2,1)S(1)}, bf16[4,128,256]{2,1,0:T(8,128)(2,1)}, u32[]{:S(2)}) copy-start(bf16[4,128,256]{2,1,0:T(8,128)(2,1)} %param.16) | copy-start | bytes 786436
  10.0 31.1 %collective-permute-start = (bf16[4,4,128,1]{3,2,1,0:T(8,128)(2,1)}, bf16[4,4,128,1]{3,2,1,0:T(8,128)(2,1)S(1)}, u32[]{:S(2)}, u32[]{:S(2)}) collective-permute-start(bf16[4,4,128,1]{3,2,1,0:T(8,128)(2,1)} %get-tuple-element.52), channel_id=1, source_target_pairs={{0,32},{32,64},{64,96},{1,33},{33,65},{65,97},{2,34},{34,66},{66,9... | collective-permute-start | bytes 12296 | tf_op jit(solution)/shard_map/ppermute | solution.py:20
  14.6 26.6 %collective-permute-start.1 = (bf16[4,4,128,1]{3,2,1,0:T(8,128)(2,1)}, bf16[4,4,128,1]{3,2,1,0:T(8,128)(2,1)}, u32[]{:S(2)}, u32[]{:S(2)}) collective-permute-start(bf16[4,4,128,1]{3,2,1,0:T(8,128)(2,1)} %get-tuple-element.53), channel_id=1, source_target_pairs={{32,0},{64,32},{96,64},{33,1},{65,33},{97,65},{34,2},{66,34},{98,6... | collective-permute-start | bytes 12296 | tf_op jit(solution)/shard_map/ppermute | solution.py:21
  16.0 19.2 %copy-start.18 = (s32[3000]{0:T(1024)S(1)}, s32[3000]{0:T(1024)}, u32[]{:S(2)}) copy-start(s32[3000]{0:T(1024)} %param.23) | copy-start | bytes 36004
  16.0 19.2 %copy-start.19 = (s32[3000]{0:T(1024)S(1)}, s32[3000]{0:T(1024)}, u32[]{:S(2)}) copy-start(s32[3000]{0:T(1024)} %param.22) | copy-start | bytes 36004
  16.0 25.2 %copy-start.8 = (bf16[4,128,256]{2,1,0:T(8,128)(2,1)S(1)}, bf16[4,128,256]{2,1,0:T(8,128)(2,1)}, u32[]{:S(2)}) copy-start(bf16[4,128,256]{2,1,0:T(8,128)(2,1)} %param.19) | copy-start | bytes 786436
  16.0 25.2 %copy-start.10 = (bf16[4,128,256]{2,1,0:T(8,128)(2,1)S(1)}, bf16[4,128,256]{2,1,0:T(8,128)(2,1)}, u32[]{:S(2)}) copy-start(bf16[4,128,256]{2,1,0:T(8,128)(2,1)} %param.18) | copy-start | bytes 786436
  22.2 25.1 %copy-start = (f32[4,128,256]{2,1,0:T(8,128)S(1)}, f32[4,128,256]{2,1,0:T(8,128)}, u32[]{:S(2)}) copy-start(f32[4,128,256]{2,1,0:T(8,128)} %param.14) | copy-start | bytes 1572868
  35.2 26.1 %copy-start.4 = (bf16[3000,4]{1,0:T(8,128)(2,1)}, bf16[3000,4]{1,0:T(8,128)(2,1)S(1)}, u32[]{:S(2)}) copy-start(bf16[3000,4]{1,0:T(8,128)(2,1)S(1)} %gather_fusion) | copy-start | bytes 72004
  41.2 12.1 %copy-start.11 = (bf16[4,128,256]{2,1,0:T(8,128)(2,1)S(1)}, bf16[4,128,256]{2,1,0:T(8,128)(2,1)}, u32[]{:S(2)}) copy-start(bf16[4,128,256]{2,1,0:T(8,128)(2,1)} %param.17) | copy-start | bytes 786436
  42.2 11.1 %collective-permute-start.2 = (bf16[4,4,1,258]{3,2,1,0:T(2,128)(2,1)S(1)}, bf16[4,4,1,258]{3,2,1,0:T(2,128)(2,1)S(1)}, u32[]{:S(2)}, u32[]{:S(2)}) collective-permute-start(bf16[4,4,1,258]{3,2,1,0:T(2,128)(2,1)S(1)} %get-tuple-element.30), channel_id=1, source_target_pairs={{0,2},{2,4},{4,6},{6,8},{8,10},{10,12},{12,14},{14,16},{16,18},{18... | collective-permute-start | bytes 24776 | tf_op jit(solution)/shard_map/ppermute | solution.py:20
  46.0 7.3 %collective-permute-start.3 = (bf16[4,4,1,258]{3,2,1,0:T(2,128)(2,1)S(1)}, bf16[4,4,1,258]{3,2,1,0:T(2,128)(2,1)S(1)}, u32[]{:S(2)}, u32[]{:S(2)}) collective-permute-start(bf16[4,4,1,258]{3,2,1,0:T(2,128)(2,1)S(1)} %get-tuple-element.31), channel_id=1, source_target_pairs={{2,0},{4,2},{6,4},{8,6},{10,8},{12,10},{14,12},{16,14},{18,16},{20... | collective-permute-start | bytes 24776 | tf_op jit(solution)/shard_map/ppermute | solution.py:21
  47.4 50.8 %collective-permute-start.9 = (f32[4,1,258]{2,1,0:T(1,128)S(1)}, f32[4,1,258]{2,1,0:T(1,128)S(1)}, u32[]{:S(2)}, u32[]{:S(2)}) collective-permute-start(f32[4,1,258]{2,1,0:T(1,128)S(1)} %get-tuple-element.54), channel_id=1, source_target_pairs={{0,2},{2,4},{4,6},{6,8},{8,10},{10,12},{12,14},{14,16},{16,18},{18... | collective-permute-start | bytes 12392 | tf_op jit(solution)/shard_map/ppermute | solution.py:20
  52.0 46.3 %collective-permute-start.8 = (f32[4,1,258]{2,1,0:T(1,128)S(1)}, f32[4,1,258]{2,1,0:T(1,128)S(1)}, u32[]{:S(2)}, u32[]{:S(2)}) collective-permute-start(f32[4,1,258]{2,1,0:T(1,128)S(1)} %get-tuple-element.55), channel_id=1, source_target_pairs={{2,0},{4,2},{6,4},{8,6},{10,8},{12,10},{14,12},{16,14},{18,16},{20... | collective-permute-start | bytes 12392 | tf_op jit(solution)/shard_map/ppermute | solution.py:21
  56.7 4.7 %copy-start.20 = (f32[3000]{0:T(1024)S(1)}, f32[3000]{0:T(1024)}, u32[]{:S(2)}) copy-start(f32[3000]{0:T(1024)} %param.25) | copy-start | bytes 36004
  57.7 46.1 %collective-permute-start.4 = (bf16[4,1,130,258]{3,2,1,0:T(8,128)(2,1)}, bf16[4,1,130,258]{3,2,1,0:T(8,128)(2,1)}, u32[]{:S(2)}, u32[]{:S(2)}) collective-permute-start(bf16[4,1,130,258]{3,2,1,0:T(8,128)(2,1)} %get-tuple-element.32), channel_id=1, source_target_pairs={{0,1},{2,3},{4,5},{6,7},{8,9},{10,11},{12,13},{14,15},{16,17},{18,... | collective-permute-start | bytes 804968 | tf_op jit(solution)/shard_map/ppermute | solution.py:20
  60.0 43.7 %collective-permute-start.5 = (bf16[4,1,130,258]{3,2,1,0:T(8,128)(2,1)}, bf16[4,1,130,258]{3,2,1,0:T(8,128)(2,1)}, u32[]{:S(2)}, u32[]{:S(2)}) collective-permute-start(bf16[4,1,130,258]{3,2,1,0:T(8,128)(2,1)} %get-tuple-element.33), channel_id=1, source_target_pairs={{1,0},{3,2},{5,4},{7,6},{9,8},{11,10},{13,12},{15,14},{17,16},{19,... | collective-permute-start | bytes 804968 | tf_op jit(solution)/shard_map/ppermute | solution.py:21
  87.5 16.3 %copy-start.12 = (bf16[4,128,256]{2,1,0:T(8,128)(2,1)S(1)}, bf16[4,128,256]{2,1,0:T(8,128)(2,1)}, u32[]{:S(2)}) copy-start(bf16[4,128,256]{2,1,0:T(8,128)(2,1)} %param.17) | copy-start | bytes 786436
  98.5 12.2 %collective-permute-start.10 = (f32[1,130,258]{2,1,0:T(8,128)S(1)}, f32[1,130,258]{2,1,0:T(8,128)S(1)}, u32[]{:S(2)}, u32[]{:S(2)}) collective-permute-start(f32[1,130,258]{2,1,0:T(8,128)S(1)} %get-tuple-element.42), channel_id=1, source_target_pairs={{1,0},{3,2},{5,4},{7,6},{9,8},{11,10},{13,12},{15,14},{17,16},{19,... | collective-permute-start | bytes 402488 | tf_op jit(solution)/shard_map/ppermute | solution.py:21
  99.8 10.9 %collective-permute-start.11 = (f32[1,130,258]{2,1,0:T(8,128)S(1)}, f32[1,130,258]{2,1,0:T(8,128)S(1)}, u32[]{:S(2)}, u32[]{:S(2)}) collective-permute-start(f32[1,130,258]{2,1,0:T(8,128)S(1)} %get-tuple-element.43), channel_id=1, source_target_pairs={{0,1},{2,3},{4,5},{6,7},{8,9},{10,11},{12,13},{14,15},{16,17},{18,... | collective-permute-start | bytes 402488 | tf_op jit(solution)/shard_map/ppermute | solution.py:20
  109.6 64.5 %copy-start.6 = (f32[6,130,258]{2,1,0:T(8,128)}, f32[6,130,258]{2,1,0:T(8,128)S(1)}, u32[]{:S(2)}) copy-start(f32[6,130,258]{2,1,0:T(8,128)S(1)} %get-tuple-element.26) | copy-start | bytes 2414884
  110.7 1.0 copy-start.13
  111.7 6.6 %copy-start.24 = (s32[3000]{0:T(1024)S(1)}, s32[3000]{0:T(1024)}, u32[]{:S(2)}) copy-start(s32[3000]{0:T(1024)} %param.24) | copy-start | bytes 36004
  111.7 6.6 %copy-start.25 = (f32[4]{0:T(128)S(1)}, f32[4]{0:T(128)}, u32[]{:S(2)}) copy-start(f32[4]{0:T(128)} %param.27) | copy-start | bytes 52
  112.5 115.7 %copy-start.1 = (f32[4,128,256]{2,1,0:T(8,128)}, f32[4,128,256]{2,1,0:T(8,128)S(1)}, u32[]{:S(2)}) copy-start(f32[4,128,256]{2,1,0:T(8,128)S(1)} %get-tuple-element.19) | copy-start | bytes 1572868
  112.7 9.5 %collective-permute-start.13 = (f32[4,128,1]{2,1,0:T(8,128)S(1)}, f32[4,128,1]{2,1,0:T(8,128)S(1)}, u32[]{:S(2)}, u32[]{:S(2)}) collective-permute-start(f32[4,128,1]{2,1,0:T(8,128)S(1)} %get-tuple-element.62), channel_id=1, source_target_pairs={{0,32},{32,64},{64,96},{1,33},{33,65},{65,97},{2,34},{34,66},{66,9... | collective-permute-start | bytes 6152 | tf_op jit(solution)/shard_map/ppermute | solution.py:20
  117.1 9.2 %collective-permute-start.12 = (f32[4,128,1]{2,1,0:T(8,128)S(1)}, f32[4,128,1]{2,1,0:T(8,128)S(1)}, u32[]{:S(2)}, u32[]{:S(2)}) collective-permute-start(f32[4,128,1]{2,1,0:T(8,128)S(1)} %get-tuple-element.63), channel_id=1, source_target_pairs={{32,0},{64,32},{96,64},{33,1},{65,33},{97,65},{34,2},{66,34},{98,6... | collective-permute-start | bytes 6152 | tf_op jit(solution)/shard_map/ppermute | solution.py:21
  126.4 5.9 %collective-permute-start.15 = (f32[4,1,258]{2,1,0:T(1,128)S(1)}, f32[4,1,258]{2,1,0:T(1,128)S(1)}, u32[]{:S(2)}, u32[]{:S(2)}) collective-permute-start(f32[4,1,258]{2,1,0:T(1,128)S(1)} %get-tuple-element.50), channel_id=1, source_target_pairs={{0,2},{2,4},{4,6},{6,8},{8,10},{10,12},{12,14},{14,16},{16,18},{18... | collective-permute-start | bytes 12392 | tf_op jit(solution)/shard_map/ppermute | solution.py:20
  130.6 5.5 %collective-permute-start.14 = (f32[4,1,258]{2,1,0:T(1,128)S(1)}, f32[4,1,258]{2,1,0:T(1,128)S(1)}, u32[]{:S(2)}, u32[]{:S(2)}) collective-permute-start(f32[4,1,258]{2,1,0:T(1,128)S(1)} %get-tuple-element.51), channel_id=1, source_target_pairs={{2,0},{4,2},{6,4},{8,6},{10,8},{12,10},{14,12},{16,14},{18,16},{20... | collective-permute-start | bytes 12392 | tf_op jit(solution)/shard_map/ppermute | solution.py:21
  136.4 4.6 %collective-permute-start.16 = (f32[1,130,258]{2,1,0:T(8,128)S(1)}, f32[1,130,258]{2,1,0:T(8,128)S(1)}, u32[]{:S(2)}, u32[]{:S(2)}) collective-permute-start(f32[1,130,258]{2,1,0:T(8,128)S(1)} %get-tuple-element.40), channel_id=1, source_target_pairs={{1,0},{3,2},{5,4},{7,6},{9,8},{11,10},{13,12},{15,14},{17,16},{19,... | collective-permute-start | bytes 402488 | tf_op jit(solution)/shard_map/ppermute | solution.py:21
  137.7 4.1 collective-permute-start.17
  142.8 9.9 %collective-permute-start.19 = (f32[4,128,1]{2,1,0:T(8,128)S(1)}, f32[4,128,1]{2,1,0:T(8,128)S(1)}, u32[]{:S(2)}, u32[]{:S(2)}) collective-permute-start(f32[4,128,1]{2,1,0:T(8,128)S(1)} %get-tuple-element.60), channel_id=1, source_target_pairs={{0,32},{32,64},{64,96},{1,33},{33,65},{65,97},{2,34},{34,66},{66,9... | collective-permute-start | bytes 6152 | tf_op jit(solution)/shard_map/ppermute | solution.py:20
  146.6 10.2 %collective-permute-start.18 = (f32[4,128,1]{2,1,0:T(8,128)S(1)}, f32[4,128,1]{2,1,0:T(8,128)S(1)}, u32[]{:S(2)}, u32[]{:S(2)}) collective-permute-start(f32[4,128,1]{2,1,0:T(8,128)S(1)} %get-tuple-element.61), channel_id=1, source_target_pairs={{32,0},{64,32},{96,64},{33,1},{65,33},{97,65},{34,2},{66,34},{98,6... | collective-permute-start | bytes 6152 | tf_op jit(solution)/shard_map/ppermute | solution.py:21
  156.9 5.5 %collective-permute-start.21 = (f32[4,1,258]{2,1,0:T(1,128)S(1)}, f32[4,1,258]{2,1,0:T(1,128)S(1)}, u32[]{:S(2)}, u32[]{:S(2)}) collective-permute-start(f32[4,1,258]{2,1,0:T(1,128)S(1)} %get-tuple-element.48), channel_id=1, source_target_pairs={{0,2},{2,4},{4,6},{6,8},{8,10},{10,12},{12,14},{14,16},{16,18},{18... | collective-permute-start | bytes 12392 | tf_op jit(solution)/shard_map/ppermute | solution.py:20
  160.8 7.4 %collective-permute-start.20 = (f32[4,1,258]{2,1,0:T(1,128)S(1)}, f32[4,1,258]{2,1,0:T(1,128)S(1)}, u32[]{:S(2)}, u32[]{:S(2)}) collective-permute-start(f32[4,1,258]{2,1,0:T(1,128)S(1)} %get-tuple-element.49), channel_id=1, source_target_pairs={{2,0},{4,2},{6,4},{8,6},{10,8},{12,10},{14,12},{16,14},{18,16},{20... | collective-permute-start | bytes 12392 | tf_op jit(solution)/shard_map/ppermute | solution.py:21
  168.4 4.8 %collective-permute-start.22 = (f32[1,130,258]{2,1,0:T(8,128)S(1)}, f32[1,130,258]{2,1,0:T(8,128)S(1)}, u32[]{:S(2)}, u32[]{:S(2)}) collective-permute-start(f32[1,130,258]{2,1,0:T(8,128)S(1)} %get-tuple-element.38), channel_id=1, source_target_pairs={{1,0},{3,2},{5,4},{7,6},{9,8},{11,10},{13,12},{15,14},{17,16},{19,... | collective-permute-start | bytes 402488 | tf_op jit(solution)/shard_map/ppermute | solution.py:21
  169.7 4.1 collective-permute-start.23
  173.2 1.0 copy-start.17
  229.4 9.5 %collective-permute-start.25 = (f32[4,128,1]{2,1,0:T(8,128)S(1)}, f32[4,128,1]{2,1,0:T(8,128)S(1)}, u32[]{:S(2)}, u32[]{:S(2)}) collective-permute-start(f32[4,128,1]{2,1,0:T(8,128)S(1)} %get-tuple-element.58), channel_id=1, source_target_pairs={{0,32},{32,64},{64,96},{1,33},{33,65},{65,97},{2,34},{34,66},{66,9... | collective-permute-start | bytes 6152 | tf_op jit(solution)/shard_map/ppermute | solution.py:20
  232.9 10.1 %collective-permute-start.24 = (f32[4,128,1]{2,1,0:T(8,128)S(1)}, f32[4,128,1]{2,1,0:T(8,128)S(1)}, u32[]{:S(2)}, u32[]{:S(2)}) collective-permute-start(f32[4,128,1]{2,1,0:T(8,128)S(1)} %get-tuple-element.59), channel_id=1, source_target_pairs={{32,0},{64,32},{96,64},{33,1},{65,33},{97,65},{34,2},{66,34},{98,6... | collective-permute-start | bytes 6152 | tf_op jit(solution)/shard_map/ppermute | solution.py:21
  243.1 7.6 %collective-permute-start.27 = (f32[4,1,258]{2,1,0:T(1,128)S(1)}, f32[4,1,258]{2,1,0:T(1,128)S(1)}, u32[]{:S(2)}, u32[]{:S(2)}) collective-permute-start(f32[4,1,258]{2,1,0:T(1,128)S(1)} %get-tuple-element.46), channel_id=1, source_target_pairs={{0,2},{2,4},{4,6},{6,8},{8,10},{10,12},{12,14},{14,16},{16,18},{18... | collective-permute-start | bytes 12392 | tf_op jit(solution)/shard_map/ppermute | solution.py:20
  249.2 5.5 %collective-permute-start.26 = (f32[4,1,258]{2,1,0:T(1,128)S(1)}, f32[4,1,258]{2,1,0:T(1,128)S(1)}, u32[]{:S(2)}, u32[]{:S(2)}) collective-permute-start(f32[4,1,258]{2,1,0:T(1,128)S(1)} %get-tuple-element.47), channel_id=1, source_target_pairs={{2,0},{4,2},{6,4},{8,6},{10,8},{12,10},{14,12},{16,14},{18,16},{20... | collective-permute-start | bytes 12392 | tf_op jit(solution)/shard_map/ppermute | solution.py:21
  254.9 4.6 %collective-permute-start.28 = (f32[1,130,258]{2,1,0:T(8,128)S(1)}, f32[1,130,258]{2,1,0:T(8,128)S(1)}, u32[]{:S(2)}, u32[]{:S(2)}) collective-permute-start(f32[1,130,258]{2,1,0:T(8,128)S(1)} %get-tuple-element.36), channel_id=1, source_target_pairs={{1,0},{3,2},{5,4},{7,6},{9,8},{11,10},{13,12},{15,14},{17,16},{19,... | collective-permute-start | bytes 402488 | tf_op jit(solution)/shard_map/ppermute | solution.py:21
  256.2 4.1 collective-permute-start.29
  259.5 1.1 copy-start.2
  259.5 1.2 copy-start.9
  264.0 29.8 %collective-permute-start.31 = (f32[4,128,1]{2,1,0:T(8,128)}, f32[4,128,1]{2,1,0:T(8,128)S(1)}, u32[]{:S(2)}, u32[]{:S(2)}) collective-permute-start(f32[4,128,1]{2,1,0:T(8,128)} %get-tuple-element.56), channel_id=1, source_target_pairs={{0,32},{32,64},{64,96},{1,33},{33,65},{65,97},{2,34},{34,66},{66,9... | collective-permute-start | bytes 6152 | tf_op jit(solution)/shard_map/ppermute | solution.py:20
  266.2 27.6 %collective-permute-start.30 = (f32[4,128,1]{2,1,0:T(8,128)}, f32[4,128,1]{2,1,0:T(8,128)}, u32[]{:S(2)}, u32[]{:S(2)}) collective-permute-start(f32[4,128,1]{2,1,0:T(8,128)} %get-tuple-element.57), channel_id=1, source_target_pairs={{32,0},{64,32},{96,64},{33,1},{65,33},{97,65},{34,2},{66,34},{98,6... | collective-permute-start | bytes 6152 | tf_op jit(solution)/shard_map/ppermute | solution.py:21
  294.6 6.6 %collective-permute-start.33 = (f32[4,1,258]{2,1,0:T(1,128)S(1)}, f32[4,1,258]{2,1,0:T(1,128)S(1)}, u32[]{:S(2)}, u32[]{:S(2)}) collective-permute-start(f32[4,1,258]{2,1,0:T(1,128)S(1)} %get-tuple-element.44), channel_id=1, source_target_pairs={{0,2},{2,4},{4,6},{6,8},{8,10},{10,12},{12,14},{14,16},{16,18},{18... | collective-permute-start | bytes 12392 | tf_op jit(solution)/shard_map/ppermute | solution.py:20
  298.6 5.5 %collective-permute-start.32 = (f32[4,1,258]{2,1,0:T(1,128)S(1)}, f32[4,1,258]{2,1,0:T(1,128)S(1)}, u32[]{:S(2)}, u32[]{:S(2)}) collective-permute-start(f32[4,1,258]{2,1,0:T(1,128)S(1)} %get-tuple-element.45), channel_id=1, source_target_pairs={{2,0},{4,2},{6,4},{8,6},{10,8},{12,10},{14,12},{16,14},{18,16},{20... | collective-permute-start | bytes 12392 | tf_op jit(solution)/shard_map/ppermute | solution.py:21
  305.3 4.6 %collective-permute-start.34 = (f32[1,130,258]{2,1,0:T(8,128)S(1)}, f32[1,130,258]{2,1,0:T(8,128)S(1)}, u32[]{:S(2)}, u32[]{:S(2)}) collective-permute-start(f32[1,130,258]{2,1,0:T(8,128)S(1)} %get-tuple-element.34), channel_id=1, source_target_pairs={{1,0},{3,2},{5,4},{7,6},{9,8},{11,10},{13,12},{15,14},{17,16},{19,... | collective-permute-start | bytes 402488 | tf_op jit(solution)/shard_map/ppermute | solution.py:21
  306.6 4.1 collective-permute-start.35
  309.9 1.1 copy-start.3
  309.9 1.2 copy-start.14
  312.8 8.8 %copy-start.15 = (f32[4,128,256]{2,1,0:T(8,128)}, f32[4,128,256]{2,1,0:T(8,128)S(1)}, u32[]{:S(2)}) copy-start(f32[4,128,256]{2,1,0:T(8,128)S(1)} %fusion.47) | copy-start | bytes 1572868
  312.8 25.5 %copy-start.5 = (bf16[3000,4]{1,0:T(8,128)(2,1)S(1)}, bf16[3000,4]{1,0:T(8,128)(2,1)}, u32[]{:S(2)}) copy-start(bf16[3000,4]{1,0:T(8,128)(2,1)} %copy-done.4) | copy-start | bytes 72004
  312.8 25.5 %copy-start.16 = (f32[3000,4]{1,0:T(8,128)S(1)}, f32[3000,4]{1,0:T(8,128)}, u32[]{:S(2)}) copy-start(f32[3000,4]{1,0:T(8,128)} %gather_fusion.1) | copy-start | bytes 144004
  338.2 74.8 %copy-start.23 = (f32[3000]{0:T(1024)S(1)}, f32[3000]{0:T(1024)}, u32[]{:S(2)}) copy-start(f32[3000]{0:T(1024)} %param.26) | copy-start | bytes 36004
where the time goes:
time: 419 us; the launch traced here: 415 us
  local copies, waits for them, and re-layouts  109 us (26%)
  other arithmetic  96.2 us (23%)
  starting transfers between devices  90.6 us (22%)
  blocking collectives  71.5 us (17%)
  waiting for transfers between devices  45 us (11%)
    psum x1, blocking collectives, per_device(): adjoint_screen = lax.psum(adjoint_part, ('east', 'north', 'layer'))  68.2 us
    ppermute x18, starting transfers between devices, extended(): before = lax.ppermute(last, axis, up)  67.4 us
    scatter-add x1, other arithmetic, per_device(): load = departure.reshape(flat_shape).at[:, cells].add(-(prices * pump_rat...  31.2 us
    ppermute x18, waiting for transfers between devices, extended(): after = lax.ppermute(initial, axis, down)  29 us
    scatter-add x1, other arithmetic, per_device(): source = jnp.zeros(flat_shape, jnp.float32).at[:, cells].add(pump_rates[N...  26.2 us
    ppermute x18, starting transfers between devices, extended(): after = lax.ppermute(initial, axis, down)  23.2 us
    add x2, local copies, waits for them, and re-layouts, chebyshev(): iterate = trim(iterate) + direction  18.4 us
    gather x1, local copies, waits for them, and re-layouts, per_device(): adjoint_head.reshape(flat_shape)[:, cells]  16.7 us
  transfers between devices with their start and end apart: 36, of which 14 were waited for; matrix products, arithmetic and copies ran while one was open for 25% of the time, Pallas kernels for 0%

commit v1 on v0

v1 whole, which is shorter than its diff:
```python
import functools

import jax
import jax.numpy as jnp
from jax import lax
from jax.experimental import pallas as pl
from jax.experimental.pallas import tpu as pltpu
from jax.sharding import PartitionSpec as P

MESH = pl.DeviceIdType.MESH
F32 = jnp.float32
BF16 = jnp.bfloat16

SWEEPS = 3
CENTRE = 1.0
HALF_WIDTH = 0.95

HALO = 8
REACH = 5
LANES = 128
SLOTS = 128


def steps_of():
    sigma = CENTRE / HALF_WIDTH
    factor = 1.0 / sigma
    found = []
    for _ in range(SWEEPS - 1):
        after = 1.0 / (2.0 * sigma - factor)
        found.append((after * factor, 2.0 * after / HALF_WIDTH))
        factor = after
    return found


def iota(shape, dim):
    return lax.broadcasted_iota(jnp.int32, shape, dim)


def roll(value, shift, dim):
    shift = shift % value.shape[dim]
    return pltpu.roll(value, shift, dim) if shift else value


def exchange(
    sizes,
    head, target, k_east, k_north, k_up, stored,
    p_head, p_target, p_east, p_north, p_up, p_stored,
    nf, nb, ef, eb, cf, cb,
    p_nf, p_nb, p_ef, p_eb, p_cf, p_cb,
    s_nf, s_nb, s_ef, s_eb, s_cf, s_cb,
    send_sem, recv_sem,
):
    n_east, n_north = sizes
    depth, rows, cols = head.shape
    me_e, me_n, me_l = lax.axis_index("east"), lax.axis_index("north"), lax.axis_index("layer")

    def east_of(side):
        return lax.rem(me_e + (n_east - 1 if side == 0 else 1), n_east)

    def north_of(side):
        return lax.rem(me_n + (n_north - 1 if side == 0 else 1), n_north)

    partner = (me_e, me_n, 1 - me_l)
    to_north = [(me_e, north_of(s), me_l) for s in (0, 1)]
    to_east = [(east_of(s), me_n, me_l) for s in (0, 1)]
    to_corner = [(east_of(c), north_of(r), me_l) for r in (0, 1) for c in (0, 1)]

    barrier = pltpu.get_barrier_semaphore()
    for device in [partner] + to_north + to_east + to_corner:
        pl.semaphore_signal(barrier, inc=1, device_id=device, device_id_type=MESH)

    lane = iota((8, LANES), 1)
    sub = iota((8, LANES), 0)
    group = lane // HALO
    wide_sub = iota((8, cols), 0)
    coefs = (k_east, k_north, k_up, stored)
    last = cols - LANES

    def pack(z, carry):
        for side in (0, 1):
            c0 = last * side
            kept = jnp.zeros((8, LANES), F32)
            fields = [jnp.zeros((8, LANES), F32) for _ in coefs]
            for pair in range(rows // 16):
                tiles = [
                    ref[z, pl.ds(16 * pair, 16), pl.ds(c0, LANES)].astype(F32) for ref in coefs
                ]
                for half in (0, 1):
                    j = 2 * pair + half
                    shift = HALO * j - (LANES - HALO) * side
                    h = head[z, pl.ds(8 * j, 8), pl.ds(c0, LANES)]
                    t = target[z, pl.ds(8 * j, 8), pl.ds(c0, LANES)]
                    if side == 0:
                        both = jnp.where(lane >= HALO - 2, roll(t, HALO - 2, 1), h)
                    else:
                        both = jnp.where(lane < LANES - HALO + 2, roll(t, 2 - HALO, 1), h)
                    here = group == j
                    kept = jnp.where(here, roll(both, shift, 1), kept)
                    for a in range(4):
                        piece = tiles[a][8 * half:8 * half + 8]
                        fields[a] = jnp.where(here, roll(piece, shift, 1), fields[a])
            s_ef[side, z] = kept
            s_eb[side, z, pl.ds(0, 16)] = jnp.concatenate(fields[:2], axis=0).astype(BF16)
            s_eb[side, z, pl.ds(16, 16)] = jnp.concatenate(fields[2:], axis=0).astype(BF16)
            r0 = (rows - 8) * side
            h = head[z, pl.ds(r0, 8), :]
            t = target[z, pl.ds(r0, 8), :]
            if side == 0:
                both = jnp.where(wide_sub >= HALO - 2, roll(t, HALO - 2, 0), h)
            else:
                both = jnp.where(wide_sub < 2, roll(t, 2, 0), h)
            s_nf[side, z] = both
            edge = [
                ref[z, pl.ds((rows - 16) * side, 16), :].astype(F32)[8 * side:8 * side + 8]
                for ref in coefs
            ]
            s_nb[side, z, pl.ds(0, 16)] = jnp.concatenate(edge[:2], axis=0).astype(BF16)
            s_nb[side, z, pl.ds(16, 16)] = jnp.concatenate(edge[2:], axis=0).astype(BF16)
        return carry

    lax.fori_loop(0, depth, pack, 0)

    for r in (0, 1):
        for c in (0, 1):
            c0 = last * c
            kept = jnp.zeros((8, LANES), F32)
            mixed = jnp.zeros((8, LANES), F32)
            for z in range(depth):
                both = s_nf[r, z, :, pl.ds(c0, LANES)]
                kept = jnp.where(group == z, roll(both, HALO * z - (LANES - HALO) * c, 1), kept)
                for half in (0, 1):
                    two = s_nb[r, z, pl.ds(16 * half, 16), pl.ds(c0, LANES)].astype(F32)
                    for k in (0, 1):
                        slot = (2 * half + k) * depth + z
                        moved = roll(two[8 * k:8 * k + 8], HALO * slot - (LANES - HALO) * c, 1)
                        mixed = jnp.where(group == slot, moved, mixed)
            s_cf[2 * r + c] = kept
            s_cb[2 * r + c] = jnp.concatenate([mixed, mixed], axis=0).astype(BF16)

    pl.semaphore_wait(barrier, 9)

    count = [0]

    def send(src, dst, device):
        copy = pltpu.make_async_remote_copy(
            src_ref=src,
            dst_ref=dst,
            send_sem=send_sem.at[count[0]],
            recv_sem=recv_sem.at[count[0]],
            device_id=device,
            device_id_type=MESH,
        )
        count[0] += 1
        copy.start()
        return copy

    halos = []
    for side in (0, 1):
        halos.append(send(s_nb.at[side], nb.at[side], to_north[side]))
        halos.append(send(s_nf.at[side], nf.at[side], to_north[side]))
    for side in (0, 1):
        halos.append(send(s_eb.at[side], eb.at[side], to_east[side]))
        halos.append(send(s_ef.at[side], ef.at[side], to_east[side]))
    for d in range(4):
        halos.append(send(s_cb.at[d], cb.at[d], to_corner[d]))
        halos.append(send(s_cf.at[d], cf.at[d], to_corner[d]))
    blocks = [
        send(src, dst, partner)
        for src, dst in (
            (head, p_head), (target, p_target), (k_east, p_east),
            (k_north, p_north), (k_up, p_up), (stored, p_stored),
        )
    ]
    for copy in halos:
        copy.wait_recv()
    forwards = [
        send(src, dst, partner)
        for src, dst in (
            (nf, p_nf), (nb, p_nb), (ef, p_ef), (eb, p_eb), (cf, p_cf), (cb, p_cb),
        )
    ]
    for copy in halos:
        copy.wait_send()
    for copy in blocks + forwards:
        copy.wait()


def run_exchange(sizes, head, target, k_east, k_north, k_up, stored):
    depth, rows, cols = head.shape
    fields = [head, target, k_east, k_north, k_up, stored]
    blocks = [jax.ShapeDtypeStruct(x.shape, x.dtype) for x in fields]
    halos = [
        ((2, depth, 8, cols), F32),
        ((2, depth, 32, cols), BF16),
        ((2, depth, 8, LANES), F32),
        ((2, depth, 32, LANES), BF16),
        ((4, 8, LANES), F32),
        ((4, 16, LANES), BF16),
    ]
    shaped = [jax.ShapeDtypeStruct(s, d) for s, d in halos]
    outs = blocks + shaped + shaped
    copies = 16 + 6 + 6
    return pl.pallas_call(
        functools.partial(exchange, sizes),
        out_shape=outs,
        in_specs=[pl.BlockSpec(memory_space=pltpu.VMEM)] * 6,
        out_specs=[pl.BlockSpec(memory_space=pl.ANY)] * len(outs),
        scratch_shapes=[pltpu.VMEM(s, d) for s, d in halos]
        + [pltpu.SemaphoreType.DMA((copies,)), pltpu.SemaphoreType.DMA((copies,))],
        compiler_params=pltpu.CompilerParams(
            collective_id=0, has_side_effects=True, vmem_limit_bytes=32 * 1024 * 1024
        ),
        name="exchange",
    )(*fields)


def split(value, parts):
    found = []
    for _ in range(parts):
        top = value.astype(BF16)
        found.append(top)
        value = value - top.astype(F32)
    return found


def dot(a, b, dims):
    return lax.dot_general(a, b, (dims, ((), ())), preferred_element_type=F32)


NN = ((1,), (0,))
NT = ((1,), (1,))


def reciprocal(x):
    first = pl.reciprocal(x, approx=True)
    second = first * (2.0 - x * first)
    return second * (2.0 - x * second)


def solve(
    sizes,
    head, target, k_east, k_north, k_up, stored,
    p_head, p_target, p_east, p_north, p_up, p_stored,
    nf, nb, ef, eb, cf, cb,
    p_nf, p_nb, p_ef, p_eb, p_cf, p_cb,
    wells,
    head_new, adjoint, parts,
    hx, tx, ke, kn, kv, st, fe, fn, fu, inv, src, lw, d0, d1, s1, pt, comps, shares,
):
    n_east, n_north = sizes
    depth, rows, cols = head.shape
    layers, ext_rows, ext_cols = hx.shape
    chunks_of_rows = ext_rows // 8
    n_wells = wells.shape[1]
    groups = n_wells // LANES
    me_e, me_n, me_l = lax.axis_index("east"), lax.axis_index("north"), lax.axis_index("layer")

    lane = iota((8, LANES), 1)
    low_half = lane < LANES // 2
    extra = pl.ds(cols, LANES)
    inside_cols = pl.ds(0, cols)

    for own, src_refs in (
        (True, (head, target, k_east, k_north, k_up, stored, nf, nb, ef, eb, cf, cb)),
        (False, (p_head, p_target, p_east, p_north, p_up, p_stored, p_nf, p_nb, p_ef, p_eb, p_cf, p_cb)),
    ):
        b_head, b_target, b_e, b_n, b_u, b_s, bnf, bnb, bef, beb, bcf, bcb = src_refs
        base = depth * (me_l if own else 1 - me_l)

        def fill(z, carry):
            zz = base + z
            inner = pl.ds(8, rows)
            hx[zz, inner, inside_cols] = b_head[z]
            tx[zz, inner, inside_cols] = b_target[z]
            for a, (dst, ref) in enumerate(((ke, b_e), (kn, b_n), (kv, b_u), (st, b_s))):
                dst[zz, inner, inside_cols] = ref[z].astype(F32)
            for side, r0 in ((0, rows + 8), (1, 0)):
                both = bnf[side, z]
                hx[zz, pl.ds(r0, 8), inside_cols] = both
                tx[zz, pl.ds(r0, 8), inside_cols] = roll(both, 2 if side == 0 else 6, 0)
                for half, pair in ((0, (ke, kn)), (1, (kv, st))):
                    two = bnb[side, z, pl.ds(16 * half, 16)].astype(F32)
                    pair[0][zz, pl.ds(r0, 8), inside_cols] = two[:8]
                    pair[1][zz, pl.ds(r0, 8), inside_cols] = two[8:]
            right, left = bef[0, z], bef[1, z]
            for j in range(rows // 8):
                both = jnp.where(
                    low_half, roll(right, -HALO * j, 1), roll(left, LANES - HALO - HALO * j, 1)
                )
                hx[zz, pl.ds(8 + 8 * j, 8), extra] = both
                tx[zz, pl.ds(8 + 8 * j, 8), extra] = jnp.where(
                    low_half, roll(both, 2 - HALO, 1), roll(both, HALO - 2, 1)
                )
            for half, pair in ((0, (ke, kn)), (1, (kv, st))):
                rights = beb[0, z, pl.ds(16 * half, 16)].astype(F32)
                lefts = beb[1, z, pl.ds(16 * half, 16)].astype(F32)
                for k in (0, 1):
                    right, left = rights[8 * k:8 * k + 8], lefts[8 * k:8 * k + 8]
                    for j in range(rows // 8):
                        pair[k][zz, pl.ds(8 + 8 * j, 8), extra] = jnp.where(
                            low_half,
                            roll(right, -HALO * j, 1),
                            roll(left, LANES - HALO - HALO * j, 1),
                        )
            return carry

        lax.fori_loop(0, depth, fill, 0)
        for r, r0 in ((0, rows + 8), (1, 0)):
            at = pl.ds(r0, 8)
            right, left = bcf[2 * r], bcf[2 * r + 1]
            rights, lefts = bcb[2 * r].astype(F32)[:8], bcb[2 * r + 1].astype(F32)[:8]
            for z in range(depth):
                both = jnp.where(
                    low_half, roll(right, -HALO * z, 1), roll(left, LANES - HALO - HALO * z, 1)
                )
                hx[base + z, at, extra] = both
                tx[base + z, at, extra] = roll(both, 2 if r == 0 else 6, 0)
                for a, dst in enumerate((ke, kn, kv, st)):
                    slot = a * depth + z
                    dst[base + z, at, extra] = jnp.where(
                        low_half,
                        roll(rights, -HALO * slot, 1),
                        roll(lefts, LANES - HALO - HALO * slot, 1),
                    )

    at_east = wells[0:1, :] - (me_e * cols).astype(F32)
    at_north = wells[1:2, :] - (me_n * rows).astype(F32)
    near = (
        (at_east >= -REACH) & (at_east < cols + REACH)
        & (at_north >= -REACH) & (at_north < rows + REACH)
    )
    mine = (at_east >= 0) & (at_east < cols) & (at_north >= 0) & (at_north < rows)
    near_row = jnp.where(near, 1.0, 0.0)
    near_tile = jnp.concatenate(
        [near_row[:, LANES * k:LANES * (k + 1)] for k in range(groups)], axis=0
    )
    before = (iota((LANES, LANES), 0) < iota((LANES, LANES), 1)).astype(F32).astype(BF16)
    in_row = dot(near_tile.astype(BF16), before, NN)
    above = (iota((groups, groups), 1) < iota((groups, groups), 0)).astype(F32).astype(BF16)
    rows_above = jnp.sum(dot(above, near_tile.astype(BF16), NN), axis=1, keepdims=True)
    rank = jnp.where(near_tile > 0, in_row + rows_above, -1.0)
    total_near = jnp.sum(near_tile).astype(jnp.int32)
    chunks = (total_near + (SLOTS - 1)) // SLOTS

    place = jnp.concatenate(
        [
            jnp.where(at_east < 0, at_east + ext_cols, at_east),
            at_north + 8.0,
            wells[2:7, :],
            jnp.where(mine, 1.0, 0.0),
        ],
        axis=0,
    )
    place_parts = jnp.concatenate([p.astype(F32) for p in split(place, 3)], axis=0).astype(BF16)
    slot_of = iota((SLOTS, LANES), 0).astype(F32)

    def build_places(chunk):
        first = (chunk * SLOTS).astype(F32) if not isinstance(chunk, int) else float(chunk * SLOTS)
        for k in range(groups):
            row = rank[k:k + 1, :] - first
            pt[:, pl.ds(LANES * k, LANES)] = jnp.where(slot_of == row, 1.0, 0.0).astype(BF16)

    def one_hots(comp):
        col = jnp.where(iota((ext_cols, SLOTS), 0).astype(F32) == comp[0:1], 1.0, 0.0)
        row = jnp.where(iota((ext_rows, SLOTS), 0).astype(F32) == comp[1:2], 1.0, 0.0)
        return col.astype(BF16), row

    def add_wells(chunk, first):
        build_places(chunk)
        three = dot(place_parts, pt[...], NT)
        comp = three[0:8] + three[8:16] + three[16:24]
        comps[chunk] = comp
        col_hot, row_hot = one_hots(comp)
        weights = []
        for z in range(layers):
            found = dot(ke[z].astype(BF16), col_hot, NN)
            k_at = jnp.sum(found * row_hot, axis=0, keepdims=True)
            screened = (comp[2:3] <= z) & (comp[3:4] >= z)
            weights.append(jnp.where(screened, k_at, 0.0))
        weight = jnp.concatenate(weights, axis=0)
        total = jnp.sum(weight, axis=0, keepdims=True)
        share = weight / jnp.where(total > 0, total, 1.0)
        shares[chunk] = share
        pumped = share * comp[4:5]
        priced = pumped * comp[5:6]
        col_two = jnp.concatenate([col_hot, col_hot], axis=1)
        for z in range(layers):
            left = []
            for value in (pumped, priced):
                top, rest = split(value[z:z + 1], 2)
                left.append(
                    jnp.concatenate([row_hot * top.astype(F32), row_hot * rest.astype(F32)], axis=1)
                )
            left = jnp.concatenate(left, axis=0).astype(BF16)
            field = dot(left, col_two, NT)
            if first:
                src[z] = field[:ext_rows]
                lw[z] = field[ext_rows:]
            else:
                src[z] = src[z] + field[:ext_rows]
                lw[z] = lw[z] + field[ext_rows:]

    add_wells(0, True)

    def more_wells(chunk, carry):
        add_wells(chunk, False)
        return carry

    lax.fori_loop(1, chunks, more_wells, 0)

    wide = (8, ext_cols)
    sub = iota(wide, 0)
    col = iota(wide, 1)
    closed_col = ((col == cols - 1) & (me_e == n_east - 1)) | ((col == ext_cols - 1) & (me_e == 0))
    open_east = jnp.where(closed_col, 0.0, 2.0)
    open_low = jnp.where((sub == 7) & (me_n == 0), 0.0, 2.0)
    open_high = jnp.where((sub == 7) & (me_n == n_north - 1), 0.0, 2.0)

    def east(v):
        return roll(v, ext_cols - 1, 1)

    def west(v):
        return roll(v, 1, 1)

    def north(now, after):
        return jnp.where(sub < 7, roll(now, 7, 0), roll(after, 7, 0))

    def south(now, prior):
        return jnp.where(sub > 0, roll(now, 1, 0), roll(prior, 1, 0))

    def at(j):
        return pl.ds(8 * j, 8)

    fu[0] = jnp.zeros((ext_rows, ext_cols), F32)

    def start(z, carry):
        up = jnp.minimum(z + 1, layers - 1)
        down = jnp.maximum(z - 1, 0)
        open_up = jnp.where(z < layers - 1, 2.0, 0.0)
        fn_prior = jnp.zeros(wide, F32)
        gn_prior = jnp.zeros(wide, F32)
        k_n, h = kn[z, at(0)], hx[z, at(0)]
        for j in range(chunks_of_rows):
            j_after = min(j + 1, chunks_of_rows - 1)
            k_e, k_u, k_u2 = ke[z, at(j)], kv[z, at(j)], kv[up, at(j)]
            k_e2 = east(k_e)
            k_after, h_after = kn[z, at(j_after)], hx[z, at(j_after)]
            k_n2 = north(k_n, k_after)
            f_e = open_east * k_e * k_e2 * reciprocal(k_e + k_e2)
            opened = open_low if j == 0 else open_high if j == chunks_of_rows - 2 else 2.0
            f_n = opened * k_n * k_n2 * reciprocal(k_n + k_n2)
            f_u = open_up * k_u * k_u2 * reciprocal(k_u + k_u2)
            f_d = fu[z, at(j)]
            fe[z, at(j)] = f_e
            fn[z, at(j)] = f_n
            fu[z + 1, at(j)] = f_u
            diagonal = st[z, at(j)] + f_e + west(f_e) + f_n + south(f_n, fn_prior) + f_u + f_d
            inverse = reciprocal(diagonal)
            inv[z, at(j)] = inverse
            g_e = f_e * (east(h) - h)
            g_n = f_n * (north(h, h_after) - h)
            g_u = f_u * (hx[up, at(j)] - h)
            g_d = f_d * (h - hx[down, at(j)])
            residual = (g_e - west(g_e)) + (g_n - south(g_n, gn_prior)) + (g_u - g_d)
            d0[z, at(j)] = inverse * (residual - src[z, at(j)])
            fn_prior, gn_prior, k_n, h = f_n, g_n, k_after, h_after
        return carry

    lax.fori_loop(0, layers, start, 0)

    def sweep(field, margin, finish, chunk_from, chunk_to):
        def layer(i, carry):
            z = (depth - margin) * me_l + i
            up = jnp.minimum(z + 1, layers - 1)
            down = jnp.maximum(z - 1, 0)
            if chunk_from == 0:
                b_prior = jnp.zeros(wide, F32)
            else:
                b_prior = fn[z, at(chunk_from - 1)] * field[z, at(chunk_from - 1)]
            d = field[z, at(chunk_from)]
            for j in range(chunk_from, chunk_to):
                d_after = field[z, at(min(j + 1, chunks_of_rows - 1))]
                f_e, f_n = fe[z, at(j)], fn[z, at(j)]
                b = f_n * d
                moved = f_e * east(d) + west(f_e * d)
                moved = moved + f_n * north(d, d_after) + south(b, b_prior)
                moved = moved + fu[z + 1, at(j)] * field[up, at(j)] + fu[z, at(j)] * field[down, at(j)]
                finish(i, z, j, d, inv[z, at(j)] * moved)
                b_prior, d = b, d_after
            return carry

        lax.fori_loop(0, depth + margin, layer, 0)

    (a1, b1), (a2, b2) = steps_of()

    def first_sweep(i, z, j, d, pulled):
        s1[z, at(j)] = pulled
        d1[z, at(j)] = a1 * d + b1 * pulled

    def end_forward(i, z, j, d, pulled):
        s2 = s1[z, at(j)] - d + pulled
        d2 = a2 * d + b2 * s2
        new = hx[z, at(j)] + d0[z, at(j)] + d + d2
        hx[z, at(j)] = new
        load = new - tx[z, at(j)] - lw[z, at(j)]
        src[z, at(j)] = inv[z, at(j)] * load

    sweep(d0, 3, first_sweep, 0, chunks_of_rows)
    sweep(d1, 2, end_forward, 0, chunks_of_rows)
    sweep(src, 1, first_sweep, 0, chunks_of_rows)

    parts[...] = jnp.zeros(parts.shape, F32)
    st[0, at(0)] = jnp.zeros(wide, F32)

    def end_adjoint(i, z, j, d, pulled):
        s2 = s1[z, at(j)] - d + pulled
        d2 = a2 * d + b2 * s2
        adj = src[z, at(j)] + d + d2
        adjoint[i, at(j - 1)] = adj[:, :cols]
        new = hx[z, at(j), inside_cols]
        head_new[i, at(j - 1)] = new
        departure = new - tx[z, at(j), inside_cols]
        st[0, at(0), inside_cols] = st[0, at(0), inside_cols] + departure * departure

    sweep(d1, 0, end_adjoint, 1, chunks_of_rows - 1)

    squared = st[0, at(0), inside_cols]
    squared = jnp.sum(squared, axis=0, keepdims=True)
    squared = sum(squared[:, LANES * k:LANES * (k + 1)] for k in range(cols // LANES))
    squared = squared * (1.0 / (float(layers * rows * cols) * n_east * n_north))
    base_layer = jnp.where(me_l == 0, 1.0, 0.0)

    def collect(chunk, first):
        comp = comps[chunk]
        share = shares[chunk]
        col_hot, row_hot = one_hots(comp)
        col_hot, row_hot = col_hot[:cols], row_hot[8:8 + rows]
        head_at = jnp.zeros((1, SLOTS), F32)
        adj_at = jnp.zeros((1, SLOTS), F32)
        for i in range(depth):
            z_share = jnp.where(me_l == 0, share[i:i + 1], share[depth + i:depth + i + 1])
            stack = split(head_new[i], 2) + split(adjoint[i], 2)
            found = [dot(piece, col_hot, NN) for piece in stack]
            head_at += z_share * jnp.sum((found[0] + found[1]) * row_hot, axis=0, keepdims=True)
            adj_at += z_share * jnp.sum((found[2] + found[3]) * row_hot, axis=0, keepdims=True)
        lift = (comp[6:7] * base_layer - head_at) * comp[7:8]
        priced = comp[5:6] * lift
        slope = priced - adj_at * comp[7:8]
        three = jnp.concatenate(
            [p.astype(F32) for p in split(slope, 3)] + [jnp.zeros((5, SLOTS), F32)], axis=0
        ).astype(BF16)
        if not first:
            build_places(chunk)
        spread = dot(three, pt[...], NN)
        spread = spread[0:1] + spread[1:2] + spread[2:3]
        tile = jnp.concatenate(
            [spread[:, LANES * k:LANES * (k + 1)] for k in range(groups)], axis=0
        )
        parts[pl.ds(0, groups)] += tile
        parts[pl.ds(groups, 1)] += priced * comp[4:5]

    @pl.when(chunks > 1)
    def _():
        build_places(0)

    collect(0, True)

    def collect_more(chunk, carry):
        collect(chunk, False)
        return carry

    lax.fori_loop(1, chunks, collect_more, 0)
    parts[pl.ds(groups + 1, 1)] = squared


def run_solve(sizes, fields, moved, wells):
    depth, rows, cols = fields[0].shape
    layers, ext_rows, ext_cols = 2 * depth, rows + 16, cols + LANES
    groups = wells.shape[1] // LANES
    out = jax.ShapeDtypeStruct((depth, rows, cols), F32)
    ext = pltpu.VMEM((layers, ext_rows, ext_cols), F32)
    return pl.pallas_call(
        functools.partial(solve, sizes),
        out_shape=[out, out, jax.ShapeDtypeStruct((groups + 8, LANES), F32)],
        in_specs=[pl.BlockSpec(memory_space=pltpu.VMEM)] * (len(fields) + len(moved) + 1),
        out_specs=[pl.BlockSpec(memory_space=pltpu.VMEM)] * 3,
        scratch_shapes=[ext] * 8
        + [pltpu.VMEM((layers + 1, ext_rows, ext_cols), F32)]
        + [ext] * 6
        + [
            pltpu.VMEM((SLOTS, wells.shape[1]), BF16),
            pltpu.VMEM((groups, 8, SLOTS), F32),
            pltpu.VMEM((groups, 8, SLOTS), F32),
        ],
        compiler_params=pltpu.CompilerParams(vmem_limit_bytes=56 * 1024 * 1024),
        name="solve",
    )(*fields, *moved, wells)


def add_up(sizes, part, out, box0, box1, box2, box3, send_sem, recv_sem):
    n_east, n_x, n_z = sizes
    me_e, me_n, me_l = lax.axis_index("east"), lax.axis_index("north"), lax.axis_index("layer")
    me_x, me_z = me_n // n_z, lax.rem(me_n, n_z)
    phases = (
        (box0, 2, me_l, lambda i: (me_e, me_n, i)),
        (box1, n_z, me_z, lambda i: (me_e, me_x * n_z + i, me_l)),
        (box2, n_east, me_e, lambda i: (i, me_n, me_l)),
        (box3, n_x, me_x, lambda i: (me_e, i * n_z + me_z, me_l)),
    )
    barrier = pltpu.get_barrier_semaphore()
    peers = 0
    for _, size, mine, device in phases:
        for k in range(1, size):
            pl.semaphore_signal(
                barrier, inc=1, device_id=device(lax.rem(mine + k, size)), device_id_type=MESH
            )
            peers += 1
    pl.semaphore_wait(barrier, peers)
    total = part[...]
    used = 0
    for box, size, mine, device in phases:
        box[mine] = total
        copies = []
        for k in range(1, size):
            copy = pltpu.make_async_remote_copy(
                src_ref=box.at[mine],
                dst_ref=box.at[mine],
                send_sem=send_sem.at[used],
                recv_sem=recv_sem.at[used],
                device_id=device(lax.rem(mine + k, size)),
                device_id_type=MESH,
            )
            copy.start()
            copies.append(copy)
            used += 1
        for copy in copies:
            copy.wait()
        total = box[0]
        for k in range(1, size):
            total = total + box[k]
    tail = part.shape[0] - 8
    out[pl.ds(0, tail)] = total[:tail]
    out[pl.ds(tail, 8)] = jnp.broadcast_to(
        jnp.sum(total[tail:], axis=1, keepdims=True), (8, LANES)
    )


def run_add_up(sizes, part):
    peers = 1 + sum(n - 1 for n in sizes)
    return pl.pallas_call(
        functools.partial(add_up, sizes),
        out_shape=jax.ShapeDtypeStruct(part.shape, F32),
        in_specs=[pl.BlockSpec(memory_space=pltpu.VMEM)],
        out_specs=pl.BlockSpec(memory_space=pltpu.VMEM),
        scratch_shapes=[
            pltpu.VMEM((n,) + part.shape, F32) for n in (2, sizes[2], sizes[0], sizes[1])
        ]
        + [pltpu.SemaphoreType.DMA((peers,)), pltpu.SemaphoreType.DMA((peers,))],
        compiler_params=pltpu.CompilerParams(collective_id=1, has_side_effects=True),
        name="add_up",
    )(part)


def per_device(
    sizes,
    head_old, head_target, conductivity_east, conductivity_north, conductivity_vertical, storage,
    well_east, well_north, screen_top, screen_bottom, tariff_band, pump_rates, ground_level,
    band_prices,
):
    n_east, n_x, n_z = sizes
    n_wells = well_east.shape[0]
    band_ids = jnp.arange(band_prices.shape[0], dtype=jnp.int32)
    prices = jnp.sum(
        jnp.where(tariff_band[None, :] == band_ids[:, None], band_prices[:, None], 0.0), axis=0
    )
    padded = -(-n_wells // LANES) * LANES
    rows = [well_east, well_north, screen_top, screen_bottom, pump_rates, prices, ground_level]
    rows = jnp.stack([r.astype(F32) for r in rows] + [jnp.zeros((n_wells,), F32)])
    wells = jnp.pad(rows, ((0, 0), (0, padded - n_wells)), constant_values=-1e6)
    fields = (
        head_old, head_target, conductivity_east, conductivity_north, conductivity_vertical, storage
    )
    moved = run_exchange((n_east, n_x * n_z), *fields)
    head_new, adjoint, part = run_solve((n_east, n_x * n_z), fields, moved, wells)
    total = run_add_up(sizes, part)
    tail = part.shape[0] - 8
    rate_gradient = total[:tail].reshape(padded)[:n_wells]
    return head_new, adjoint, rate_gradient, total[tail, 0], total[tail + 1, 0]


def solution(mesh):
    field = P("layer", "north", "east")
    n_north = mesh.shape["north"]
    n_x = 4 if n_north % 4 == 0 else 1
    sizes = (mesh.shape["east"], n_x, n_north // n_x)
    return jax.shard_map(
        functools.partial(per_device, sizes),
        mesh=mesh,
        in_specs=(field,) * 6 + (P(),) * 8,
        out_specs=(field, field, P(), P(), P()),
        check_vma=False,
    )
```

time: 419 us -> 79.2 us (0.19)
  other arithmetic: 96.2 us -> 3.72 us
  starting transfers between devices: 90.6 us -> 0 us
  local copies, waits for them, and re-layouts: 109 us -> 20.2 us
  blocking collectives: 71.5 us -> 0 us
  Pallas kernels: 0 us -> 53.7 us
  waiting for transfers between devices: 45 us -> 0 us
    ppermute x36 -> x0, starting transfers between devices: 90.6 us -> none  [the longest x18 67.4 us: extended(): before = lax.ppermute(last, axis, up)]
    psum x2 -> x0, blocking collectives: 71.5 us -> none  [the longest x1 68.2 us: per_device(): adjoint_screen = lax.psum(adjoint_part, ('east', 'north', 'layer'))]
    scatter-add x2 -> x0, other arithmetic: 57.4 us -> none  [the longest x1 31.2 us: per_device(): load = departure.reshape(flat_shape).at[:, cells].add(-(prices * pump_rat...]
    pallas_call x0 -> x3, Pallas kernels: none -> 53.7 us  [the longest x1 22.3 us: run_solve(): pl.pallas_call(functools.partial(solve, sizes), out_shape=[out, out, jax....]
    gather x3 -> x0, local copies, waits for them, and re-layouts: 46.3 us -> none  [the longest x1 16.7 us: per_device(): adjoint_head.reshape(flat_shape)[:, cells]]
    ppermute x36 -> x0, waiting for transfers between devices: 45 us -> none  [the longest x18 29 us: extended(): after = lax.ppermute(initial, axis, down)]
    reshape x2 -> x1, local copies, waits for them, and re-layouts: 21.4 us -> 1.31 us  [per_device(): rate_gradient = total[:tail].reshape(padded)[:n_wells]]
    add x2 -> x0, local copies, waits for them, and re-layouts: 18.4 us -> none  [chebyshev(): iterate = trim(iterate) + direction]
  transfers between devices with their start and end apart: 36 -> 0, of which waited for: 14 -> 0; matrix products, arithmetic and copies ran while one was open for 25% -> 0% of each run, Pallas kernels for 0% -> 0%
where the time goes in v1:
time: 79.2 us; the launch traced here: 78.3 us
  Pallas kernels  53.7 us (68%)
  local copies, waits for them, and re-layouts  20.2 us (26%)
  other arithmetic  3.72 us (5%)
    pallas_call x1, Pallas kernels, run_solve(): pl.pallas_call(functools.partial(solve, sizes), out_shape=[out, out, jax....  22.3 us
    pallas_call x1, Pallas kernels, run_add_up(): pl.pallas_call(functools.partial(add_up, sizes), out_shape=jax.ShapeDtype...  16.3 us
    unnamed x48, local copies, waits for them, and re-layouts  16.1 us
    pallas_call x1, Pallas kernels, run_exchange(): pl.pallas_call(functools.partial(exchange, sizes), out_shape=outs, in_spe...  15.1 us
    convert_element_type x4, other arithmetic, per_device(): r.astype(F32)  2.89 us

profile of v1, /device:TPU:0, one launch (start us, length us, event | category | flops | bytes accessed | tf_op | source)
XLA Modules:
  0.0 78.3 jit_solution(13847673016249970974)
XLA Ops:
  0.6 0.0 copy-start
  0.6 0.8 convert_element_type.12
  1.4 0.7 convert_element_type.13
  2.1 0.7 convert_element_type.14
  2.8 0.7 convert_element_type.15
  3.5 0.8 %select_reduce_fusion = f32[3000]{0:T(1024)S(1)} fusion(f32[4]{0:T(128)} %param.27, s32[3000]{0:T(1024)} %param.24), kind=kLoop, calls=%fused_computation | loop fusion | flops 33000 | bytes 24016 | tf_op jit(solution)/shard_map/reduce_sum | solution.py:673
  4.4 0.9 %stack.31 = f32[8,3000]{1,0:T(8,128)S(1)} concatenate(f32[1,3000]{1,0:T(1,128)S(1)} %bitcast.12, f32[1,3000]{1,0:T(1,128)S(1)} %bitcast.13, f32[1,3000]{1,0:T(1,128)S(1)} %bitcast.14, f32[1,3000]{1,0:T(1,128)S(1)} %bitcast.15, f32[1,3000]{1,0:T(1,128)} %bitcast.17, f32[1,3000]{1,0:T(1,128)S(1)} %bitcast.16, f32[1,3000]{1,0:T(1,128)} %bitcast.18, f32[1,3000]{1,0:T(1,128)S(1)} %stack_broadcast_in_dim.3), dimensions={0} | concatenate | bytes 192000 | tf_op jit(solution)/shard_map/stack | solution.py:678
  5.3 0.7 pad.4.wells
  5.9 0.0 copy-done
  5.9 0.0 copy-start.1
  5.9 1.0 %copy-done.1 = f32[4,128,256]{2,1,0:T(8,128)S(1)} copy-done((f32[4,128,256]{2,1,0:T(8,128)S(1)}, f32[4,128,256]{2,1,0:T(8,128)}, u32[]{:S(2)}) %copy-start.1) | copy-done | bytes 524312
  7.0 0.0 copy-start.2
  7.0 0.9 %copy-done.2 = bf16[4,128,256]{2,1,0:T(8,128)(2,1)S(1)} copy-done((bf16[4,128,256]{2,1,0:T(8,128)(2,1)S(1)}, bf16[4,128,256]{2,1,0:T(8,128)(2,1)}, u32[]{:S(2)}) %copy-start.2) | copy-done | bytes 262168
  7.9 0.0 copy-start.3
  7.9 0.9 %copy-done.3 = bf16[4,128,256]{2,1,0:T(8,128)(2,1)S(1)} copy-done((bf16[4,128,256]{2,1,0:T(8,128)(2,1)S(1)}, bf16[4,128,256]{2,1,0:T(8,128)(2,1)}, u32[]{:S(2)}) %copy-start.3) | copy-done | bytes 262168
  8.9 0.0 copy-start.4
  8.9 0.9 %copy-done.4 = bf16[4,128,256]{2,1,0:T(8,128)(2,1)S(1)} copy-done((bf16[4,128,256]{2,1,0:T(8,128)(2,1)S(1)}, bf16[4,128,256]{2,1,0:T(8,128)(2,1)}, u32[]{:S(2)}) %copy-start.4) | copy-done | bytes 262168
  9.8 0.0 copy-start.5
  9.8 0.9 %copy-done.5 = bf16[4,128,256]{2,1,0:T(8,128)(2,1)S(1)} copy-done((bf16[4,128,256]{2,1,0:T(8,128)(2,1)S(1)}, bf16[4,128,256]{2,1,0:T(8,128)(2,1)}, u32[]{:S(2)}) %copy-start.5) | copy-done | bytes 262168
  10.8 15.1 %exchange.1 = (f32[4,128,256]{2,1,0:T(8,128)S(1)}, f32[4,128,256]{2,1,0:T(8,128)S(1)}, bf16[4,128,256]{2,1,0:T(8,128)(2,1)S(1)}, bf16[4,128,256]{2,1,0:T(8,128)(...) custom-call(f32[4,128,256]{2,1,0:T(8,128)S(1)} %copy-done, ...), custom_call_target="tpu_custom_call" | custom-call | tf_op jit(solution)/shard_map/exchange/pallas_call | solution.py:203
  25.8 0.0 copy-start.6
  25.9 0.8 %copy-done.6 = f32[4,128,256]{2,1,0:T(8,128)} copy-done((f32[4,128,256]{2,1,0:T(8,128)}, f32[4,128,256]{2,1,0:T(8,128)S(1)}, u32[]{:S(2)}) %copy-start.6) | copy-done | bytes 524312
  26.7 0.0 copy-start.7
  26.7 0.8 %copy-done.7 = f32[4,128,256]{2,1,0:T(8,128)} copy-done((f32[4,128,256]{2,1,0:T(8,128)}, f32[4,128,256]{2,1,0:T(8,128)S(1)}, u32[]{:S(2)}) %copy-start.7) | copy-done | bytes 524312
  27.5 0.0 copy-start.8
  27.5 0.7 copy-done.8
  28.2 0.0 copy-start.9
  28.2 0.7 copy-done.9
  28.9 0.0 copy-start.10
  28.9 0.7 copy-done.10
  29.6 0.0 copy-start.11
  29.6 0.7 copy-done.11
  30.3 0.0 copy-start.12
  30.3 0.7 copy-done.12
  30.9 0.0 copy-start.13
  30.9 0.6 copy-done.13
  31.6 0.0 copy-start.14
  31.6 0.6 copy-done.14
  32.2 0.0 copy-start.15
  32.2 0.6 copy-done.15
  32.8 0.0 copy-start.16
  32.8 0.6 copy-done.16
  33.5 0.0 copy-start.17
  33.5 0.6 copy-done.17
  34.1 0.0 copy-start.18
  34.1 0.6 copy-done.18
  34.7 0.0 copy-start.19
  34.7 0.6 copy-done.19
  35.3 0.0 copy-start.22
  35.3 0.6 copy-done.22
  35.9 0.0 copy-start.23
  35.9 0.6 copy-done.23
  36.5 0.0 copy-start.20
  36.5 0.0 copy-start.21
  36.5 0.6 copy-done.20
  37.1 0.0 copy-done.21
  37.1 22.3 %solve.1 = (f32[4,128,256]{2,1,0:T(8,128)}, f32[4,128,256]{2,1,0:T(8,128)}, f32[32,128]{1,0:T(8,128)}) custom-call(f32[4,128,256]{2,1,0:T(8,128)} %head.3, f32[4,128,256]{2,1,0:T(8,128)} %target.3, bf16[4,128,256]{2,1,0:T(8,128)(2,1)} %k_east.3, bf16[4,128,256]{2,1,0:T(8,128)(2,1)} %k_north.3, bf16[4,128,256]{2,1,0:T(8,128)(2,1)} %k_up.3, ...), custom_call_target="tpu_custom_call" | custom-call | tf_op jit(solution)/shard_map/solve/pallas_call | solution.py:582
  59.4 16.3 %add_up.1 = f32[32,128]{1,0:T(8,128)} custom-call(f32[32,128]{1,0:T(8,128)} %get-tuple-element.46.part), custom_call_target="tpu_custom_call" | custom-call | tf_op jit(solution)/shard_map/add_up/pallas_call | solution.py:650
  75.7 1.3 %fusion = (f32[1,1]{1,0:T(1,128)}, f32[1,1]{1,0:T(1,128)}) fusion(f32[32,128]{1,0:T(8,128)} %add_up.1), kind=kLoop, calls=%fused_computation.3 | loop fusion | bytes 16 | tf_op jit(solution)/shard_map/slice | solution.py:688
  77.0 1.3 %slice_bitcast_fusion = f32[3072]{0:T(1024)} fusion(f32[32,128]{1,0:T(8,128)} %add_up.1), kind=kLoop, calls=%fused_computation.2 | loop fusion | bytes 24576 | tf_op jit(solution)/shard_map/reshape | solution.py:687
  (1 shorter events, 0.0 us)
Async XLA Ops:
  0.6 5.3 %copy-start = (f32[4,128,256]{2,1,0:T(8,128)S(1)}, f32[4,128,256]{2,1,0:T(8,128)}, u32[]{:S(2)}) copy-start(f32[4,128,256]{2,1,0:T(8,128)} %head.3) | copy-start | bytes 1572868
  5.9 1.0 %copy-start.1 = (f32[4,128,256]{2,1,0:T(8,128)S(1)}, f32[4,128,256]{2,1,0:T(8,128)}, u32[]{:S(2)}) copy-start(f32[4,128,256]{2,1,0:T(8,128)} %target.3) | copy-start | bytes 1572868
  7.0 0.9 %copy-start.2 = (bf16[4,128,256]{2,1,0:T(8,128)(2,1)S(1)}, bf16[4,128,256]{2,1,0:T(8,128)(2,1)}, u32[]{:S(2)}) copy-start(bf16[4,128,256]{2,1,0:T(8,128)(2,1)} %k_east.3) | copy-start | bytes 786436
  7.9 0.9 %copy-start.3 = (bf16[4,128,256]{2,1,0:T(8,128)(2,1)S(1)}, bf16[4,128,256]{2,1,0:T(8,128)(2,1)}, u32[]{:S(2)}) copy-start(bf16[4,128,256]{2,1,0:T(8,128)(2,1)} %k_north.3) | copy-start | bytes 786436
  8.9 0.9 %copy-start.4 = (bf16[4,128,256]{2,1,0:T(8,128)(2,1)S(1)}, bf16[4,128,256]{2,1,0:T(8,128)(2,1)}, u32[]{:S(2)}) copy-start(bf16[4,128,256]{2,1,0:T(8,128)(2,1)} %k_up.3) | copy-start | bytes 786436
  9.8 0.9 %copy-start.5 = (bf16[4,128,256]{2,1,0:T(8,128)(2,1)S(1)}, bf16[4,128,256]{2,1,0:T(8,128)(2,1)}, u32[]{:S(2)}) copy-start(bf16[4,128,256]{2,1,0:T(8,128)(2,1)} %stored.3) | copy-start | bytes 786436
  25.8 0.8 %copy-start.6 = (f32[4,128,256]{2,1,0:T(8,128)}, f32[4,128,256]{2,1,0:T(8,128)S(1)}, u32[]{:S(2)}) copy-start(f32[4,128,256]{2,1,0:T(8,128)S(1)} %get-tuple-element.26.p_head) | copy-start | bytes 1572868
  26.7 0.8 %copy-start.7 = (f32[4,128,256]{2,1,0:T(8,128)}, f32[4,128,256]{2,1,0:T(8,128)S(1)}, u32[]{:S(2)}) copy-start(f32[4,128,256]{2,1,0:T(8,128)S(1)} %get-tuple-element.27.p_target) | copy-start | bytes 1572868
  27.5 0.7 copy-start.8
  28.2 0.7 copy-start.9
  28.9 0.7 copy-start.10
  29.6 0.7 copy-start.11
  30.3 0.7 copy-start.12
  30.9 0.6 copy-start.13
  31.6 0.6 copy-start.14
  32.2 0.6 copy-start.15
  32.8 0.6 copy-start.16
  33.5 0.6 copy-start.17
  34.1 0.6 copy-start.18
  34.7 0.6 copy-start.19
  35.3 0.6 copy-start.22
  35.9 0.6 copy-start.23
  36.5 0.6 copy-start.20
  36.5 0.6 copy-start.21

commit v2 on v1

--- a/solution.py
+++ b/solution.py
@@ -43,12 +43,13 @@
 
 def exchange(
     sizes,
-    head, target, k_east, k_north, k_up, stored,
+    h_head, h_target, h_east, h_north, h_up, h_stored,
     p_head, p_target, p_east, p_north, p_up, p_stored,
     nf, nb, ef, eb, cf, cb,
     p_nf, p_nb, p_ef, p_eb, p_cf, p_cb,
+    head, target, k_east, k_north, k_up, stored,
     s_nf, s_nb, s_ef, s_eb, s_cf, s_cb,
-    send_sem, recv_sem,
+    load_sem, send_sem, recv_sem,
 ):
     n_east, n_north = sizes
     depth, rows, cols = head.shape
@@ -68,6 +69,16 @@
     barrier = pltpu.get_barrier_semaphore()
     for device in [partner] + to_north + to_east + to_corner:
         pl.semaphore_signal(barrier, inc=1, device_id=device, device_id_type=MESH)
+
+    loads = [
+        pltpu.make_async_copy(src, dst, load_sem.at[k])
+        for k, (src, dst) in enumerate((
+            (h_head, head), (h_target, target), (h_east, k_east),
+            (h_north, k_north), (h_up, k_up), (h_stored, stored),
+        ))
+    ]
+    for load in loads:
+        load.start()
 
     lane = iota((8, LANES), 1)
     sub = iota((8, LANES), 0)
@@ -118,6 +129,8 @@
             s_nb[side, z, pl.ds(16, 16)] = jnp.concatenate(edge[2:], axis=0).astype(BF16)
         return carry
 
+    for load in loads:
+        load.wait()
     lax.fori_loop(0, depth, pack, 0)
 
     for r in (0, 1):
@@ -167,8 +180,8 @@
     blocks = [
         send(src, dst, partner)
         for src, dst in (
-            (head, p_head), (target, p_target), (k_east, p_east),
-            (k_north, p_north), (k_up, p_up), (stored, p_stored),
+            (h_head, p_head), (h_target.at[pl.ds((depth - 2) * (1 - me_l), 2)], p_target),
+            (h_east, p_east), (h_north, p_north), (h_up, p_up), (h_stored, p_stored),
         )
     ]
     for copy in halos:
@@ -189,6 +202,7 @@
     depth, rows, cols = head.shape
     fields = [head, target, k_east, k_north, k_up, stored]
     blocks = [jax.ShapeDtypeStruct(x.shape, x.dtype) for x in fields]
+    blocks[1] = jax.ShapeDtypeStruct((2, rows, cols), F32)
     halos = [
         ((2, depth, 8, cols), F32),
         ((2, depth, 32, cols), BF16),
@@ -203,12 +217,14 @@
     return pl.pallas_call(
         functools.partial(exchange, sizes),
         out_shape=outs,
-        in_specs=[pl.BlockSpec(memory_space=pltpu.VMEM)] * 6,
-        out_specs=[pl.BlockSpec(memory_space=pl.ANY)] * len(outs),
-        scratch_shapes=[pltpu.VMEM(s, d) for s, d in halos]
+        in_specs=[pl.BlockSpec(memory_space=pltpu.HBM)] * 6,
+        out_specs=[pl.BlockSpec(memory_space=pltpu.HBM)] * len(outs),
+        scratch_shapes=[pltpu.VMEM(x.shape, x.dtype) for x in fields]
+        + [pltpu.VMEM(s, d) for s, d in halos]
+        + [pltpu.SemaphoreType.DMA((6,))]
         + [pltpu.SemaphoreType.DMA((copies,)), pltpu.SemaphoreType.DMA((copies,))],
         compiler_params=pltpu.CompilerParams(
-            collective_id=0, has_side_effects=True, vmem_limit_bytes=32 * 1024 * 1024
+            collective_id=0, has_side_effects=True, vmem_limit_bytes=60 * 1024 * 1024
         ),
         name="exchange",
     )(*fields)
@@ -239,16 +255,18 @@
 
 def solve(
     sizes,
-    head, target, k_east, k_north, k_up, stored,
-    p_head, p_target, p_east, p_north, p_up, p_stored,
-    nf, nb, ef, eb, cf, cb,
-    p_nf, p_nb, p_ef, p_eb, p_cf, p_cb,
-    wells,
-    head_new, adjoint, parts,
-    hx, tx, ke, kn, kv, st, fe, fn, fu, inv, src, lw, d0, d1, s1, pt, comps, shares,
+    *refs,
 ):
     n_east, n_north = sizes
-    depth, rows, cols = head.shape
+    fields, refs = (refs[:6], refs[6:12]), refs[12:]
+    halos, refs = (refs[:6], refs[6:12]), refs[12:]
+    well_refs, refs = refs[:8], refs[8:]
+    head_new, adjoint, parts = refs[:3]
+    hx, tx, ke, kn, kv, st, fe, fn, fu, inv, src, lw, d0, d1, s1, pt, comps, shares = refs[3:21]
+    staged, refs = refs[21:25], refs[25:]
+    nbs, efs, ebs, cfs, cbs = refs[:5]
+    well_rows, wells, sems = refs[5:13], refs[13], refs[14]
+    depth, rows, cols = head_new.shape
     layers, ext_rows, ext_cols = hx.shape
     chunks_of_rows = ext_rows // 8
     n_wells = wells.shape[1]
@@ -259,69 +277,105 @@
     low_half = lane < LANES // 2
     extra = pl.ds(cols, LANES)
     inside_cols = pl.ds(0, cols)
-
-    for own, src_refs in (
-        (True, (head, target, k_east, k_north, k_up, stored, nf, nb, ef, eb, cf, cb)),
-        (False, (p_head, p_target, p_east, p_north, p_up, p_stored, p_nf, p_nb, p_ef, p_eb, p_cf, p_cb)),
-    ):
-        b_head, b_target, b_e, b_n, b_u, b_s, bnf, bnb, bef, beb, bcf, bcb = src_refs
-        base = depth * (me_l if own else 1 - me_l)
-
-        def fill(z, carry):
-            zz = base + z
-            inner = pl.ds(8, rows)
-            hx[zz, inner, inside_cols] = b_head[z]
-            tx[zz, inner, inside_cols] = b_target[z]
-            for a, (dst, ref) in enumerate(((ke, b_e), (kn, b_n), (kv, b_u), (st, b_s))):
-                dst[zz, inner, inside_cols] = ref[z].astype(F32)
-            for side, r0 in ((0, rows + 8), (1, 0)):
-                both = bnf[side, z]
-                hx[zz, pl.ds(r0, 8), inside_cols] = both
-                tx[zz, pl.ds(r0, 8), inside_cols] = roll(both, 2 if side == 0 else 6, 0)
+    inner = pl.ds(8, rows)
+    starts = (depth * me_l, depth * (1 - me_l))
+    high, low = pl.ds(rows + 8, 8), pl.ds(0, 8)
+
+    small, large = [], []
+
+    def load(found, src_ref, dst_ref):
+        copy = pltpu.make_async_copy(src_ref, dst_ref, sems.at[len(small) + len(large)])
+        copy.start()
+        found.append(copy)
+
+    for src_ref, dst_ref in zip(well_refs, well_rows):
+        load(small, src_ref, dst_ref)
+    for who in (0, 1):
+        here = pl.ds(starts[who], depth)
+        for a in range(4):
+            load(large, fields[who][2 + a], staged[a].at[here])
+        b_nf, b_nb, b_ef, b_eb, b_cf, b_cb = halos[who]
+        load(large, b_nb, nbs.at[who])
+        load(large, b_eb, ebs.at[who])
+        load(large, b_cb, cbs.at[who])
+        load(large, fields[who][0], hx.at[here, inner, inside_cols])
+        load(large, b_nf.at[0], hx.at[here, high, inside_cols])
+        load(large, b_nf.at[1], hx.at[here, low, inside_cols])
+        load(large, b_ef, efs.at[who])
+        load(large, b_cf, cfs.at[who])
+        there = here if who == 0 else pl.ds(depth - 2 * me_l, 2)
+        load(large, fields[who][1], tx.at[there, inner, inside_cols])
+
+    def fill_fields():
+        for who in (0, 1):
+            base = starts[who]
+
+            def fill(z, carry):
+                zz = base + z
+                for dst, ref in zip((ke, kn, kv, st), staged):
+                    dst[zz, inner, inside_cols] = ref[zz].astype(F32)
+                for side, at_rows in ((0, high), (1, low)):
+                    tx[zz, at_rows, inside_cols] = roll(
+                        hx[zz, at_rows, inside_cols], 2 if side == 0 else 6, 0
+                    )
+                    for half, pair in ((0, (ke, kn)), (1, (kv, st))):
+                        two = nbs[who, side, z, pl.ds(16 * half, 16)].astype(F32)
+                        pair[0][zz, at_rows, inside_cols] = two[:8]
+                        pair[1][zz, at_rows, inside_cols] = two[8:]
+                right, left = efs[who, 0, z], efs[who, 1, z]
+                for j in range(rows // 8):
+                    both = jnp.where(
+                        low_half, roll(right, -HALO * j, 1), roll(left, LANES - HALO - HALO * j, 1)
+                    )
+                    hx[zz, pl.ds(8 + 8 * j, 8), extra] = both
+                    tx[zz, pl.ds(8 + 8 * j, 8), extra] = jnp.where(
+                        low_half, roll(both, 2 - HALO, 1), roll(both, HALO - 2, 1)
+                    )
                 for half, pair in ((0, (ke, kn)), (1, (kv, st))):
-                    two = bnb[side, z, pl.ds(16 * half, 16)].astype(F32)
-                    pair[0][zz, pl.ds(r0, 8), inside_cols] = two[:8]
-                    pair[1][zz, pl.ds(r0, 8), inside_cols] = two[8:]
-            right, left = bef[0, z], bef[1, z]
-            for j in range(rows // 8):
-                both = jnp.where(
-                    low_half, roll(right, -HALO * j, 1), roll(left, LANES - HALO - HALO * j, 1)
-                )
-                hx[zz, pl.ds(8 + 8 * j, 8), extra] = both
-                tx[zz, pl.ds(8 + 8 * j, 8), extra] = jnp.where(
-                    low_half, roll(both, 2 - HALO, 1), roll(both, HALO - 2, 1)
-                )
-            for half, pair in ((0, (ke, kn)), (1, (kv, st))):
-                rights = beb[0, z, pl.ds(16 * half, 16)].astype(F32)
-                lefts = beb[1, z, pl.ds(16 * half, 16)].astype(F32)
-                for k in (0, 1):
-                    right, left = rights[8 * k:8 * k + 8], lefts[8 * k:8 * k + 8]
-                    for j in range(rows // 8):
-                        pair[k][zz, pl.ds(8 + 8 * j, 8), extra] = jnp.where(
+                    rights = ebs[who, 0, z, pl.ds(16 * half, 16)].astype(F32)
+                    lefts = ebs[who, 1, z, pl.ds(16 * half, 16)].astype(F32)
+                    for k in (0, 1):
+                        right, left = rights[8 * k:8 * k + 8], lefts[8 * k:8 * k + 8]
+                        for j in range(rows // 8):
+                            pair[k][zz, pl.ds(8 + 8 * j, 8), extra] = jnp.where(
+                                low_half,
+                                roll(right, -HALO * j, 1),
+                                roll(left, LANES - HALO - HALO * j, 1),
+                            )
+                return carry
+
+            lax.fori_loop(0, depth, fill, 0)
+            for r, at_rows in ((0, high), (1, low)):
+                right, left = cfs[who, 2 * r], cfs[who, 2 * r + 1]
+                rights = cbs[who, 2 * r].astype(F32)[:8]
+                lefts = cbs[who, 2 * r + 1].astype(F32)[:8]
+                for z in range(depth):
+                    both = jnp.where(
+                        low_half, roll(right, -HALO * z, 1), roll(left, LANES - HALO - HALO * z, 1)
+                    )
+                    hx[base + z, at_rows, extra] = both
+                    tx[base + z, at_rows, extra] = roll(both, 2 if r == 0 else 6, 0)
+                    for a, dst in enumerate((ke, kn, kv, st)):
+                        slot = a * depth + z
+                        dst[base + z, at_rows, extra] = jnp.where(
                             low_half,
-                            roll(right, -HALO * j, 1),
-                            roll(left, LANES - HALO - HALO * j, 1),
+                            roll(rights, -HALO * slot, 1),
+                            roll(lefts, LANES - HALO - HALO * slot, 1),
                         )
-            return carry
-
-        lax.fori_loop(0, depth, fill, 0)
-        for r, r0 in ((0, rows + 8), (1, 0)):
-            at = pl.ds(r0, 8)
-            right, left = bcf[2 * r], bcf[2 * r + 1]
-            rights, lefts = bcb[2 * r].astype(F32)[:8], bcb[2 * r + 1].astype(F32)[:8]
-            for z in range(depth):
-                both = jnp.where(
-                    low_half, roll(right, -HALO * z, 1), roll(left, LANES - HALO - HALO * z, 1)
-                )
-                hx[base + z, at, extra] = both
-                tx[base + z, at, extra] = roll(both, 2 if r == 0 else 6, 0)
-                for a, dst in enumerate((ke, kn, kv, st)):
-                    slot = a * depth + z
-                    dst[base + z, at, extra] = jnp.where(
-                        low_half,
-                        roll(rights, -HALO * slot, 1),
-                        roll(lefts, LANES - HALO - HALO * slot, 1),
-                    )
+
+    for copy in small:
+        copy.wait()
+    wells[...] = jnp.full(wells.shape, -1e6, F32)
+    width = pl.ds(0, well_rows[0].shape[1])
+    for row, ref in enumerate(well_rows[:5]):
+        wells[pl.ds(row, 1), width] = ref[...].astype(F32)
+    band = well_rows[5][...]
+    bands = well_rows[7][...]
+    price = jnp.zeros(band.shape, F32)
+    for b in range(bands.shape[1]):
+        price = jnp.where(band == b, bands[0:1, b:b + 1], price)
+    wells[pl.ds(5, 1), width] = price
+    wells[pl.ds(6, 1), width] = well_rows[6][...]
 
     at_east = wells[0:1, :] - (me_e * cols).astype(F32)
     at_north = wells[1:2, :] - (me_n * rows).astype(F32)
@@ -400,6 +454,9 @@
                 src[z] = src[z] + field[:ext_rows]
                 lw[z] = lw[z] + field[ext_rows:]
 
+    for copy in large:
+        copy.wait()
+    fill_fields()
     add_wells(0, True)
 
     def more_wells(chunk, carry):
@@ -576,25 +633,37 @@
 def run_solve(sizes, fields, moved, wells):
     depth, rows, cols = fields[0].shape
     layers, ext_rows, ext_cols = 2 * depth, rows + 16, cols + LANES
-    groups = wells.shape[1] // LANES
+    n_wells = wells[0].shape[1]
+    groups = -(-n_wells // LANES)
     out = jax.ShapeDtypeStruct((depth, rows, cols), F32)
     ext = pltpu.VMEM((layers, ext_rows, ext_cols), F32)
+    operands = (*fields, *moved, *wells)
     return pl.pallas_call(
         functools.partial(solve, sizes),
         out_shape=[out, out, jax.ShapeDtypeStruct((groups + 8, LANES), F32)],
-        in_specs=[pl.BlockSpec(memory_space=pltpu.VMEM)] * (len(fields) + len(moved) + 1),
+        in_specs=[pl.BlockSpec(memory_space=pltpu.HBM)] * len(operands),
         out_specs=[pl.BlockSpec(memory_space=pltpu.VMEM)] * 3,
         scratch_shapes=[ext] * 8
         + [pltpu.VMEM((layers + 1, ext_rows, ext_cols), F32)]
         + [ext] * 6
         + [
-            pltpu.VMEM((SLOTS, wells.shape[1]), BF16),
+            pltpu.VMEM((SLOTS, groups * LANES), BF16),
             pltpu.VMEM((groups, 8, SLOTS), F32),
             pltpu.VMEM((groups, 8, SLOTS), F32),
-        ],
-        compiler_params=pltpu.CompilerParams(vmem_limit_bytes=56 * 1024 * 1024),
+        ]
+        + [pltpu.VMEM((layers, rows, cols), BF16)] * 4
+        + [
+            pltpu.VMEM((2, 2, depth, 32, cols), BF16),
+            pltpu.VMEM((2, 2, depth, 8, LANES), F32),
+            pltpu.VMEM((2, 2, depth, 32, LANES), BF16),
+            pltpu.VMEM((2, 4, 8, LANES), F32),
+            pltpu.VMEM((2, 4, 16, LANES), BF16),
+        ]
+        + [pltpu.VMEM(w.shape, w.dtype) for w in wells]
+        + [pltpu.VMEM((8, groups * LANES), F32), pltpu.SemaphoreType.DMA((8 + 26,))],
+        compiler_params=pltpu.CompilerParams(vmem_limit_bytes=60 * 1024 * 1024),
         name="solve",
-    )(*fields, *moved, wells)
+    )(*operands)
 
 
 def add_up(sizes, part, out, box0, box1, box2, box3, send_sem, recv_sem):
@@ -669,14 +738,13 @@
 ):
     n_east, n_x, n_z = sizes
     n_wells = well_east.shape[0]
-    band_ids = jnp.arange(band_prices.shape[0], dtype=jnp.int32)
-    prices = jnp.sum(
-        jnp.where(tariff_band[None, :] == band_ids[:, None], band_prices[:, None], 0.0), axis=0
-    )
-    padded = -(-n_wells // LANES) * LANES
-    rows = [well_east, well_north, screen_top, screen_bottom, pump_rates, prices, ground_level]
-    rows = jnp.stack([r.astype(F32) for r in rows] + [jnp.zeros((n_wells,), F32)])
-    wells = jnp.pad(rows, ((0, 0), (0, padded - n_wells)), constant_values=-1e6)
+    wells = [
+        w.reshape(1, -1)
+        for w in (
+            well_east, well_north, screen_top, screen_bottom, pump_rates, tariff_band,
+            ground_level, band_prices,
+        )
+    ]
     fields = (
         head_old, head_target, conductivity_east, conductivity_north, conductivity_vertical, storage
     )
@@ -684,7 +752,7 @@
     head_new, adjoint, part = run_solve((n_east, n_x * n_z), fields, moved, wells)
     total = run_add_up(sizes, part)
     tail = part.shape[0] - 8
-    rate_gradient = total[:tail].reshape(padded)[:n_wells]
+    rate_gradient = total[:tail].reshape(-1)[:n_wells]
     return head_new, adjoint, rate_gradient, total[tail, 0], total[tail + 1, 0]
 
 

time: 79.2 us -> 58.6 us (0.74)
  local copies, waits for them, and re-layouts: 20.2 us -> 2.57 us
  other arithmetic: 3.72 us -> 0 us
  Pallas kernels: 53.7 us -> 54.9 us
    unnamed x48 -> x0, local copies, waits for them, and re-layouts: 16.1 us -> none
    convert_element_type x4 -> x0, other arithmetic: 2.89 us -> none  [per_device(): r.astype(F32)]
    pallas_call x1, Pallas kernels: 15.1 us -> 17.3 us  [run_exchange(): pl.pallas_call(functools.partial(exchange, sizes), out_shape=outs, in_spe...]
    pallas_call x1, Pallas kernels: 16.3 us -> 14.8 us  [run_add_up(): pl.pallas_call(functools.partial(add_up, sizes), out_shape=jax.ShapeDtype...]
    another operation x2 -> x0, local copies, waits for them, and re-layouts: 0.88 us -> none  [per_device(): jnp.stack([r.astype(F32) for r in rows] + [jnp.zeros((n_wells,), F32)])]
    reduce_sum x1 -> x0, other arithmetic: 0.82 us -> none  [per_device(): jnp.sum(jnp.where(tariff_band[None, :] == band_ids[:, None], band_prices[...]
where the time goes in v2:
time: 58.6 us; the launch traced here: 58.1 us
  Pallas kernels  54.9 us (94%)
  local copies, waits for them, and re-layouts  2.57 us (4%)
  between operations  0.65 us (1%)
    pallas_call x1, Pallas kernels, run_solve(): pl.pallas_call(functools.partial(solve, sizes), out_shape=[out, out, jax....  22.9 us
    pallas_call x1, Pallas kernels, run_exchange(): pl.pallas_call(functools.partial(exchange, sizes), out_shape=outs, in_spe...  17.3 us
    pallas_call x1, Pallas kernels, run_add_up(): pl.pallas_call(functools.partial(add_up, sizes), out_shape=jax.ShapeDtype...  14.8 us
    reshape x1, local copies, waits for them, and re-layouts, per_device(): rate_gradient = total[:tail].reshape(-1)[:n_wells]  1.31 us
    slice x1, local copies, waits for them, and re-layouts, per_device(): total[tail + 1, 0]  1.27 us

profile of v2, /device:TPU:0, one launch (start us, length us, event | category | flops | bytes accessed | tf_op | source)
XLA Modules:
  0.0 58.1 jit_solution(17578058942040536737)
XLA Ops:
  0.6 17.3 %exchange.1 = (f32[4,128,256]{2,1,0:T(8,128)}, f32[2,128,256]{2,1,0:T(8,128)}, bf16[4,128,256]{2,1,0:T(8,128)(2,1)}, bf16[4,128,256]{2,1,0:T(8,128)(2,1)}, bf16[...) custom-call(f32[4,128,256]{2,1,0:T(8,128)} %refs_0_.1, ...), custom_call_target="tpu_custom_call" | custom-call | tf_op jit(solution)/shard_map/exchange/pallas_call | solution.py:217
  17.9 22.9 %solve.1 = (f32[4,128,256]{2,1,0:T(8,128)}, f32[4,128,256]{2,1,0:T(8,128)}, f32[32,128]{1,0:T(8,128)}) custom-call(f32[4,128,256]{2,1,0:T(8,128)} %refs_0_.1, f32[4,128,256]{2,1,0:T(8,128)} %refs_1_.1, bf16[4,128,256]{2,1,0:T(8,128)(2,1)} %refs_2_.1, bf16[4,128,256]{2,1,0:T(8,128)(2,1)} %refs_3_.1, bf16[4,128,256]{2,1,0:T(8,128)(2,1)} %refs_4_.1, ...), custom_call_target="tpu_custom_call" | custom-call | tf_op jit(solution)/shard_map/solve/pallas_call | solution.py:641
  40.8 14.8 %add_up.1 = f32[32,128]{1,0:T(8,128)} custom-call(f32[32,128]{1,0:T(8,128)} %get-tuple-element.46.part), custom_call_target="tpu_custom_call" | custom-call | tf_op jit(solution)/shard_map/add_up/pallas_call | solution.py:719
  55.6 1.3 %fusion = (f32[1,1]{1,0:T(1,128)}, f32[1,1]{1,0:T(1,128)}) fusion(f32[32,128]{1,0:T(8,128)} %add_up.1), kind=kLoop, calls=%fused_computation.1 | loop fusion | bytes 16 | tf_op jit(solution)/shard_map/slice | solution.py:756
  56.8 1.3 %slice_bitcast_fusion = f32[3072]{0:T(1024)} fusion(f32[32,128]{1,0:T(8,128)} %add_up.1), kind=kLoop, calls=%fused_computation | loop fusion | bytes 24576 | tf_op jit(solution)/shard_map/reshape | solution.py:755

commit v3 on v2

--- a/solution.py
+++ b/solution.py
@@ -19,6 +19,7 @@
 REACH = 5
 LANES = 128
 SLOTS = 128
+START_UNIT, SWEEP_UNIT, LAST_UNIT = 9, 18, 16
 
 
 def steps_of():
@@ -249,8 +250,7 @@
 
 def reciprocal(x):
     first = pl.reciprocal(x, approx=True)
-    second = first * (2.0 - x * first)
-    return second * (2.0 - x * second)
+    return first * (2.0 - x * first)
 
 
 def solve(
@@ -485,26 +485,44 @@
     def south(now, prior):
         return jnp.where(sub > 0, roll(now, 1, 0), roll(prior, 1, 0))
 
+    fu[0] = jnp.zeros((ext_rows, ext_cols), F32)
+
+    def row_chunks(begin, end, unit, body, carry):
+        if end - begin == unit:
+            for j in range(begin, end):
+                carry = body(j, carry)
+            return carry
+
+        def several(k, carry):
+            for i in range(unit):
+                carry = body(begin + k * unit + i, carry)
+            return carry
+
+        return lax.fori_loop(0, (end - begin) // unit, several, carry)
+
     def at(j):
-        return pl.ds(8 * j, 8)
-
-    fu[0] = jnp.zeros((ext_rows, ext_cols), F32)
+        return pl.ds(8 * j if isinstance(j, int) else pl.multiple_of(8 * j, 8), 8)
+
+    def next_of(j):
+        return min(j + 1, chunks_of_rows - 1) if isinstance(j, int) else jnp.minimum(j + 1, chunks_of_rows - 1)
 
     def start(z, carry):
         up = jnp.minimum(z + 1, layers - 1)
         down = jnp.maximum(z - 1, 0)
         open_up = jnp.where(z < layers - 1, 2.0, 0.0)
-        fn_prior = jnp.zeros(wide, F32)
-        gn_prior = jnp.zeros(wide, F32)
-        k_n, h = kn[z, at(0)], hx[z, at(0)]
-        for j in range(chunks_of_rows):
-            j_after = min(j + 1, chunks_of_rows - 1)
+
+        def chunk(j, carry):
+            fn_prior, gn_prior, k_n, h = carry
             k_e, k_u, k_u2 = ke[z, at(j)], kv[z, at(j)], kv[up, at(j)]
             k_e2 = east(k_e)
-            k_after, h_after = kn[z, at(j_after)], hx[z, at(j_after)]
+            k_after, h_after = kn[z, at(next_of(j))], hx[z, at(next_of(j))]
             k_n2 = north(k_n, k_after)
             f_e = open_east * k_e * k_e2 * reciprocal(k_e + k_e2)
-            opened = open_low if j == 0 else open_high if j == chunks_of_rows - 2 else 2.0
+            if isinstance(j, int):
+                opened = open_low if j == 0 else open_high if j == chunks_of_rows - 2 else 2.0
+            else:
+                edge = ((j == 0) & (me_n == 0)) | ((j == chunks_of_rows - 2) & (me_n == n_north - 1))
+                opened = jnp.where((sub == 7) & edge, 0.0, 2.0)
             f_n = opened * k_n * k_n2 * reciprocal(k_n + k_n2)
             f_u = open_up * k_u * k_u2 * reciprocal(k_u + k_u2)
             f_d = fu[z, at(j)]
@@ -520,7 +538,10 @@
             g_d = f_d * (h - hx[down, at(j)])
             residual = (g_e - west(g_e)) + (g_n - south(g_n, gn_prior)) + (g_u - g_d)
             d0[z, at(j)] = inverse * (residual - src[z, at(j)])
-            fn_prior, gn_prior, k_n, h = f_n, g_n, k_after, h_after
+            return f_n, g_n, k_after, h_after
+
+        none = jnp.zeros(wide, F32)
+        row_chunks(0, chunks_of_rows, START_UNIT, chunk, (none, none, kn[z, at(0)], hx[z, at(0)]))
         return carry
 
     lax.fori_loop(0, layers, start, 0)
@@ -530,20 +551,24 @@
             z = (depth - margin) * me_l + i
             up = jnp.minimum(z + 1, layers - 1)
             down = jnp.maximum(z - 1, 0)
-            if chunk_from == 0:
-                b_prior = jnp.zeros(wide, F32)
-            else:
-                b_prior = fn[z, at(chunk_from - 1)] * field[z, at(chunk_from - 1)]
-            d = field[z, at(chunk_from)]
-            for j in range(chunk_from, chunk_to):
-                d_after = field[z, at(min(j + 1, chunks_of_rows - 1))]
+
+            def chunk(j, carry):
+                b_prior, d = carry
+                d_after = field[z, at(next_of(j))]
                 f_e, f_n = fe[z, at(j)], fn[z, at(j)]
                 b = f_n * d
                 moved = f_e * east(d) + west(f_e * d)
                 moved = moved + f_n * north(d, d_after) + south(b, b_prior)
                 moved = moved + fu[z + 1, at(j)] * field[up, at(j)] + fu[z, at(j)] * field[down, at(j)]
                 finish(i, z, j, d, inv[z, at(j)] * moved)
-                b_prior, d = b, d_after
+                return b, d_after
+
+            if chunk_from == 0:
+                b_prior = jnp.zeros(wide, F32)
+            else:
+                b_prior = fn[z, at(chunk_from - 1)] * field[z, at(chunk_from - 1)]
+            unit = SWEEP_UNIT if chunk_from == 0 else LAST_UNIT
+            row_chunks(chunk_from, chunk_to, unit, chunk, (b_prior, field[z, at(chunk_from)]))
             return carry
 
         lax.fori_loop(0, depth + margin, layer, 0)

time: 58.6 us -> 55.3 us (0.944)
  Pallas kernels: 54.9 us -> 51.6 us
    pallas_call x1, Pallas kernels: 22.9 us -> 19.6 us  [run_solve(): pl.pallas_call(functools.partial(solve, sizes), out_shape=[out, out, jax....]
where the time goes in v3:
time: 55.3 us; the launch traced here: 54.9 us
  Pallas kernels  51.6 us (93%)
  local copies, waits for them, and re-layouts  2.57 us (5%)
  between operations  0.65 us (1%)
    pallas_call x1, Pallas kernels, run_solve(): pl.pallas_call(functools.partial(solve, sizes), out_shape=[out, out, jax....  19.6 us
    pallas_call x1, Pallas kernels, run_exchange(): pl.pallas_call(functools.partial(exchange, sizes), out_shape=outs, in_spe...  17.3 us
    pallas_call x1, Pallas kernels, run_add_up(): pl.pallas_call(functools.partial(add_up, sizes), out_shape=jax.ShapeDtype...  14.8 us
    reshape x1, local copies, waits for them, and re-layouts, per_device(): rate_gradient = total[:tail].reshape(-1)[:n_wells]  1.31 us
    slice x1, local copies, waits for them, and re-layouts, per_device(): total[tail + 1, 0]  1.27 us

profile of v3, /device:TPU:0, one launch (start us, length us, event | category | flops | bytes accessed | tf_op | source)
XLA Modules:
  0.0 54.9 jit_solution(11884597460741637824)
XLA Ops:
  0.6 17.3 %exchange.1 = (f32[4,128,256]{2,1,0:T(8,128)}, f32[2,128,256]{2,1,0:T(8,128)}, bf16[4,128,256]{2,1,0:T(8,128)(2,1)}, bf16[4,128,256]{2,1,0:T(8,128)(2,1)}, bf16[...) custom-call(f32[4,128,256]{2,1,0:T(8,128)} %refs_0_.1, ...), custom_call_target="tpu_custom_call" | custom-call | tf_op jit(solution)/shard_map/exchange/pallas_call | solution.py:218
  17.9 19.6 %solve.1 = (f32[4,128,256]{2,1,0:T(8,128)}, f32[4,128,256]{2,1,0:T(8,128)}, f32[32,128]{1,0:T(8,128)}) custom-call(f32[4,128,256]{2,1,0:T(8,128)} %refs_0_.1, f32[4,128,256]{2,1,0:T(8,128)} %refs_1_.1, bf16[4,128,256]{2,1,0:T(8,128)(2,1)} %refs_2_.1, bf16[4,128,256]{2,1,0:T(8,128)(2,1)} %refs_3_.1, bf16[4,128,256]{2,1,0:T(8,128)(2,1)} %refs_4_.1, ...), custom_call_target="tpu_custom_call" | custom-call | tf_op jit(solution)/shard_map/solve/pallas_call | solution.py:666
  37.5 14.8 %add_up.1 = f32[32,128]{1,0:T(8,128)} custom-call(f32[32,128]{1,0:T(8,128)} %get-tuple-element.46.part), custom_call_target="tpu_custom_call" | custom-call | tf_op jit(solution)/shard_map/add_up/pallas_call | solution.py:744
  52.3 1.3 %fusion = (f32[1,1]{1,0:T(1,128)}, f32[1,1]{1,0:T(1,128)}) fusion(f32[32,128]{1,0:T(8,128)} %add_up.1), kind=kLoop, calls=%fused_computation.1 | loop fusion | bytes 16 | tf_op jit(solution)/shard_map/slice | solution.py:781
  53.6 1.3 %slice_bitcast_fusion = f32[3072]{0:T(1024)} fusion(f32[32,128]{1,0:T(8,128)} %add_up.1), kind=kLoop, calls=%fused_computation | loop fusion | bytes 24576 | tf_op jit(solution)/shard_map/reshape | solution.py:780

commit v4 on v0

--- a/solution.py
+++ b/solution.py
@@ -1,13 +1,46 @@
+import functools
+
 import jax
 import jax.numpy as jnp
 from jax import lax
+from jax.experimental import pallas as pl
+from jax.experimental.layout import Layout, with_layout_constraint
+from jax.experimental.pallas import tpu as pltpu
 from jax.sharding import PartitionSpec as P
 
+MESH = pl.DeviceIdType.MESH
+F32 = jnp.float32
+BF16 = jnp.bfloat16
+
 SWEEPS = 3
-
-
 CENTRE = 1.0
 HALF_WIDTH = 0.95
+
+HALO = 8
+REACH = 5
+LANES = 128
+SLOTS = 128
+START_UNIT, SWEEP_UNIT, LAST_UNIT = 9, 18, 16
+
+
+def steps_of():
+    sigma = CENTRE / HALF_WIDTH
+    factor = 1.0 / sigma
+    found = []
+    for _ in range(SWEEPS - 1):
+        after = 1.0 / (2.0 * sigma - factor)
+        found.append((after * factor, 2.0 * after / HALF_WIDTH))
+        factor = after
+    return found
+
+
+def iota(shape, dim):
+    return lax.broadcasted_iota(jnp.int32, shape, dim)
+
+
+def roll(value, shift, dim):
+    shift = shift % value.shape[dim]
+    return pltpu.roll(value, shift, dim) if shift else value
 
 
 def extended(value, sides, width):
@@ -89,7 +122,7 @@
     return iterate
 
 
-def per_device(
+def plain(
     head_old,
     head_target,
     conductivity_east,
@@ -194,24 +227,666 @@
     return (head_new, adjoint_head, rate_gradient, pumping_cost, misfit)
 
 
+def split(value, parts):
+    found = []
+    for _ in range(parts):
+        top = value.astype(BF16)
+        found.append(top)
+        value = value - top.astype(F32)
+    return found
+
+
+def dot(a, b, dims):
+    return lax.dot_general(a, b, (dims, ((), ())), preferred_element_type=F32)
+
+
+NN = ((1,), (0,))
+NT = ((1,), (1,))
+
+
+def reciprocal(x):
+    first = pl.reciprocal(x, approx=True)
+    return first * (2.0 - x * first)
+
+
+def kernel(sizes, *refs):
+    n_east, n_x, n_z = sizes
+    n_north = n_x * n_z
+    fields, well_refs, refs = refs[:6], refs[6:14], refs[14:]
+    out_new, out_adjoint, out_slope, out_cost, out_misfit, out_crowded = refs[:6]
+    hx, tx, ke, kn, kv, st, fe, fn, fu, inv, src, lw, d0, d1, s1, pt = refs[6:22]
+    head_new, adjoint, parts = refs[22:25]
+    staged, (nbs, efs, ebs, cfs, cbs), refs = refs[25:29], refs[29:34], refs[34:]
+    (s_nf, s_nb, s_ef, s_eb, s_cf, s_cb), refs = refs[:6], refs[6:]
+    well_rows, wells, boxes, refs = refs[:8], refs[8], refs[9:13], refs[13:]
+    load_sem, send_sem, recv_sem, sum_send, sum_recv = refs
+    depth, rows, cols = head_new.shape
+    layers, ext_rows, ext_cols = hx.shape
+    chunks_of_rows = ext_rows // 8
+    groups = wells.shape[1] // LANES
+    me_e, me_n, me_l = lax.axis_index("east"), lax.axis_index("north"), lax.axis_index("layer")
+    me_x, me_z = me_n // n_z, lax.rem(me_n, n_z)
+    own, other = depth * me_l, depth * (1 - me_l)
+    own_layers = pl.ds(own, depth)
+
+    def east_of(side):
+        return lax.rem(me_e + (n_east - 1 if side == 0 else 1), n_east)
+
+    def north_of(side):
+        return lax.rem(me_n + (n_north - 1 if side == 0 else 1), n_north)
+
+    partner = (me_e, me_n, 1 - me_l)
+    to_north = [(me_e, north_of(s), me_l) for s in (0, 1)]
+    to_east = [(east_of(s), me_n, me_l) for s in (0, 1)]
+    to_corner = [(east_of(c), north_of(r), me_l) for r in (0, 1) for c in (0, 1)]
+    phases = []
+    for box, size, mine, device in (
+        (boxes[0], 2, me_l, lambda i: (me_e, me_n, i)),
+        (boxes[1], n_z, me_z, lambda i: (me_e, me_x * n_z + i, me_l)),
+        (boxes[2], n_east, me_e, lambda i: (i, me_n, me_l)),
+        (boxes[3], n_x, me_x, lambda i: (me_e, i * n_z + me_z, me_l)),
+    ):
+        phases.append((box, mine, [device(lax.rem(mine + k, size)) for k in range(1, size)]))
+
+    greeted = [partner] + to_north + to_east + to_corner
+    for _, _, peers in phases:
+        greeted = greeted + peers
+    barrier = pltpu.get_barrier_semaphore()
+    for device in greeted:
+        pl.semaphore_signal(barrier, inc=1, device_id=device, device_id_type=MESH)
+
+    loaded = [0]
+
+    def load(src_ref, dst_ref):
+        copy = pltpu.make_async_copy(src_ref, dst_ref, load_sem.at[loaded[0]])
+        loaded[0] += 1
+        copy.start()
+        return copy
+
+    lane = iota((8, LANES), 1)
+    group = lane // HALO
+    wide_sub = iota((8, cols), 0)
+    last = cols - LANES
+    low_half = lane < LANES // 2
+    extra = pl.ds(cols, LANES)
+    inside_cols = pl.ds(0, cols)
+    inner = pl.ds(8, rows)
+    edge_rows = (pl.ds(rows + 8, 8), pl.ds(0, 8))
+
+    block_loads = [
+        load(fields[0], hx.at[own_layers, inner, inside_cols]),
+        load(fields[1], tx.at[own_layers, inner, inside_cols]),
+    ] + [load(fields[2 + a], staged[a].at[own_layers]) for a in range(4)]
+    well_loads = [load(a, b) for a, b in zip(well_refs, well_rows)]
+    for copy in block_loads:
+        copy.wait()
+
+    def pack(z, carry):
+        for side in (0, 1):
+            c0 = last * side
+            kept = jnp.zeros((8, LANES), F32)
+            fields = [jnp.zeros((8, LANES), F32) for _ in staged]
+            for pair in range(rows // 16):
+                tiles = [
+                    ref[own + z, pl.ds(16 * pair, 16), pl.ds(c0, LANES)].astype(F32) for ref in staged
+                ]
+                for half in (0, 1):
+                    j = 2 * pair + half
+                    shift = HALO * j - (LANES - HALO) * side
+                    h = hx[own + z, pl.ds(8 + 8 * j, 8), pl.ds(c0, LANES)]
+                    t = tx[own + z, pl.ds(8 + 8 * j, 8), pl.ds(c0, LANES)]
+                    if side == 0:
+                        both = jnp.where(lane >= HALO - 2, roll(t, HALO - 2, 1), h)
+                    else:
+                        both = jnp.where(lane < LANES - HALO + 2, roll(t, 2 - HALO, 1), h)
+                    here = group == j
+                    kept = jnp.where(here, roll(both, shift, 1), kept)
+                    for a in range(4):
+                        piece = tiles[a][8 * half:8 * half + 8]
+                        fields[a] = jnp.where(here, roll(piece, shift, 1), fields[a])
+            s_ef[side, z] = kept
+            s_eb[side, z, pl.ds(0, 16)] = jnp.concatenate(fields[:2], axis=0).astype(BF16)
+            s_eb[side, z, pl.ds(16, 16)] = jnp.concatenate(fields[2:], axis=0).astype(BF16)
+            r0 = (rows - 8) * side
+            h = hx[own + z, pl.ds(8 + r0, 8), inside_cols]
+            t = tx[own + z, pl.ds(8 + r0, 8), inside_cols]
+            if side == 0:
+                both = jnp.where(wide_sub >= HALO - 2, roll(t, HALO - 2, 0), h)
+            else:
+                both = jnp.where(wide_sub < 2, roll(t, 2, 0), h)
+            s_nf[side, z] = both
+            edge = [
+                ref[own + z, pl.ds((rows - 16) * side, 16), :].astype(F32)[8 * side:8 * side + 8]
+                for ref in staged
+            ]
+            s_nb[side, z, pl.ds(0, 16)] = jnp.concatenate(edge[:2], axis=0).astype(BF16)
+            s_nb[side, z, pl.ds(16, 16)] = jnp.concatenate(edge[2:], axis=0).astype(BF16)
+        return carry
+
+    lax.fori_loop(0, depth, pack, 0)
+
+    for r in (0, 1):
+        for c in (0, 1):
+            c0 = last * c
+            kept = jnp.zeros((8, LANES), F32)
+            mixed = jnp.zeros((8, LANES), F32)
+            for z in range(depth):
+                both = s_nf[r, z, :, pl.ds(c0, LANES)]
+                kept = jnp.where(group == z, roll(both, HALO * z - (LANES - HALO) * c, 1), kept)
+                for half in (0, 1):
+                    two = s_nb[r, z, pl.ds(16 * half, 16), pl.ds(c0, LANES)].astype(F32)
+                    for k in (0, 1):
+                        slot = (2 * half + k) * depth + z
+                        moved = roll(two[8 * k:8 * k + 8], HALO * slot - (LANES - HALO) * c, 1)
+                        mixed = jnp.where(group == slot, moved, mixed)
+            s_cf[2 * r + c] = kept
+            s_cb[2 * r + c] = jnp.concatenate([mixed, mixed], axis=0).astype(BF16)
+
+    pl.semaphore_wait(barrier, len(greeted))
+
+    sent = [0]
+
+    def send(src_ref, dst_ref, device):
+        copy = pltpu.make_async_remote_copy(
+            src_ref=src_ref,
+            dst_ref=dst_ref,
+            send_sem=send_sem.at[sent[0]],
+            recv_sem=recv_sem.at[sent[0]],
+            device_id=device,
+            device_id_type=MESH,
+        )
+        sent[0] += 1
+        copy.start()
+        return copy
+
+    norths, easts, corners = [], [], []
+    for side in (0, 1):
+        norths.append(send(s_nb.at[side], nbs.at[0, side], to_north[side]))
+        norths.append(
+            send(s_nf.at[side], hx.at[own_layers, edge_rows[side], inside_cols], to_north[side])
+        )
+    for side in (0, 1):
+        easts.append(send(s_eb.at[side], ebs.at[0, side], to_east[side]))
+        easts.append(send(s_ef.at[side], efs.at[0, side], to_east[side]))
+    for d in range(4):
+        corners.append(send(s_cb.at[d], cbs.at[0, d], to_corner[d]))
+        corners.append(send(s_cf.at[d], cfs.at[0, d], to_corner[d]))
+    two = (depth - 2) * (1 - me_l)
+    blocks = [send(fields[2 + a], staged[a].at[own_layers], partner) for a in range(4)]
+    blocks.append(send(fields[0], hx.at[own_layers, inner, inside_cols], partner))
+    blocks.append(
+        send(
+            fields[1].at[pl.ds(two, 2)], tx.at[pl.ds(own + two, 2), inner, inside_cols], partner
+        )
+    )
+
+    for copy in well_loads:
+        copy.wait()
+    wells[...] = jnp.full(wells.shape, -1e6, F32)
+    width = pl.ds(0, well_rows[0].shape[1])
+    for row, ref in enumerate(well_rows[:5]):
+        wells[pl.ds(row, 1), width] = ref[...].astype(F32)
+    band = well_rows[5][...]
+    bands = well_rows[7][...]
+    price = jnp.zeros(band.shape, F32)
+    for b in range(bands.shape[1]):
+        price = jnp.where(band == b, bands[0:1, b:b + 1], price)
+    wells[pl.ds(5, 1), width] = price
+    wells[pl.ds(6, 1), width] = well_rows[6][...]
+
+    at_east = wells[0:1, :] - (me_e * cols).astype(F32)
+    at_north = wells[1:2, :] - (me_n * rows).astype(F32)
+    near = (
+        (at_east >= -REACH) & (at_east < cols + REACH)
+        & (at_north >= -REACH) & (at_north < rows + REACH)
+    )
+    mine = (at_east >= 0) & (at_east < cols) & (at_north >= 0) & (at_north < rows)
+    near_row = jnp.where(near, 1.0, 0.0)
+    near_tile = jnp.concatenate(
+        [near_row[:, LANES * k:LANES * (k + 1)] for k in range(groups)], axis=0
+    )
+    before = (iota((LANES, LANES), 0) < iota((LANES, LANES), 1)).astype(F32).astype(BF16)
+    in_row = dot(near_tile.astype(BF16), before, NN)
+    above = (iota((groups, groups), 1) < iota((groups, groups), 0)).astype(F32).astype(BF16)
+    rows_above = jnp.sum(dot(above, near_tile.astype(BF16), NN), axis=1, keepdims=True)
+    rank = jnp.where(near_tile > 0, in_row + rows_above, -1.0)
+    found = jnp.sum(jnp.sum(near_tile, axis=1, keepdims=True), axis=0, keepdims=True)
+    crowded = jnp.where(found > SLOTS, 1.0, 0.0)
+
+    place = jnp.concatenate(
+        [
+            jnp.where(at_east < 0, at_east + ext_cols, at_east),
+            at_north + 8.0,
+            wells[2:7, :],
+            jnp.where(mine, 1.0, 0.0),
+        ],
+        axis=0,
+    )
+    place_parts = jnp.concatenate([p.astype(F32) for p in split(place, 3)], axis=0).astype(BF16)
+    slot_of = iota((SLOTS, LANES), 0).astype(F32)
+
+    for k in range(groups):
+        pt[:, pl.ds(LANES * k, LANES)] = jnp.where(slot_of == rank[k:k + 1, :], 1.0, 0.0).astype(BF16)
+    three = dot(place_parts, pt[...], NT)
+    comp = three[0:8] + three[8:16] + three[16:24]
+    col_hot = jnp.where(iota((ext_cols, SLOTS), 0).astype(F32) == comp[0:1], 1.0, 0.0)
+    row_hot = jnp.where(iota((ext_rows, SLOTS), 0).astype(F32) == comp[1:2], 1.0, 0.0)
+    col_hot = col_hot.astype(BF16)
+
+
+    def fill_inner(base):
+        def fill(z, carry):
+            for dst, ref in zip((ke, kn, kv, st), staged):
+                dst[base + z, inner, inside_cols] = ref[base + z].astype(F32)
+            return carry
+
+        lax.fori_loop(0, depth, fill, 0)
+
+    def fill_east(who, base):
+        def fill(z, carry):
+            zz = base + z
+            right, left = efs[who, 0, z], efs[who, 1, z]
+            for j in range(rows // 8):
+                both = jnp.where(
+                    low_half, roll(right, -HALO * j, 1), roll(left, LANES - HALO - HALO * j, 1)
+                )
+                hx[zz, pl.ds(8 + 8 * j, 8), extra] = both
+                tx[zz, pl.ds(8 + 8 * j, 8), extra] = jnp.where(
+                    low_half, roll(both, 2 - HALO, 1), roll(both, HALO - 2, 1)
+                )
+            for half, pair in ((0, (ke, kn)), (1, (kv, st))):
+                rights = ebs[who, 0, z, pl.ds(16 * half, 16)].astype(F32)
+                lefts = ebs[who, 1, z, pl.ds(16 * half, 16)].astype(F32)
+                for k in (0, 1):
+                    right, left = rights[8 * k:8 * k + 8], lefts[8 * k:8 * k + 8]
+                    for j in range(rows // 8):
+                        pair[k][zz, pl.ds(8 + 8 * j, 8), extra] = jnp.where(
+                            low_half,
+                            roll(right, -HALO * j, 1),
+                            roll(left, LANES - HALO - HALO * j, 1),
+                        )
+            return carry
+
+        lax.fori_loop(0, depth, fill, 0)
+
+    def fill_north(who, base):
+        def fill(z, carry):
+            zz = base + z
+            for side, at_rows in enumerate(edge_rows):
+                tx[zz, at_rows, inside_cols] = roll(
+                    hx[zz, at_rows, inside_cols], 2 if side == 0 else 6, 0
+                )
+                for half, pair in ((0, (ke, kn)), (1, (kv, st))):
+                    both = nbs[who, side, z, pl.ds(16 * half, 16)].astype(F32)
+                    pair[0][zz, at_rows, inside_cols] = both[:8]
+                    pair[1][zz, at_rows, inside_cols] = both[8:]
+            return carry
+
+        lax.fori_loop(0, depth, fill, 0)
+
+    def fill_corners(who, base):
+        for r, at_rows in enumerate(edge_rows):
+            right, left = cfs[who, 2 * r], cfs[who, 2 * r + 1]
+            rights = cbs[who, 2 * r].astype(F32)[:8]
+            lefts = cbs[who, 2 * r + 1].astype(F32)[:8]
+            for z in range(depth):
+                both = jnp.where(
+                    low_half, roll(right, -HALO * z, 1), roll(left, LANES - HALO - HALO * z, 1)
+                )
+                hx[base + z, at_rows, extra] = both
+                tx[base + z, at_rows, extra] = roll(both, 2 if r == 0 else 6, 0)
+                for a, dst in enumerate((ke, kn, kv, st)):
+                    slot = a * depth + z
+                    dst[base + z, at_rows, extra] = jnp.where(
+                        low_half,
+                        roll(rights, -HALO * slot, 1),
+                        roll(lefts, LANES - HALO - HALO * slot, 1),
+                    )
+
+    fill_inner(own)
+    for copy in easts:
+        copy.wait_recv()
+    forwards = [send(efs.at[0], efs.at[1], partner), send(ebs.at[0], ebs.at[1], partner)]
+    fill_east(0, own)
+    for copy in norths:
+        copy.wait_recv()
+    forwards.append(send(nbs.at[0], nbs.at[1], partner))
+    for side in (0, 1):
+        place_of = hx.at[own_layers, edge_rows[side], inside_cols]
+        forwards.append(send(place_of, place_of, partner))
+    for copy in corners:
+        copy.wait_recv()
+    forwards.append(send(cfs.at[0], cfs.at[1], partner))
+    forwards.append(send(cbs.at[0], cbs.at[1], partner))
+    fill_north(0, own)
+    fill_corners(0, own)
+    for copy in blocks:
+        copy.wait_recv()
+    fill_inner(other)
+    for copy in forwards:
+        copy.wait_recv()
+    fill_east(1, other)
+    fill_north(1, other)
+    fill_corners(1, other)
+    for copy in norths + easts + corners + blocks + forwards:
+        copy.wait_send()
+
+    weights = []
+    for z in range(layers):
+        found = dot(ke[z].astype(BF16), col_hot, NN)
+        k_at = jnp.sum(found * row_hot, axis=0, keepdims=True)
+        screened = (comp[2:3] <= z) & (comp[3:4] >= z)
+        weights.append(jnp.where(screened, k_at, 0.0))
+    weight = jnp.concatenate(weights, axis=0)
+    total = jnp.sum(weight, axis=0, keepdims=True)
+    share = weight / jnp.where(total > 0, total, 1.0)
+    pumped = share * comp[4:5]
+    priced = pumped * comp[5:6]
+    col_two = jnp.concatenate([col_hot, col_hot], axis=1)
+    for z in range(layers):
+        left = []
+        for value in (pumped, priced):
+            top, rest = split(value[z:z + 1], 2)
+            left.append(
+                jnp.concatenate([row_hot * top.astype(F32), row_hot * rest.astype(F32)], axis=1)
+            )
+        left = jnp.concatenate(left, axis=0).astype(BF16)
+        field = dot(left, col_two, NT)
+        src[z] = field[:ext_rows]
+        lw[z] = field[ext_rows:]
+
+    wide = (8, ext_cols)
+    sub = iota(wide, 0)
+    col = iota(wide, 1)
+    closed_col = ((col == cols - 1) & (me_e == n_east - 1)) | ((col == ext_cols - 1) & (me_e == 0))
+    open_east = jnp.where(closed_col, 0.0, 2.0)
+    open_low = jnp.where((sub == 7) & (me_n == 0), 0.0, 2.0)
+    open_high = jnp.where((sub == 7) & (me_n == n_north - 1), 0.0, 2.0)
+
+    def east(v):
+        return roll(v, ext_cols - 1, 1)
+
+    def west(v):
+        return roll(v, 1, 1)
+
+    def north(now, after):
+        return jnp.where(sub < 7, roll(now, 7, 0), roll(after, 7, 0))
+
+    def south(now, prior):
+        return jnp.where(sub > 0, roll(now, 1, 0), roll(prior, 1, 0))
+
+    fu[0] = jnp.zeros((ext_rows, ext_cols), F32)
+
+    def row_chunks(begin, end, unit, body, carry):
+        if end - begin == unit:
+            for j in range(begin, end):
+                carry = body(j, carry)
+            return carry
+
+        def several(k, carry):
+            for i in range(unit):
+                carry = body(begin + k * unit + i, carry)
+            return carry
+
+        return lax.fori_loop(0, (end - begin) // unit, several, carry)
+
+    def at(j):
+        return pl.ds(8 * j if isinstance(j, int) else pl.multiple_of(8 * j, 8), 8)
+
+    def next_of(j):
+        return min(j + 1, chunks_of_rows - 1) if isinstance(j, int) else jnp.minimum(j + 1, chunks_of_rows - 1)
+
+    def start(z, carry):
+        up = jnp.minimum(z + 1, layers - 1)
+        down = jnp.maximum(z - 1, 0)
+        open_up = jnp.where(z < layers - 1, 2.0, 0.0)
+
+        def chunk(j, carry):
+            fn_prior, gn_prior, k_n, h = carry
+            k_e, k_u, k_u2 = ke[z, at(j)], kv[z, at(j)], kv[up, at(j)]
+            k_e2 = east(k_e)
+            k_after, h_after = kn[z, at(next_of(j))], hx[z, at(next_of(j))]
+            k_n2 = north(k_n, k_after)
+            f_e = open_east * k_e * k_e2 * reciprocal(k_e + k_e2)
+            if isinstance(j, int):
+                opened = open_low if j == 0 else open_high if j == chunks_of_rows - 2 else 2.0
+            else:
+                edge = ((j == 0) & (me_n == 0)) | ((j == chunks_of_rows - 2) & (me_n == n_north - 1))
+                opened = jnp.where((sub == 7) & edge, 0.0, 2.0)
+            f_n = opened * k_n * k_n2 * reciprocal(k_n + k_n2)
+            f_u = open_up * k_u * k_u2 * reciprocal(k_u + k_u2)
+            f_d = fu[z, at(j)]
+            fe[z, at(j)] = f_e
+            fn[z, at(j)] = f_n
+            fu[z + 1, at(j)] = f_u
+            diagonal = st[z, at(j)] + f_e + west(f_e) + f_n + south(f_n, fn_prior) + f_u + f_d
+            inverse = reciprocal(diagonal)
+            inv[z, at(j)] = inverse
+            g_e = f_e * (east(h) - h)
+            g_n = f_n * (north(h, h_after) - h)
+            g_u = f_u * (hx[up, at(j)] - h)
+            g_d = f_d * (h - hx[down, at(j)])
+            residual = (g_e - west(g_e)) + (g_n - south(g_n, gn_prior)) + (g_u - g_d)
+            d0[z, at(j)] = inverse * (residual - src[z, at(j)])
+            return f_n, g_n, k_after, h_after
+
+        none = jnp.zeros(wide, F32)
+        row_chunks(0, chunks_of_rows, START_UNIT, chunk, (none, none, kn[z, at(0)], hx[z, at(0)]))
+        return carry
+
+    lax.fori_loop(0, layers, start, 0)
+
+    def sweep(field, margin, finish, chunk_from, chunk_to):
+        def layer(i, carry):
+            z = (depth - margin) * me_l + i
+            up = jnp.minimum(z + 1, layers - 1)
+            down = jnp.maximum(z - 1, 0)
+
+            def chunk(j, carry):
+                b_prior, d = carry
+                d_after = field[z, at(next_of(j))]
+                f_e, f_n = fe[z, at(j)], fn[z, at(j)]
+                b = f_n * d
+                moved = f_e * east(d) + west(f_e * d)
+                moved = moved + f_n * north(d, d_after) + south(b, b_prior)
+                moved = moved + fu[z + 1, at(j)] * field[up, at(j)] + fu[z, at(j)] * field[down, at(j)]
+                finish(i, z, j, d, inv[z, at(j)] * moved)
+                return b, d_after
+
+            if chunk_from == 0:
+                b_prior = jnp.zeros(wide, F32)
+            else:
+                b_prior = fn[z, at(chunk_from - 1)] * field[z, at(chunk_from - 1)]
+            unit = SWEEP_UNIT if chunk_from == 0 else LAST_UNIT
+            row_chunks(chunk_from, chunk_to, unit, chunk, (b_prior, field[z, at(chunk_from)]))
+            return carry
+
+        lax.fori_loop(0, depth + margin, layer, 0)
+
+    (a1, b1), (a2, b2) = steps_of()
+
+    def first_sweep(i, z, j, d, pulled):
+        s1[z, at(j)] = pulled
+        d1[z, at(j)] = a1 * d + b1 * pulled
+
+    def end_forward(i, z, j, d, pulled):
+        s2 = s1[z, at(j)] - d + pulled
+        d2 = a2 * d + b2 * s2
+        new = hx[z, at(j)] + d0[z, at(j)] + d + d2
+        hx[z, at(j)] = new
+        load = new - tx[z, at(j)] - lw[z, at(j)]
+        src[z, at(j)] = inv[z, at(j)] * load
+
+    sweep(d0, 3, first_sweep, 0, chunks_of_rows)
+    sweep(d1, 2, end_forward, 0, chunks_of_rows)
+    sweep(src, 1, first_sweep, 0, chunks_of_rows)
+
+    st[0, at(0)] = jnp.zeros(wide, F32)
+
+    def end_adjoint(i, z, j, d, pulled):
+        s2 = s1[z, at(j)] - d + pulled
+        d2 = a2 * d + b2 * s2
+        adj = src[z, at(j)] + d + d2
+        adjoint[i, at(j - 1)] = adj[:, :cols]
+        new = hx[z, at(j), inside_cols]
+        head_new[i, at(j - 1)] = new
+        departure = new - tx[z, at(j), inside_cols]
+        st[0, at(0), inside_cols] = st[0, at(0), inside_cols] + departure * departure
+
+    sweep(d1, 0, end_adjoint, 1, chunks_of_rows - 1)
+
+    writes = [load(head_new, out_new), load(adjoint, out_adjoint)]
+
+    squared = st[0, at(0), inside_cols]
+    squared = jnp.sum(squared, axis=0, keepdims=True)
+    squared = sum(squared[:, LANES * k:LANES * (k + 1)] for k in range(cols // LANES))
+    squared = squared * (1.0 / (float(layers * rows * cols) * n_east * n_north))
+    base_layer = jnp.where(me_l == 0, 1.0, 0.0)
+
+    col_hot, row_hot = col_hot[:cols], row_hot[8:8 + rows]
+    head_at = jnp.zeros((1, SLOTS), F32)
+    adj_at = jnp.zeros((1, SLOTS), F32)
+    for i in range(depth):
+        z_share = jnp.where(me_l == 0, share[i:i + 1], share[depth + i:depth + i + 1])
+        stack = split(head_new[i], 2) + split(adjoint[i], 2)
+        found = [dot(piece, col_hot, NN) for piece in stack]
+        head_at += z_share * jnp.sum((found[0] + found[1]) * row_hot, axis=0, keepdims=True)
+        adj_at += z_share * jnp.sum((found[2] + found[3]) * row_hot, axis=0, keepdims=True)
+    lift = (comp[6:7] * base_layer - head_at) * comp[7:8]
+    priced = comp[5:6] * lift
+    slope = priced - adj_at * comp[7:8]
+    three = jnp.concatenate(
+        [p.astype(F32) for p in split(slope, 3)] + [jnp.zeros((5, SLOTS), F32)], axis=0
+    ).astype(BF16)
+    spread = dot(three, pt[...], NN)
+    spread = spread[0:1] + spread[1:2] + spread[2:3]
+    tile = jnp.concatenate(
+        [spread[:, LANES * k:LANES * (k + 1)] for k in range(groups)], axis=0
+    )
+    parts[pl.ds(0, groups)] = tile
+    parts[pl.ds(groups, 8)] = jnp.concatenate(
+        [
+            priced * comp[4:5],
+            squared,
+            jnp.broadcast_to(crowded, (1, LANES)),
+            jnp.zeros((5, LANES), F32),
+        ],
+        axis=0,
+    )
+
+    total = parts[...]
+    used = 0
+    for box, mine, peers in phases:
+        box[mine] = total
+        copies = []
+        for device in peers:
+            copy = pltpu.make_async_remote_copy(
+                src_ref=box.at[mine],
+                dst_ref=box.at[mine],
+                send_sem=sum_send.at[used],
+                recv_sem=sum_recv.at[used],
+                device_id=device,
+                device_id_type=MESH,
+            )
+            copy.start()
+            copies.append(copy)
+            used += 1
+        for copy in copies:
+            copy.wait()
+        total = box[0]
+        for k in range(1, len(peers) + 1):
+            total = total + box[k]
+    n_wells = out_slope.shape[1]
+    for k in range(groups):
+        width = min(LANES, n_wells - LANES * k)
+        out_slope[:, pl.ds(LANES * k, width)] = total[k:k + 1, :width]
+    sums = jnp.sum(total[groups:], axis=1, keepdims=True)
+    out_cost[...] = sums[0:1]
+    out_misfit[...] = sums[1:2]
+    out_crowded[...] = sums[2:3]
+    for copy in writes:
+        copy.wait()
+
+
+def run_kernel(sizes, fields, wells):
+    depth, rows, cols = fields[0].shape
+    layers, ext_rows, ext_cols = 2 * depth, rows + 16, cols + LANES
+    n_wells = wells[0].shape[1]
+    groups = -(-n_wells // LANES)
+    n_east, n_x, n_z = sizes
+    block = jax.ShapeDtypeStruct((depth, rows, cols), F32)
+    one = jax.ShapeDtypeStruct((1, 1), F32)
+    ext = pltpu.VMEM((layers, ext_rows, ext_cols), F32)
+    operands = (*fields, *wells)
+    copies = 4 + 4 + 8 + 6 + 7
+    peers = 1 + n_z + n_east + n_x - 3
+    return pl.pallas_call(
+        functools.partial(kernel, sizes),
+        out_shape=[block, block, jax.ShapeDtypeStruct((1, n_wells), F32), one, one, one],
+        in_specs=[pl.BlockSpec(memory_space=pltpu.HBM)] * len(operands),
+        out_specs=[pl.BlockSpec(memory_space=pltpu.HBM)] * 2
+        + [pl.BlockSpec(memory_space=pltpu.VMEM)] * 4,
+        scratch_shapes=[ext] * 8
+        + [pltpu.VMEM((layers + 1, ext_rows, ext_cols), F32)]
+        + [ext] * 6
+        + [pltpu.VMEM((SLOTS, groups * LANES), BF16)]
+        + [pltpu.VMEM((depth, rows, cols), F32)] * 2
+        + [pltpu.VMEM((groups + 8, LANES), F32)]
+        + [pltpu.VMEM((layers, rows, cols), BF16)] * 4
+        + [
+            pltpu.VMEM((2, 2, depth, 32, cols), BF16),
+            pltpu.VMEM((2, 2, depth, 8, LANES), F32),
+            pltpu.VMEM((2, 2, depth, 32, LANES), BF16),
+            pltpu.VMEM((2, 4, 8, LANES), F32),
+            pltpu.VMEM((2, 4, 16, LANES), BF16),
+            pltpu.VMEM((2, depth, 8, cols), F32),
+            pltpu.VMEM((2, depth, 32, cols), BF16),
+            pltpu.VMEM((2, depth, 8, LANES), F32),
+            pltpu.VMEM((2, depth, 32, LANES), BF16),
+            pltpu.VMEM((4, 8, LANES), F32),
+            pltpu.VMEM((4, 16, LANES), BF16),
+        ]
+        + [pltpu.VMEM(w.shape, w.dtype) for w in wells]
+        + [pltpu.VMEM((8, groups * LANES), F32)]
+        + [pltpu.VMEM((n, groups + 8, LANES), F32) for n in (2, n_z, n_east, n_x)]
+        + [pltpu.SemaphoreType.DMA((16,))]
+        + [pltpu.SemaphoreType.DMA((copies,))] * 2
+        + [pltpu.SemaphoreType.DMA((peers,))] * 2,
+        compiler_params=pltpu.CompilerParams(
+            collective_id=0, has_side_effects=True, vmem_limit_bytes=60 * 1024 * 1024
+        ),
+        name="whole_step",
+    )(*operands)
+
+
+def in_order(value):
+    return with_layout_constraint(value, Layout(major_to_minor=(0, 1, 2)))
+
+
+def per_device(sizes, *arguments):
+    fields = arguments[:6]
+    e, n, top, bottom, tariff, rates, ground, prices = arguments[6:]
+    wells = [w.reshape(1, -1) for w in (e, n, top, bottom, rates, tariff, ground, prices)]
+    new, adjoint, slope, cost, misfit, crowded = run_kernel(sizes, fields, wells)
+    found = (new, adjoint, slope.reshape(-1), cost.reshape(()), misfit.reshape(()))
+
+    def again(state):
+        blocks = [in_order(x) for x in fields]
+        first, second, *others = plain(*blocks, *arguments[6:])
+        return jnp.zeros((), F32), (in_order(first), in_order(second), *others)
+
+    return lax.while_loop(lambda state: state[0] > 0, again, (crowded.reshape(()), found))[1]
+
+
 def solution(mesh):
-    in_specs = (
-        P("layer", "north", "east"),
-        P("layer", "north", "east"),
-        P("layer", "north", "east"),
-        P("layer", "north", "east"),
-        P("layer", "north", "east"),
-        P("layer", "north", "east"),
-        P(),
-        P(),
-        P(),
-        P(),
-        P(),
-        P(),
-        P(),
-        P(),
-    )
-    out_specs = (P("layer", "north", "east"), P("layer", "north", "east"), P(), P(), P())
+    field = P("layer", "north", "east")
+    n_north = mesh.shape["north"]
+    n_x = 4 if n_north % 4 == 0 else 1
+    sizes = (mesh.shape["east"], n_x, n_north // n_x)
     return jax.shard_map(
-        per_device, mesh=mesh, in_specs=in_specs, out_specs=out_specs, check_vma=False
-    )
+        functools.partial(per_device, sizes),
+        mesh=mesh,
+        in_specs=(field,) * 6 + (P(),) * 8,
+        out_specs=(field, field, P(), P(), P()),
+        check_vma=False,
+    )

time: 419 us -> 53 us (0.13)
  local copies, waits for them, and re-layouts: 109 us -> 4.37 us
  other arithmetic: 96.2 us -> 0 us
  starting transfers between devices: 90.6 us -> 0 us
  blocking collectives: 71.5 us -> 0 us
  waiting for transfers between devices: 45 us -> 0 us
  Pallas kernels: 0 us -> 43.4 us
    ppermute x36 -> x0, starting transfers between devices: 90.6 us -> none  [the longest x18 67.4 us: extended(): before = lax.ppermute(last, axis, up)]
    psum x2 -> x0, blocking collectives: 71.5 us -> none  [the longest x1 68.2 us: per_device(): adjoint_screen = lax.psum(adjoint_part, ('east', 'north', 'layer'))]
    scatter-add x2 -> x0, other arithmetic: 57.4 us -> none  [the longest x1 31.2 us: per_device(): load = departure.reshape(flat_shape).at[:, cells].add(-(prices * pump_rat...]
    gather x3 -> x0, local copies, waits for them, and re-layouts: 46.3 us -> none  [the longest x1 16.7 us: per_device(): adjoint_head.reshape(flat_shape)[:, cells]]
    ppermute x36 -> x0, waiting for transfers between devices: 45 us -> none  [the longest x18 29 us: extended(): after = lax.ppermute(initial, axis, down)]
    pallas_call x0 -> x1, Pallas kernels: none -> 43.4 us  [run_kernel(): pl.pallas_call(functools.partial(kernel, sizes), out_shape=[block, block,...]
    reshape x2 -> x0, local copies, waits for them, and re-layouts: 21.4 us -> none  [the longest x1 10.7 us: per_device(): source = jnp.zeros(flat_shape, jnp.float32).at[:, cells].add(pump_rates[N...]
    add x2 -> x0, local copies, waits for them, and re-layouts: 18.4 us -> none  [chebyshev(): iterate = trim(iterate) + direction]
  transfers between devices with their start and end apart: 36 -> 0, of which waited for: 14 -> 0; matrix products, arithmetic and copies ran while one was open for 25% -> 0% of each run, Pallas kernels for 0% -> 0%
where the time goes in v4:
time: 53 us; the launch traced here: 52.8 us
  Pallas kernels  43.4 us (82%)
  local copies, waits for them, and re-layouts  4.37 us (8%)
  between operations  4.29 us (8%)
  loops' own time  0.73 us (1%)
    pallas_call x1, Pallas kernels, run_kernel(): pl.pallas_call(functools.partial(kernel, sizes), out_shape=[block, block,...  43.4 us
    unnamed x15, local copies, waits for them, and re-layouts  4.37 us

profile of v4, /device:TPU:0, one launch (start us, length us, event | category | flops | bytes accessed | tf_op | source)
XLA Modules:
  0.0 52.8 jit_solution(5674396202577515618)
XLA Ops:
  0.6 0.0 copy-start.26
  0.6 0.0 copy-start.15
  0.7 0.0 copy-start.13
  0.7 0.0 copy-start.9
  0.7 0.0 copy-start
  0.7 43.4 %whole_step.1 = (f32[4,128,256]{2,1,0:T(8,128)}, f32[4,128,256]{2,1,0:T(8,128)}, f32[1,3000]{1,0:T(1,128)}, f32[1,1]{1,0:T(1,128)}, f32[1,1]{1,0:T(1,128)}, /*index=5*/f32[1,1]{1,0:T(1,128)}) custom-call(f32[4,128,256]{2,1,0:T(8,128)} %refs_0_.1, f32[4,128,256]{2,1,0:T(8,128)} %refs_1_.1, bf16[4,128,256]{2,1,0:T(8,128)(2,1)} %refs_2_.1, ...), custom_call_target="tpu_custom_call" | custom-call | tf_op jit(solution)/shard_map/whole_step/pallas_call | solution.py:823
  44.1 0.0 copy-done.26
  44.1 0.0 copy-done.15
  44.1 0.0 copy-done.13
  44.1 0.0 copy-done.9
  44.1 0.0 copy-done
  44.1 0.7 %while.17 = (f32[]{:T(128)}, f32[4,128,256]{2,1,0:T(8,128)}, f32[4,128,256]{2,1,0:T(8,128)}, f32[3000]{0:T(1024)}, f32[]{:T(128)}, /*index=5*/f32[]{:T(128)}, f3...) while((f32[]{:T(128)}, f32[4,128,256]{2,1,0:T(8,128)}, ...), condition=%region_13.14_spmd, body=%region_0.13_spmd | while | flops 59988996 | bytes 132797736 | solution.py:878
  44.9 0.0 copy-start.40
  44.9 1.9 %copy.69 = f32[4,128,256]{2,1,0:T(8,128)} copy(f32[4,128,256]{2,1,0:T(8,128)} %get-tuple-element.395) | data formatting | bytes 1048576
  46.8 1.9 %copy.70 = f32[4,128,256]{2,1,0:T(8,128)} copy(f32[4,128,256]{2,1,0:T(8,128)} %get-tuple-element.396) | data formatting | bytes 1048576
  48.6 0.0 copy-done.40
  48.6 0.6 %copy.71 = f32[3000]{0:T(1024)} copy(f32[3000]{0:T(1024)S(1)} %copy-done.40) | data formatting | bytes 24000
Async XLA Ops:
  0.6 43.5 %copy-start.26 = (f32[3000]{0:T(1024)S(1)}, f32[3000]{0:T(1024)}, u32[]{:S(2)}) copy-start(f32[3000]{0:T(1024)} %param.27) | copy-start | bytes 36004
  0.6 43.5 %copy-start.15 = (bf16[4,128,256]{2,1,0:T(8,128)(2,1)S(1)}, bf16[4,128,256]{2,1,0:T(8,128)(2,1)}, u32[]{:S(2)}) copy-start(bf16[4,128,256]{2,1,0:T(8,128)(2,1)} %refs_4_.1) | copy-start | bytes 786436
  0.7 43.4 %copy-start.13 = (bf16[4,128,256]{2,1,0:T(8,128)(2,1)S(1)}, bf16[4,128,256]{2,1,0:T(8,128)(2,1)}, u32[]{:S(2)}) copy-start(bf16[4,128,256]{2,1,0:T(8,128)(2,1)} %refs_3_.1) | copy-start | bytes 786436
  0.7 43.4 %copy-start.9 = (bf16[4,128,256]{2,1,0:T(8,128)(2,1)S(1)}, bf16[4,128,256]{2,1,0:T(8,128)(2,1)}, u32[]{:S(2)}) copy-start(bf16[4,128,256]{2,1,0:T(8,128)(2,1)} %refs_2_.1) | copy-start | bytes 786436
  0.7 43.4 %copy-start = (f32[4,128,256]{2,1,0:T(8,128)S(1)}, f32[4,128,256]{2,1,0:T(8,128)}, u32[]{:S(2)}) copy-start(f32[4,128,256]{2,1,0:T(8,128)} %refs_0_.1) | copy-start | bytes 1572868
  44.9 3.8 %copy-start.40 = (f32[3000]{0:T(1024)S(1)}, f32[3000]{0:T(1024)}, u32[]{:S(2)}) copy-start(f32[3000]{0:T(1024)} %get-tuple-element.397) | copy-start | bytes 36004

commit v5 on v4

--- a/solution.py
+++ b/solution.py
@@ -859,6 +859,29 @@
     )(*operands)
 
 
+def hand_over(*refs):
+    count = len(refs) // 2
+    copies = [
+        pltpu.make_async_copy(refs[k], refs[count + k], refs[-1].at[k]) for k in range(count)
+    ]
+    for copy in copies:
+        copy.start()
+    for copy in copies:
+        copy.wait()
+
+
+def run_hand_over(values):
+    return pl.pallas_call(
+        hand_over,
+        out_shape=[jax.ShapeDtypeStruct(v.shape, v.dtype) for v in values],
+        in_specs=[pl.BlockSpec(memory_space=pltpu.HBM)] * len(values),
+        out_specs=[pl.BlockSpec(memory_space=pltpu.HBM)] * len(values),
+        scratch_shapes=[pltpu.SemaphoreType.DMA((len(values),))],
+        compiler_params=pltpu.CompilerParams(vmem_limit_bytes=60 * 1024 * 1024),
+        name="hand_over",
+    )(*values)
+
+
 def in_order(value):
     return with_layout_constraint(value, Layout(major_to_minor=(0, 1, 2)))
 
@@ -868,14 +891,17 @@
     e, n, top, bottom, tariff, rates, ground, prices = arguments[6:]
     wells = [w.reshape(1, -1) for w in (e, n, top, bottom, rates, tariff, ground, prices)]
     new, adjoint, slope, cost, misfit, crowded = run_kernel(sizes, fields, wells)
-    found = (new, adjoint, slope.reshape(-1), cost.reshape(()), misfit.reshape(()))
+    found = (new, adjoint, slope, cost, misfit)
 
     def again(state):
         blocks = [in_order(x) for x in fields]
         first, second, *others = plain(*blocks, *arguments[6:])
+        others = [x.reshape(1, -1) for x in others]
         return jnp.zeros((), F32), (in_order(first), in_order(second), *others)
 
-    return lax.while_loop(lambda state: state[0] > 0, again, (crowded.reshape(()), found))[1]
+    _, found = lax.while_loop(lambda state: state[0] > 0, again, (crowded.reshape(()), found))
+    new, adjoint, slope, cost, misfit = run_hand_over(found)
+    return new, adjoint, slope.reshape(-1), cost.reshape(()), misfit.reshape(())
 
 
 def solution(mesh):

time: 53 us -> 79.8 us (1.51)
  Pallas kernels: 43.4 us -> 78 us
  local copies, waits for them, and re-layouts: 4.37 us -> 0.03 us
  between operations: 4.29 us -> 0.89 us
    pallas_call x0 -> x1, Pallas kernels: none -> 34.6 us  [run_hand_over(): pl.pallas_call(hand_over, out_shape=[jax.ShapeDtypeStruct(v.shape, v.dtyp...]
    unnamed x15 -> x10, local copies, waits for them, and re-layouts: 4.37 us -> 0.03 us
where the time goes in v5:
time: 79.8 us; the launch traced here: 79.6 us
  Pallas kernels  78 us (98%)
  between operations  0.89 us (1%)
    pallas_call x1, Pallas kernels, run_kernel(): pl.pallas_call(functools.partial(kernel, sizes), out_shape=[block, block,...  43.4 us
    pallas_call x1, Pallas kernels, run_hand_over(): pl.pallas_call(hand_over, out_shape=[jax.ShapeDtypeStruct(v.shape, v.dtyp...  34.6 us

profile of v5, /device:TPU:0, one launch (start us, length us, event | category | flops | bytes accessed | tf_op | source)
XLA Modules:
  0.0 79.6 jit_solution(10503030703256273913)
XLA Ops:
  0.6 0.0 copy-start.26
  0.6 0.0 copy-start.15
  0.7 0.0 copy-start.13
  0.7 0.0 copy-start.9
  0.7 0.0 copy-start
  0.7 43.4 %whole_step.1 = (f32[4,128,256]{2,1,0:T(8,128)}, f32[4,128,256]{2,1,0:T(8,128)}, f32[1,3000]{1,0:T(1,128)}, f32[1,1]{1,0:T(1,128)}, f32[1,1]{1,0:T(1,128)}, /*index=5*/f32[1,1]{1,0:T(1,128)}) custom-call(f32[4,128,256]{2,1,0:T(8,128)} %refs_0_.1, f32[4,128,256]{2,1,0:T(8,128)} %refs_1_.1, bf16[4,128,256]{2,1,0:T(8,128)(2,1)} %refs_2_.1, ...), custom_call_target="tpu_custom_call" | custom-call | tf_op jit(solution)/shard_map/whole_step/pallas_call | solution.py:823
  44.1 0.0 copy-done.26
  44.1 0.0 copy-done.15
  44.1 0.0 copy-done.13
  44.1 0.0 copy-done.9
  44.1 0.0 copy-done
  44.1 0.7 while.17
  44.9 34.6 %hand_over.1 = (f32[4,128,256]{2,1,0:T(8,128)}, f32[4,128,256]{2,1,0:T(8,128)}, f32[1,3000]{1,0:T(1,128)}, f32[1,1]{1,0:T(1,128)}, f32[1,1]{1,0:T(1,128)}) custom-call(f32[4,128,256]{2,1,0:T(8,128)} %get-tuple-element.395, f32[4,128,256]{2,1,0:T(8,128)} %get-tuple-element.396, f32[1,3000]{1,0:T(1,128)} %get-tuple-element.397, f32[1,1]{1,0:T(1,128)} %get-tuple-element.398, ...), custom_call_target="tpu_custom_call" | custom-call | tf_op jit(solution)/shard_map/hand_over/pallas_call | solution.py:874
Async XLA Ops:
  0.6 43.5 %copy-start.26 = (f32[3000]{0:T(1024)S(1)}, f32[3000]{0:T(1024)}, u32[]{:S(2)}) copy-start(f32[3000]{0:T(1024)} %param.27) | copy-start | bytes 36004
  0.6 43.5 %copy-start.15 = (bf16[4,128,256]{2,1,0:T(8,128)(2,1)S(1)}, bf16[4,128,256]{2,1,0:T(8,128)(2,1)}, u32[]{:S(2)}) copy-start(bf16[4,128,256]{2,1,0:T(8,128)(2,1)} %refs_4_.1) | copy-start | bytes 786436
  0.7 43.4 %copy-start.13 = (bf16[4,128,256]{2,1,0:T(8,128)(2,1)S(1)}, bf16[4,128,256]{2,1,0:T(8,128)(2,1)}, u32[]{:S(2)}) copy-start(bf16[4,128,256]{2,1,0:T(8,128)(2,1)} %refs_3_.1) | copy-start | bytes 786436
  0.7 43.4 %copy-start.9 = (bf16[4,128,256]{2,1,0:T(8,128)(2,1)S(1)}, bf16[4,128,256]{2,1,0:T(8,128)(2,1)}, u32[]{:S(2)}) copy-start(bf16[4,128,256]{2,1,0:T(8,128)(2,1)} %refs_2_.1) | copy-start | bytes 786436
  0.7 43.4 %copy-start = (f32[4,128,256]{2,1,0:T(8,128)S(1)}, f32[4,128,256]{2,1,0:T(8,128)}, u32[]{:S(2)}) copy-start(f32[4,128,256]{2,1,0:T(8,128)} %refs_0_.1) | copy-start | bytes 1572868

commit v6 on v5

--- a/solution.py
+++ b/solution.py
@@ -860,13 +860,17 @@
 
 
 def hand_over(*refs):
-    count = len(refs) // 2
-    copies = [
-        pltpu.make_async_copy(refs[k], refs[count + k], refs[-1].at[k]) for k in range(count)
-    ]
-    for copy in copies:
+    count = (len(refs) - 2) // 3
+    given, out, held = refs[:count], refs[count:2 * count], refs[2 * count:3 * count]
+    in_sem, out_sem = refs[3 * count:]
+    reads = [pltpu.make_async_copy(given[k], held[k], in_sem.at[k]) for k in range(count)]
+    writes = [pltpu.make_async_copy(held[k], out[k], out_sem.at[k]) for k in range(count)]
+    for copy in reads:
         copy.start()
-    for copy in copies:
+    for read, write in zip(reads, writes):
+        read.wait()
+        write.start()
+    for copy in writes:
         copy.wait()
 
 
@@ -876,7 +880,8 @@
         out_shape=[jax.ShapeDtypeStruct(v.shape, v.dtype) for v in values],
         in_specs=[pl.BlockSpec(memory_space=pltpu.HBM)] * len(values),
         out_specs=[pl.BlockSpec(memory_space=pltpu.HBM)] * len(values),
-        scratch_shapes=[pltpu.SemaphoreType.DMA((len(values),))],
+        scratch_shapes=[pltpu.VMEM(v.shape, v.dtype) for v in values]
+        + [pltpu.SemaphoreType.DMA((len(values),))] * 2,
         compiler_params=pltpu.CompilerParams(vmem_limit_bytes=60 * 1024 * 1024),
         name="hand_over",
     )(*values)

time: 79.8 us -> 48.6 us (0.61)
  Pallas kernels: 78 us -> 46.8 us
    pallas_call x1, Pallas kernels: 34.6 us -> 3.4 us  [run_hand_over(): pl.pallas_call(hand_over, out_shape=[jax.ShapeDtypeStruct(v.shape, v.dtyp...]
where the time goes in v6:
time: 48.6 us; the launch traced here: 48.4 us
  Pallas kernels  46.8 us (96%)
  between operations  0.89 us (2%)
  loops' own time  0.73 us (2%)
    pallas_call x1, Pallas kernels, run_kernel(): pl.pallas_call(functools.partial(kernel, sizes), out_shape=[block, block,...  43.4 us
    pallas_call x1, Pallas kernels, run_hand_over(): pl.pallas_call(hand_over, out_shape=[jax.ShapeDtypeStruct(v.shape, v.dtyp...  3.4 us

profile of v6, /device:TPU:0, one launch (start us, length us, event | category | flops | bytes accessed | tf_op | source)
XLA Modules:
  0.0 48.4 jit_solution(8732187880987630128)
XLA Ops:
  0.6 0.0 copy-start.26
  0.6 0.0 copy-start.15
  0.7 0.0 copy-start.13
  0.7 0.0 copy-start.9
  0.7 0.0 copy-start
  0.7 43.4 %whole_step.1 = (f32[4,128,256]{2,1,0:T(8,128)}, f32[4,128,256]{2,1,0:T(8,128)}, f32[1,3000]{1,0:T(1,128)}, f32[1,1]{1,0:T(1,128)}, f32[1,1]{1,0:T(1,128)}, /*index=5*/f32[1,1]{1,0:T(1,128)}) custom-call(f32[4,128,256]{2,1,0:T(8,128)} %refs_0_.1, f32[4,128,256]{2,1,0:T(8,128)} %refs_1_.1, bf16[4,128,256]{2,1,0:T(8,128)(2,1)} %refs_2_.1, ...), custom_call_target="tpu_custom_call" | custom-call | tf_op jit(solution)/shard_map/whole_step/pallas_call | solution.py:823
  44.1 0.0 copy-done.26
  44.1 0.0 copy-done.15
  44.1 0.0 copy-done.13
  44.1 0.0 copy-done.9
  44.1 0.0 copy-done
  44.1 0.7 %while.17 = (f32[]{:T(128)}, f32[4,128,256]{2,1,0:T(8,128)}, f32[4,128,256]{2,1,0:T(8,128)}, f32[1,3000]{1,0:T(1,128)}, f32[1,1]{1,0:T(1,128)}, /*index=5*/f32[1...) while((f32[]{:T(128)}, f32[4,128,256]{2,1,0:T(8,128)}, ...), condition=%region_13.14_spmd, body=%region_0.13_spmd | while | flops 59988996 | bytes 132797736 | solution.py:907
  44.9 3.4 %hand_over.1 = (f32[4,128,256]{2,1,0:T(8,128)}, f32[4,128,256]{2,1,0:T(8,128)}, f32[1,3000]{1,0:T(1,128)}, f32[1,1]{1,0:T(1,128)}, f32[1,1]{1,0:T(1,128)}) custom-call(f32[4,128,256]{2,1,0:T(8,128)} %get-tuple-element.395, f32[4,128,256]{2,1,0:T(8,128)} %get-tuple-element.396, f32[1,3000]{1,0:T(1,128)} %get-tuple-element.397, f32[1,1]{1,0:T(1,128)} %get-tuple-element.398, ...), custom_call_target="tpu_custom_call" | custom-call | tf_op jit(solution)/shard_map/hand_over/pallas_call | solution.py:878
Async XLA Ops:
  0.6 43.5 %copy-start.26 = (f32[3000]{0:T(1024)S(1)}, f32[3000]{0:T(1024)}, u32[]{:S(2)}) copy-start(f32[3000]{0:T(1024)} %param.27) | copy-start | bytes 36004
  0.6 43.5 %copy-start.15 = (bf16[4,128,256]{2,1,0:T(8,128)(2,1)S(1)}, bf16[4,128,256]{2,1,0:T(8,128)(2,1)}, u32[]{:S(2)}) copy-start(bf16[4,128,256]{2,1,0:T(8,128)(2,1)} %refs_4_.1) | copy-start | bytes 786436
  0.7 43.4 %copy-start.13 = (bf16[4,128,256]{2,1,0:T(8,128)(2,1)S(1)}, bf16[4,128,256]{2,1,0:T(8,128)(2,1)}, u32[]{:S(2)}) copy-start(bf16[4,128,256]{2,1,0:T(8,128)(2,1)} %refs_3_.1) | copy-start | bytes 786436
  0.7 43.4 %copy-start.9 = (bf16[4,128,256]{2,1,0:T(8,128)(2,1)S(1)}, bf16[4,128,256]{2,1,0:T(8,128)(2,1)}, u32[]{:S(2)}) copy-start(bf16[4,128,256]{2,1,0:T(8,128)(2,1)} %refs_2_.1) | copy-start | bytes 786436
  0.7 43.4 %copy-start = (f32[4,128,256]{2,1,0:T(8,128)S(1)}, f32[4,128,256]{2,1,0:T(8,128)}, u32[]{:S(2)}) copy-start(f32[4,128,256]{2,1,0:T(8,128)} %refs_0_.1) | copy-start | bytes 1572868

commit v7 on v5

--- a/solution.py
+++ b/solution.py
@@ -253,10 +253,9 @@
     n_east, n_x, n_z = sizes
     n_north = n_x * n_z
     fields, well_refs, refs = refs[:6], refs[6:14], refs[14:]
-    out_new, out_adjoint, out_slope, out_cost, out_misfit, out_crowded = refs[:6]
+    head_new, adjoint, out_slope, out_cost, out_misfit, out_crowded = refs[:6]
     hx, tx, ke, kn, kv, st, fe, fn, fu, inv, src, lw, d0, d1, s1, pt = refs[6:22]
-    head_new, adjoint, parts = refs[22:25]
-    staged, (nbs, efs, ebs, cfs, cbs), refs = refs[25:29], refs[29:34], refs[34:]
+    parts, staged, (nbs, efs, ebs, cfs, cbs), refs = refs[22], refs[23:27], refs[27:32], refs[32:]
     (s_nf, s_nb, s_ef, s_eb, s_cf, s_cb), refs = refs[:6], refs[6:]
     well_rows, wells, boxes, refs = refs[:8], refs[8], refs[9:13], refs[13:]
     load_sem, send_sem, recv_sem, sum_send, sum_recv = refs
@@ -350,17 +349,22 @@
             r0 = (rows - 8) * side
             h = hx[own + z, pl.ds(8 + r0, 8), inside_cols]
             t = tx[own + z, pl.ds(8 + r0, 8), inside_cols]
-            if side == 0:
-                both = jnp.where(wide_sub >= HALO - 2, roll(t, HALO - 2, 0), h)
-            else:
-                both = jnp.where(wide_sub < 2, roll(t, 2, 0), h)
-            s_nf[side, z] = both
             edge = [
                 ref[own + z, pl.ds((rows - 16) * side, 16), :].astype(F32)[8 * side:8 * side + 8]
                 for ref in staged
             ]
-            s_nb[side, z, pl.ds(0, 16)] = jnp.concatenate(edge[:2], axis=0).astype(BF16)
-            s_nb[side, z, pl.ds(16, 16)] = jnp.concatenate(edge[2:], axis=0).astype(BF16)
+            if side == 0:
+                both = jnp.where(wide_sub == 5, roll(edge[1], 1, 0), h)
+                both = jnp.where(wide_sub >= 6, roll(t, 6, 0), both)
+                first = jnp.where(wide_sub < 4, edge[0], roll(edge[1], 4, 0))
+                second = jnp.where(wide_sub < 4, edge[2], roll(edge[3], 4, 0))
+            else:
+                both = jnp.where(wide_sub == 2, roll(edge[1], 7, 0), h)
+                both = jnp.where(wide_sub < 2, roll(t, 2, 0), both)
+                first = jnp.where(wide_sub < 4, roll(edge[0], 4, 0), edge[1])
+                second = jnp.where(wide_sub < 4, roll(edge[2], 4, 0), edge[3])
+            s_nf[side, z] = both
+            s_nb[side, z] = jnp.concatenate([first, second], axis=0).astype(BF16)
         return carry
 
     lax.fori_loop(0, depth, pack, 0)
@@ -373,12 +377,13 @@
             for z in range(depth):
                 both = s_nf[r, z, :, pl.ds(c0, LANES)]
                 kept = jnp.where(group == z, roll(both, HALO * z - (LANES - HALO) * c, 1), kept)
+                pieces = s_nb[r, z, :, pl.ds(c0, LANES)].astype(F32)
                 for half in (0, 1):
-                    two = s_nb[r, z, pl.ds(16 * half, 16), pl.ds(c0, LANES)].astype(F32)
-                    for k in (0, 1):
-                        slot = (2 * half + k) * depth + z
-                        moved = roll(two[8 * k:8 * k + 8], HALO * slot - (LANES - HALO) * c, 1)
-                        mixed = jnp.where(group == slot, moved, mixed)
+                    slot = half * depth + z
+                    moved = roll(
+                        pieces[8 * half:8 * half + 8], HALO * slot - (LANES - HALO) * c, 1
+                    )
+                    mixed = jnp.where(group == slot, moved, mixed)
             s_cf[2 * r + c] = kept
             s_cb[2 * r + c] = jnp.concatenate([mixed, mixed], axis=0).astype(BF16)
 
@@ -509,39 +514,140 @@
 
         lax.fori_loop(0, depth, fill, 0)
 
+    def put_rows(side, zz, at_rows, at_cols, both, first, second):
+        row = iota(both.shape, 0)
+        if side == 0:
+            tx[zz, at_rows, at_cols] = roll(both, 2, 0)
+            ke[zz, at_rows, at_cols] = first
+            kn[zz, at_rows, at_cols] = jnp.where(row == 4, roll(both, 7, 0), roll(first, 4, 0))
+            kv[zz, at_rows, at_cols] = second
+            st[zz, at_rows, at_cols] = roll(second, 4, 0)
+        else:
+            tx[zz, at_rows, at_cols] = roll(both, 6, 0)
+            ke[zz, at_rows, at_cols] = roll(first, 4, 0)
+            kn[zz, at_rows, at_cols] = jnp.where(row == 3, roll(both, 1, 0), first)
+            kv[zz, at_rows, at_cols] = roll(second, 4, 0)
+            st[zz, at_rows, at_cols] = second
+
     def fill_north(who, base):
         def fill(z, carry):
-            zz = base + z
             for side, at_rows in enumerate(edge_rows):
-                tx[zz, at_rows, inside_cols] = roll(
-                    hx[zz, at_rows, inside_cols], 2 if side == 0 else 6, 0
+                pieces = nbs[who, side, z].astype(F32)
+                both = hx[base + z, at_rows, inside_cols]
+                put_rows(side, base + z, at_rows, inside_cols, both, pieces[:8], pieces[8:])
+            return carry
+
+        lax.fori_loop(0, depth, fill, 0)
+
+    def fill_corners(who, base):
+        for side, at_rows in enumerate(edge_rows):
+            right, left = cfs[who, 2 * side], cfs[who, 2 * side + 1]
+            rights = cbs[who, 2 * side].astype(F32)[:8]
+            lefts = cbs[who, 2 * side + 1].astype(F32)[:8]
+
+            def taken(a, b, slot):
+                return jnp.where(
+                    low_half, roll(a, -HALO * slot, 1), roll(b, LANES - HALO - HALO * slot, 1)
                 )
-                for half, pair in ((0, (ke, kn)), (1, (kv, st))):
-                    both = nbs[who, side, z, pl.ds(16 * half, 16)].astype(F32)
-                    pair[0][zz, at_rows, inside_cols] = both[:8]
-                    pair[1][zz, at_rows, inside_cols] = both[8:]
+
+            for z in range(depth):
+                both = taken(right, left, z)
+                hx[base + z, at_rows, extra] = both
+                put_rows(
+                    side, base + z, at_rows, extra, both,
+                    taken(rights, lefts, z), taken(rights, lefts, depth + z),
+                )
+
+    wide = (8, ext_cols)
+    sub = iota(wide, 0)
+    col = iota(wide, 1)
+    closed_col = ((col == cols - 1) & (me_e == n_east - 1)) | ((col == ext_cols - 1) & (me_e == 0))
+    open_east = jnp.where(closed_col, 0.0, 2.0)
+    open_low = jnp.where((sub == 7) & (me_n == 0), 0.0, 2.0)
+    open_high = jnp.where((sub == 7) & (me_n == n_north - 1), 0.0, 2.0)
+
+    def east(v):
+        return roll(v, ext_cols - 1, 1)
+
+    def west(v):
+        return roll(v, 1, 1)
+
+    def north(now, after):
+        return jnp.where(sub < 7, roll(now, 7, 0), roll(after, 7, 0))
+
+    def south(now, prior):
+        return jnp.where(sub > 0, roll(now, 1, 0), roll(prior, 1, 0))
+
+    fu[0] = jnp.zeros((ext_rows, ext_cols), F32)
+    fu[layers] = jnp.zeros((ext_rows, ext_cols), F32)
+
+    def row_chunks(begin, end, unit, body, carry):
+        if end - begin == unit:
+            for j in range(begin, end):
+                carry = body(j, carry)
             return carry
 
-        lax.fori_loop(0, depth, fill, 0)
-
-    def fill_corners(who, base):
-        for r, at_rows in enumerate(edge_rows):
-            right, left = cfs[who, 2 * r], cfs[who, 2 * r + 1]
-            rights = cbs[who, 2 * r].astype(F32)[:8]
-            lefts = cbs[who, 2 * r + 1].astype(F32)[:8]
-            for z in range(depth):
-                both = jnp.where(
-                    low_half, roll(right, -HALO * z, 1), roll(left, LANES - HALO - HALO * z, 1)
-                )
-                hx[base + z, at_rows, extra] = both
-                tx[base + z, at_rows, extra] = roll(both, 2 if r == 0 else 6, 0)
-                for a, dst in enumerate((ke, kn, kv, st)):
-                    slot = a * depth + z
-                    dst[base + z, at_rows, extra] = jnp.where(
-                        low_half,
-                        roll(rights, -HALO * slot, 1),
-                        roll(lefts, LANES - HALO - HALO * slot, 1),
-                    )
+        def several(k, carry):
+            for i in range(unit):
+                carry = body(begin + k * unit + i, carry)
+            return carry
+
+        return lax.fori_loop(0, (end - begin) // unit, several, carry)
+
+    def at(j):
+        return pl.ds(8 * j if isinstance(j, int) else pl.multiple_of(8 * j, 8), 8)
+
+    def next_of(j):
+        return min(j + 1, chunks_of_rows - 1) if isinstance(j, int) else jnp.minimum(j + 1, chunks_of_rows - 1)
+
+    def layer_of(k):
+        return jnp.where(me_l == 0, k, layers - 1 - k)
+
+    def start(k, carry, with_wells):
+        z = layer_of(k)
+        up = layer_of(jnp.minimum(k + 1, layers - 1))
+        down = layer_of(jnp.maximum(k - 1, 0))
+        open_up = jnp.where(k < layers - 1, 2.0, 0.0)
+
+        def chunk(j, carry):
+            fn_prior, gn_prior, k_n, h = carry
+            k_e, k_u, k_u2 = ke[z, at(j)], kv[z, at(j)], kv[up, at(j)]
+            k_e2 = east(k_e)
+            k_after, h_after = kn[z, at(next_of(j))], hx[z, at(next_of(j))]
+            k_n2 = north(k_n, k_after)
+            f_e = open_east * k_e * k_e2 * reciprocal(k_e + k_e2)
+            if isinstance(j, int):
+                opened = open_low if j == 0 else open_high if j == chunks_of_rows - 2 else 2.0
+            else:
+                edge = ((j == 0) & (me_n == 0)) | ((j == chunks_of_rows - 2) & (me_n == n_north - 1))
+                opened = jnp.where((sub == 7) & edge, 0.0, 2.0)
+            f_n = opened * k_n * k_n2 * reciprocal(k_n + k_n2)
+            f_u = open_up * k_u * k_u2 * reciprocal(k_u + k_u2)
+            f_d = fu[z + me_l, at(j)]
+            fe[z, at(j)] = f_e
+            fn[z, at(j)] = f_n
+            fu[z + 1 - me_l, at(j)] = f_u
+            diagonal = st[z, at(j)] + f_e + west(f_e) + f_n + south(f_n, fn_prior) + f_u + f_d
+            inverse = reciprocal(diagonal)
+            inv[z, at(j)] = inverse
+            g_e = f_e * (east(h) - h)
+            g_n = f_n * (north(h, h_after) - h)
+            g_u = f_u * (hx[up, at(j)] - h)
+            g_d = f_d * (h - hx[down, at(j)])
+            residual = (g_e - west(g_e)) + (g_n - south(g_n, gn_prior)) + (g_u - g_d)
+            if with_wells:
+                residual = residual - src[z, at(j)]
+            d0[z, at(j)] = inverse * residual
+            return f_n, g_n, k_after, h_after
+
+        none = jnp.zeros(wide, F32)
+        row_chunks(0, chunks_of_rows, START_UNIT, chunk, (none, none, kn[z, at(0)], hx[z, at(0)]))
+        return carry
+
+    def pump(k, carry):
+        z = layer_of(k)
+        d0[z] = d0[z] - inv[z] * src[z]
+        return carry
 
     fill_inner(own)
     for copy in easts:
@@ -560,6 +666,7 @@
     forwards.append(send(cbs.at[0], cbs.at[1], partner))
     fill_north(0, own)
     fill_corners(0, own)
+    lax.fori_loop(0, depth - 1, functools.partial(start, with_wells=False), 0)
     for copy in blocks:
         copy.wait_recv()
     fill_inner(other)
@@ -595,86 +702,8 @@
         src[z] = field[:ext_rows]
         lw[z] = field[ext_rows:]
 
-    wide = (8, ext_cols)
-    sub = iota(wide, 0)
-    col = iota(wide, 1)
-    closed_col = ((col == cols - 1) & (me_e == n_east - 1)) | ((col == ext_cols - 1) & (me_e == 0))
-    open_east = jnp.where(closed_col, 0.0, 2.0)
-    open_low = jnp.where((sub == 7) & (me_n == 0), 0.0, 2.0)
-    open_high = jnp.where((sub == 7) & (me_n == n_north - 1), 0.0, 2.0)
-
-    def east(v):
-        return roll(v, ext_cols - 1, 1)
-
-    def west(v):
-        return roll(v, 1, 1)
-
-    def north(now, after):
-        return jnp.where(sub < 7, roll(now, 7, 0), roll(after, 7, 0))
-
-    def south(now, prior):
-        return jnp.where(sub > 0, roll(now, 1, 0), roll(prior, 1, 0))
-
-    fu[0] = jnp.zeros((ext_rows, ext_cols), F32)
-
-    def row_chunks(begin, end, unit, body, carry):
-        if end - begin == unit:
-            for j in range(begin, end):
-                carry = body(j, carry)
-            return carry
-
-        def several(k, carry):
-            for i in range(unit):
-                carry = body(begin + k * unit + i, carry)
-            return carry
-
-        return lax.fori_loop(0, (end - begin) // unit, several, carry)
-
-    def at(j):
-        return pl.ds(8 * j if isinstance(j, int) else pl.multiple_of(8 * j, 8), 8)
-
-    def next_of(j):
-        return min(j + 1, chunks_of_rows - 1) if isinstance(j, int) else jnp.minimum(j + 1, chunks_of_rows - 1)
-
-    def start(z, carry):
-        up = jnp.minimum(z + 1, layers - 1)
-        down = jnp.maximum(z - 1, 0)
-        open_up = jnp.where(z < layers - 1, 2.0, 0.0)
-
-        def chunk(j, carry):
-            fn_prior, gn_prior, k_n, h = carry
-            k_e, k_u, k_u2 = ke[z, at(j)], kv[z, at(j)], kv[up, at(j)]
-            k_e2 = east(k_e)
-            k_after, h_after = kn[z, at(next_of(j))], hx[z, at(next_of(j))]
-            k_n2 = north(k_n, k_after)
-            f_e = open_east * k_e * k_e2 * reciprocal(k_e + k_e2)
-            if isinstance(j, int):
-                opened = open_low if j == 0 else open_high if j == chunks_of_rows - 2 else 2.0
-            else:
-                edge = ((j == 0) & (me_n == 0)) | ((j == chunks_of_rows - 2) & (me_n == n_north - 1))
-                opened = jnp.where((sub == 7) & edge, 0.0, 2.0)
-            f_n = opened * k_n * k_n2 * reciprocal(k_n + k_n2)
-            f_u = open_up * k_u * k_u2 * reciprocal(k_u + k_u2)
-            f_d = fu[z, at(j)]
-            fe[z, at(j)] = f_e
-            fn[z, at(j)] = f_n
-            fu[z + 1, at(j)] = f_u
-            diagonal = st[z, at(j)] + f_e + west(f_e) + f_n + south(f_n, fn_prior) + f_u + f_d
-            inverse = reciprocal(diagonal)
-            inv[z, at(j)] = inverse
-            g_e = f_e * (east(h) - h)
-            g_n = f_n * (north(h, h_after) - h)
-            g_u = f_u * (hx[up, at(j)] - h)
-            g_d = f_d * (h - hx[down, at(j)])
-            residual = (g_e - west(g_e)) + (g_n - south(g_n, gn_prior)) + (g_u - g_d)
-            d0[z, at(j)] = inverse * (residual - src[z, at(j)])
-            return f_n, g_n, k_after, h_after
-
-        none = jnp.zeros(wide, F32)
-        row_chunks(0, chunks_of_rows, START_UNIT, chunk, (none, none, kn[z, at(0)], hx[z, at(0)]))
-        return carry
-
-    lax.fori_loop(0, layers, start, 0)
+    lax.fori_loop(0, depth - 1, pump, 0)
+    lax.fori_loop(depth - 1, layers, functools.partial(start, with_wells=True), 0)
 
     def sweep(field, margin, finish, chunk_from, chunk_to):
         def layer(i, carry):
@@ -734,8 +763,6 @@
         st[0, at(0), inside_cols] = st[0, at(0), inside_cols] + departure * departure
 
     sweep(d1, 0, end_adjoint, 1, chunks_of_rows - 1)
-
-    writes = [load(head_new, out_new), load(adjoint, out_adjoint)]
 
     squared = st[0, at(0), inside_cols]
     squared = jnp.sum(squared, axis=0, keepdims=True)
@@ -804,8 +831,6 @@
     out_cost[...] = sums[0:1]
     out_misfit[...] = sums[1:2]
     out_crowded[...] = sums[2:3]
-    for copy in writes:
-        copy.wait()
 
 
 def run_kernel(sizes, fields, wells):
@@ -814,33 +839,34 @@
     n_wells = wells[0].shape[1]
     groups = -(-n_wells // LANES)
     n_east, n_x, n_z = sizes
-    block = jax.ShapeDtypeStruct((depth, rows, cols), F32)
-    one = jax.ShapeDtypeStruct((1, 1), F32)
+    block = pltpu.VMEM((depth, rows, cols), F32)
+    one = pltpu.VMEM((1, 1), F32)
     ext = pltpu.VMEM((layers, ext_rows, ext_cols), F32)
     operands = (*fields, *wells)
     copies = 4 + 4 + 8 + 6 + 7
     peers = 1 + n_z + n_east + n_x - 3
     return pl.pallas_call(
         functools.partial(kernel, sizes),
-        out_shape=[block, block, jax.ShapeDtypeStruct((1, n_wells), F32), one, one, one],
+        out_shape=[
+            block, block, pltpu.VMEM((1, n_wells), F32), one, one,
+            jax.ShapeDtypeStruct((1, 1), F32),
+        ],
         in_specs=[pl.BlockSpec(memory_space=pltpu.HBM)] * len(operands),
-        out_specs=[pl.BlockSpec(memory_space=pltpu.HBM)] * 2
-        + [pl.BlockSpec(memory_space=pltpu.VMEM)] * 4,
+        out_specs=[pl.BlockSpec(memory_space=pltpu.VMEM)] * 6,
         scratch_shapes=[ext] * 8
         + [pltpu.VMEM((layers + 1, ext_rows, ext_cols), F32)]
         + [ext] * 6
         + [pltpu.VMEM((SLOTS, groups * LANES), BF16)]
-        + [pltpu.VMEM((depth, rows, cols), F32)] * 2
         + [pltpu.VMEM((groups + 8, LANES), F32)]
         + [pltpu.VMEM((layers, rows, cols), BF16)] * 4
         + [
-            pltpu.VMEM((2, 2, depth, 32, cols), BF16),
+            pltpu.VMEM((2, 2, depth, 16, cols), BF16),
             pltpu.VMEM((2, 2, depth, 8, LANES), F32),
             pltpu.VMEM((2, 2, depth, 32, LANES), BF16),
             pltpu.VMEM((2, 4, 8, LANES), F32),
             pltpu.VMEM((2, 4, 16, LANES), BF16),
             pltpu.VMEM((2, depth, 8, cols), F32),
-            pltpu.VMEM((2, depth, 32, cols), BF16),
+            pltpu.VMEM((2, depth, 16, cols), BF16),
             pltpu.VMEM((2, depth, 8, LANES), F32),
             pltpu.VMEM((2, depth, 32, LANES), BF16),
             pltpu.VMEM((4, 8, LANES), F32),
@@ -849,7 +875,7 @@
         + [pltpu.VMEM(w.shape, w.dtype) for w in wells]
         + [pltpu.VMEM((8, groups * LANES), F32)]
         + [pltpu.VMEM((n, groups + 8, LANES), F32) for n in (2, n_z, n_east, n_x)]
-        + [pltpu.SemaphoreType.DMA((16,))]
+        + [pltpu.SemaphoreType.DMA((14,))]
         + [pltpu.SemaphoreType.DMA((copies,))] * 2
         + [pltpu.SemaphoreType.DMA((peers,))] * 2,
         compiler_params=pltpu.CompilerParams(
@@ -874,7 +900,7 @@
     return pl.pallas_call(
         hand_over,
         out_shape=[jax.ShapeDtypeStruct(v.shape, v.dtype) for v in values],
-        in_specs=[pl.BlockSpec(memory_space=pltpu.HBM)] * len(values),
+        in_specs=[pl.BlockSpec(memory_space=pltpu.VMEM)] * len(values),
         out_specs=[pl.BlockSpec(memory_space=pltpu.HBM)] * len(values),
         scratch_shapes=[pltpu.SemaphoreType.DMA((len(values),))],
         compiler_params=pltpu.CompilerParams(vmem_limit_bytes=60 * 1024 * 1024),
@@ -891,7 +917,7 @@
     e, n, top, bottom, tariff, rates, ground, prices = arguments[6:]
     wells = [w.reshape(1, -1) for w in (e, n, top, bottom, rates, tariff, ground, prices)]
     new, adjoint, slope, cost, misfit, crowded = run_kernel(sizes, fields, wells)
-    found = (new, adjoint, slope, cost, misfit)
+    found = tuple(run_hand_over((new, adjoint, slope, cost, misfit)))
 
     def again(state):
         blocks = [in_order(x) for x in fields]
@@ -900,7 +926,7 @@
         return jnp.zeros((), F32), (in_order(first), in_order(second), *others)
 
     _, found = lax.while_loop(lambda state: state[0] > 0, again, (crowded.reshape(()), found))
-    new, adjoint, slope, cost, misfit = run_hand_over(found)
+    new, adjoint, slope, cost, misfit = found
     return new, adjoint, slope.reshape(-1), cost.reshape(()), misfit.reshape(())
 
 

time: 79.8 us -> 50.1 us (0.63)
  Pallas kernels: 78 us -> 46 us
  local copies, waits for them, and re-layouts: 0.03 us -> 2.25 us
    pallas_call x1, Pallas kernels: 34.6 us -> 3.45 us  [run_hand_over(): pl.pallas_call(hand_over, out_shape=[jax.ShapeDtypeStruct(v.shape, v.dtyp...]
    unnamed x10 -> x16, local copies, waits for them, and re-layouts: 0.03 us -> 2.25 us
    pallas_call x1, Pallas kernels: 43.4 us -> 42.5 us  [run_kernel(): pl.pallas_call(functools.partial(kernel, sizes), out_shape=[block, block,...]
where the time goes in v7:
time: 50.1 us; the launch traced here: 49.9 us
  Pallas kernels  46 us (92%)
  local copies, waits for them, and re-layouts  2.25 us (4%)
  between operations  0.9 us (2%)
  loops' own time  0.8 us (2%)
    pallas_call x1, Pallas kernels, run_kernel(): pl.pallas_call(functools.partial(kernel, sizes), out_shape=[block, block,...  42.5 us
    pallas_call x1, Pallas kernels, run_hand_over(): pl.pallas_call(hand_over, out_shape=[jax.ShapeDtypeStruct(v.shape, v.dtyp...  3.45 us
    unnamed x16, local copies, waits for them, and re-layouts  2.25 us

profile of v7, /device:TPU:0, one launch (start us, length us, event | category | flops | bytes accessed | tf_op | source)
XLA Modules:
  0.0 49.9 jit_solution(6795189221783971776)
XLA Ops:
  0.6 0.0 copy-start.29
  0.6 0.0 copy-start.18
  0.7 0.0 copy-start.16
  0.7 0.0 copy-start.12
  0.7 0.0 copy-start.3
  0.7 42.5 %whole_step.1 = (f32[4,128,256]{2,1,0:T(8,128)S(1)}, f32[4,128,256]{2,1,0:T(8,128)S(1)}, f32[1,3000]{1,0:T(1,128)S(1)}, f32[1,1]{1,0:T(1,128)}, f32[1,1]{1,0:T(1,128)}, /*index=5*/f32[1,1]{1,0:T(1,128)}) custom-call(f32[4,128,256]{2,1,0:T(8,128)} %refs_0_.1, f32[4,128,256]{2,1,0:T(8,128)} %refs_1_.1, bf16[4,128,256]{2,1,0:T(8,128)(2,1)} %refs_2_.1, ...), custom_call_target="tpu_custom_call" | custom-call | tf_op jit(solution)/shard_map/whole_step/pallas_call | solution.py:848
  43.2 0.0 copy-start
  43.2 0.8 %copy-done = f32[4,128,256]{2,1,0:T(8,128)} copy-done((f32[4,128,256]{2,1,0:T(8,128)}, f32[4,128,256]{2,1,0:T(8,128)S(1)}, u32[]{:S(2)}) %copy-start) | copy-done | bytes 524312
  44.0 0.0 copy-start.1
  44.0 0.8 %copy-done.1 = f32[4,128,256]{2,1,0:T(8,128)} copy-done((f32[4,128,256]{2,1,0:T(8,128)}, f32[4,128,256]{2,1,0:T(8,128)S(1)}, u32[]{:S(2)}) %copy-start.1) | copy-done | bytes 524312
  44.8 0.0 copy-start.2
  44.8 0.6 %copy-done.2 = f32[1,3000]{1,0:T(1,128)} copy-done((f32[1,3000]{1,0:T(1,128)}, f32[1,3000]{1,0:T(1,128)S(1)}, u32[]{:S(2)}) %copy-start.2) | copy-done | bytes 12024
  45.4 3.4 %hand_over.1 = (f32[4,128,256]{2,1,0:T(8,128)}, f32[4,128,256]{2,1,0:T(8,128)}, f32[1,3000]{1,0:T(1,128)}, f32[1,1]{1,0:T(1,128)}, f32[1,1]{1,0:T(1,128)}) custom-call(f32[4,128,256]{2,1,0:T(8,128)} %copy-done, f32[4,128,256]{2,1,0:T(8,128)} %copy-done.1, f32[1,3000]{1,0:T(1,128)} %copy-done.2, f32[1,1]{1,0:T(1,128)} %get-tuple-element.120.refs_3_, ...), custom_call_target="tpu_custom_call" | custom-call | tf_op jit(solution)/shard_map/hand_over/pallas_call | solution.py:900
  48.9 0.0 copy-done.29
  48.9 0.0 copy-done.18
  48.9 0.0 copy-done.16
  48.9 0.0 copy-done.12
  48.9 0.0 copy-done.3
  48.9 0.8 %while.17 = (f32[]{:T(128)}, f32[4,128,256]{2,1,0:T(8,128)}, f32[4,128,256]{2,1,0:T(8,128)}, f32[1,3000]{1,0:T(1,128)}, f32[1,1]{1,0:T(1,128)}, /*index=5*/f32[1...) while((f32[]{:T(128)}, f32[4,128,256]{2,1,0:T(8,128)}, ...), condition=%region_13.14_spmd, body=%region_0.13_spmd | while | flops 59988996 | bytes 132797736 | solution.py:928
Async XLA Ops:
  0.6 48.3 %copy-start.29 = (f32[3000]{0:T(1024)S(1)}, f32[3000]{0:T(1024)}, u32[]{:S(2)}) copy-start(f32[3000]{0:T(1024)} %param.27) | copy-start | bytes 36004
  0.6 48.3 %copy-start.18 = (bf16[4,128,256]{2,1,0:T(8,128)(2,1)S(1)}, bf16[4,128,256]{2,1,0:T(8,128)(2,1)}, u32[]{:S(2)}) copy-start(bf16[4,128,256]{2,1,0:T(8,128)(2,1)} %refs_4_.1) | copy-start | bytes 786436
  0.7 48.3 %copy-start.16 = (bf16[4,128,256]{2,1,0:T(8,128)(2,1)S(1)}, bf16[4,128,256]{2,1,0:T(8,128)(2,1)}, u32[]{:S(2)}) copy-start(bf16[4,128,256]{2,1,0:T(8,128)(2,1)} %refs_3_.1) | copy-start | bytes 786436
  0.7 48.3 %copy-start.12 = (bf16[4,128,256]{2,1,0:T(8,128)(2,1)S(1)}, bf16[4,128,256]{2,1,0:T(8,128)(2,1)}, u32[]{:S(2)}) copy-start(bf16[4,128,256]{2,1,0:T(8,128)(2,1)} %refs_2_.1) | copy-start | bytes 786436
  0.7 48.3 %copy-start.3 = (f32[4,128,256]{2,1,0:T(8,128)S(1)}, f32[4,128,256]{2,1,0:T(8,128)}, u32[]{:S(2)}) copy-start(f32[4,128,256]{2,1,0:T(8,128)} %refs_0_.1) | copy-start | bytes 1572868
  43.2 0.8 %copy-start = (f32[4,128,256]{2,1,0:T(8,128)}, f32[4,128,256]{2,1,0:T(8,128)S(1)}, u32[]{:S(2)}) copy-start(f32[4,128,256]{2,1,0:T(8,128)S(1)} %get-tuple-element.117.refs_0_) | copy-start | bytes 1572868
  44.0 0.8 %copy-start.1 = (f32[4,128,256]{2,1,0:T(8,128)}, f32[4,128,256]{2,1,0:T(8,128)S(1)}, u32[]{:S(2)}) copy-start(f32[4,128,256]{2,1,0:T(8,128)S(1)} %get-tuple-element.118.refs_1_) | copy-start | bytes 1572868
  44.8 0.6 %copy-start.2 = (f32[1,3000]{1,0:T(1,128)}, f32[1,3000]{1,0:T(1,128)S(1)}, u32[]{:S(2)}) copy-start(f32[1,3000]{1,0:T(1,128)S(1)} %get-tuple-element.119.refs_2_) | copy-start | bytes 36004

commit v8 on v7

--- a/solution.py
+++ b/solution.py
@@ -20,7 +20,8 @@
 REACH = 5
 LANES = 128
 SLOTS = 128
-START_UNIT, SWEEP_UNIT, LAST_UNIT = 9, 18, 16
+START_UNIT = 9
+SWEEP_LAYERS = 4
 
 
 def steps_of():
@@ -706,31 +707,40 @@
     lax.fori_loop(depth - 1, layers, functools.partial(start, with_wells=True), 0)
 
     def sweep(field, margin, finish, chunk_from, chunk_to):
-        def layer(i, carry):
-            z = (depth - margin) * me_l + i
-            up = jnp.minimum(z + 1, layers - 1)
-            down = jnp.maximum(z - 1, 0)
-
-            def chunk(j, carry):
-                b_prior, d = carry
-                d_after = field[z, at(next_of(j))]
-                f_e, f_n = fe[z, at(j)], fn[z, at(j)]
-                b = f_n * d
-                moved = f_e * east(d) + west(f_e * d)
-                moved = moved + f_n * north(d, d_after) + south(b, b_prior)
-                moved = moved + fu[z + 1, at(j)] * field[up, at(j)] + fu[z, at(j)] * field[down, at(j)]
-                finish(i, z, j, d, inv[z, at(j)] * moved)
-                return b, d_after
-
+        first = (depth - margin) * me_l
+
+        def together(i, count):
+            zs = [first + i + k for k in range(count)]
+            below = jnp.maximum(zs[0] - 1, 0)
+            above = jnp.minimum(zs[-1] + 1, layers - 1)
             if chunk_from == 0:
-                b_prior = jnp.zeros(wide, F32)
+                priors = [jnp.zeros(wide, F32)] * count
             else:
-                b_prior = fn[z, at(chunk_from - 1)] * field[z, at(chunk_from - 1)]
-            unit = SWEEP_UNIT if chunk_from == 0 else LAST_UNIT
-            row_chunks(chunk_from, chunk_to, unit, chunk, (b_prior, field[z, at(chunk_from)]))
+                before = at(chunk_from - 1)
+                priors = [fn[z, before] * field[z, before] for z in zs]
+            now = [field[z, at(chunk_from)] for z in zs]
+            for j in range(chunk_from, chunk_to):
+                after = [field[z, at(min(j + 1, chunks_of_rows - 1))] for z in zs]
+                stack = [field[below, at(j)]] + now + [field[above, at(j)]]
+                for k, z in enumerate(zs):
+                    d = now[k]
+                    f_e, f_n = fe[z, at(j)], fn[z, at(j)]
+                    b = f_n * d
+                    moved = f_e * east(d) + west(f_e * d)
+                    moved = moved + f_n * north(d, after[k]) + south(b, priors[k])
+                    moved = moved + fu[z + 1, at(j)] * stack[k + 2] + fu[z, at(j)] * stack[k]
+                    finish(i + k, z, j, d, inv[z, at(j)] * moved)
+                    priors[k] = b
+                now = after
+
+        def some(i, carry):
+            together(SWEEP_LAYERS * i, SWEEP_LAYERS)
             return carry
 
-        lax.fori_loop(0, depth + margin, layer, 0)
+        total = depth + margin
+        lax.fori_loop(0, total // SWEEP_LAYERS, some, 0)
+        if total % SWEEP_LAYERS:
+            together(total - total % SWEEP_LAYERS, total % SWEEP_LAYERS)
 
     (a1, b1), (a2, b2) = steps_of()
 
@@ -903,7 +913,7 @@
         in_specs=[pl.BlockSpec(memory_space=pltpu.VMEM)] * len(values),
         out_specs=[pl.BlockSpec(memory_space=pltpu.HBM)] * len(values),
         scratch_shapes=[pltpu.SemaphoreType.DMA((len(values),))],
-        compiler_params=pltpu.CompilerParams(vmem_limit_bytes=60 * 1024 * 1024),
+        compiler_params=pltpu.CompilerParams(vmem_limit_bytes=8 * 1024 * 1024),
         name="hand_over",
     )(*values)
 

time: 50.1 us -> 45.2 us (0.902)
  Pallas kernels: 46 us -> 43.4 us
  local copies, waits for them, and re-layouts: 2.25 us -> 0.03 us
    unnamed x16 -> x10, local copies, waits for them, and re-layouts: 2.25 us -> 0.03 us
    pallas_call x1, Pallas kernels: 42.5 us -> 41.1 us  [run_kernel(): pl.pallas_call(functools.partial(kernel, sizes), out_shape=[block, block,...]
    pallas_call x1, Pallas kernels: 3.45 us -> 2.33 us  [run_hand_over(): pl.pallas_call(hand_over, out_shape=[jax.ShapeDtypeStruct(v.shape, v.dtyp...]
where the time goes in v8:
time: 45.2 us; the launch traced here: 45.1 us
  Pallas kernels  43.4 us (96%)
  between operations  0.89 us (2%)
  loops' own time  0.73 us (2%)
    pallas_call x1, Pallas kernels, run_kernel(): pl.pallas_call(functools.partial(kernel, sizes), out_shape=[block, block,...  41.1 us
    pallas_call x1, Pallas kernels, run_hand_over(): pl.pallas_call(hand_over, out_shape=[jax.ShapeDtypeStruct(v.shape, v.dtyp...  2.33 us

profile of v8, /device:TPU:0, one launch (start us, length us, event | category | flops | bytes accessed | tf_op | source)
XLA Modules:
  0.0 45.1 jit_solution(16146408121816436331)
XLA Ops:
  0.6 0.0 copy-start.26
  0.6 0.0 copy-start.15
  0.7 0.0 copy-start.13
  0.7 0.0 copy-start.9
  0.7 0.0 copy-start
  0.7 41.1 %whole_step.1 = (f32[4,128,256]{2,1,0:T(8,128)S(1)}, f32[4,128,256]{2,1,0:T(8,128)S(1)}, f32[1,3000]{1,0:T(1,128)S(1)}, f32[1,1]{1,0:T(1,128)}, f32[1,1]{1,0:T(1,128)}, /*index=5*/f32[1,1]{1,0:T(1,128)}) custom-call(f32[4,128,256]{2,1,0:T(8,128)} %refs_0_.1, f32[4,128,256]{2,1,0:T(8,128)} %refs_1_.1, bf16[4,128,256]{2,1,0:T(8,128)(2,1)} %refs_2_.1, ...), custom_call_target="tpu_custom_call" | custom-call | tf_op jit(solution)/shard_map/whole_step/pallas_call | solution.py:858
  41.8 2.3 %hand_over.1 = (f32[4,128,256]{2,1,0:T(8,128)}, f32[4,128,256]{2,1,0:T(8,128)}, f32[1,3000]{1,0:T(1,128)}, f32[1,1]{1,0:T(1,128)}, f32[1,1]{1,0:T(1,128)}) custom-call(f32[4,128,256]{2,1,0:T(8,128)S(1)} %get-tuple-element.117.refs_0_, f32[4,128,256]{2,1,0:T(8,128)S(1)} %get-tuple-element.118.refs_1_, f32[1,3000]{1,0:T(1,128)S(1)} %get-tuple-element.119.refs_2_, ...), custom_call_target="tpu_custom_call" | custom-call | tf_op jit(solution)/shard_map/hand_over/pallas_call | solution.py:910
  44.1 0.0 copy-done.26
  44.2 0.0 copy-done.15
  44.2 0.0 copy-done.13
  44.2 0.0 copy-done.9
  44.2 0.0 copy-done
  44.2 0.7 %while.17 = (f32[]{:T(128)}, f32[4,128,256]{2,1,0:T(8,128)}, f32[4,128,256]{2,1,0:T(8,128)}, f32[1,3000]{1,0:T(1,128)}, f32[1,1]{1,0:T(1,128)}, /*index=5*/f32[1...) while((f32[]{:T(128)}, f32[4,128,256]{2,1,0:T(8,128)}, ...), condition=%region_13.14_spmd, body=%region_0.13_spmd | while | flops 59988996 | bytes 132797736 | solution.py:938
Async XLA Ops:
  0.6 43.5 %copy-start.26 = (f32[3000]{0:T(1024)S(1)}, f32[3000]{0:T(1024)}, u32[]{:S(2)}) copy-start(f32[3000]{0:T(1024)} %param.27) | copy-start | bytes 36004
  0.6 43.5 %copy-start.15 = (bf16[4,128,256]{2,1,0:T(8,128)(2,1)S(1)}, bf16[4,128,256]{2,1,0:T(8,128)(2,1)}, u32[]{:S(2)}) copy-start(bf16[4,128,256]{2,1,0:T(8,128)(2,1)} %refs_4_.1) | copy-start | bytes 786436
  0.7 43.5 %copy-start.13 = (bf16[4,128,256]{2,1,0:T(8,128)(2,1)S(1)}, bf16[4,128,256]{2,1,0:T(8,128)(2,1)}, u32[]{:S(2)}) copy-start(bf16[4,128,256]{2,1,0:T(8,128)(2,1)} %refs_3_.1) | copy-start | bytes 786436
  0.7 43.5 %copy-start.9 = (bf16[4,128,256]{2,1,0:T(8,128)(2,1)S(1)}, bf16[4,128,256]{2,1,0:T(8,128)(2,1)}, u32[]{:S(2)}) copy-start(bf16[4,128,256]{2,1,0:T(8,128)(2,1)} %refs_2_.1) | copy-start | bytes 786436
  0.7 43.5 %copy-start = (f32[4,128,256]{2,1,0:T(8,128)S(1)}, f32[4,128,256]{2,1,0:T(8,128)}, u32[]{:S(2)}) copy-start(f32[4,128,256]{2,1,0:T(8,128)} %refs_0_.1) | copy-start | bytes 1572868

commit v9 on v8

--- a/solution.py
+++ b/solution.py
@@ -20,7 +20,7 @@
 REACH = 5
 LANES = 128
 SLOTS = 128
-START_UNIT = 9
+START_UNIT, START_LAYERS = 9, 1
 SWEEP_LAYERS = 4
 
 
@@ -254,9 +254,9 @@
     n_east, n_x, n_z = sizes
     n_north = n_x * n_z
     fields, well_refs, refs = refs[:6], refs[6:14], refs[14:]
-    head_new, adjoint, out_slope, out_cost, out_misfit, out_crowded = refs[:6]
-    hx, tx, ke, kn, kv, st, fe, fn, fu, inv, src, lw, d0, d1, s1, pt = refs[6:22]
-    parts, staged, (nbs, efs, ebs, cfs, cbs), refs = refs[22], refs[23:27], refs[27:32], refs[32:]
+    head_new, adjoint, out_slope, out_sums, out_crowded = refs[:5]
+    hx, tx, ke, kn, kv, st, fe, fn, fu, inv, src, lw, d0, d1, s1, pt = refs[5:21]
+    parts, staged, (nbs, efs, ebs, cfs, cbs), refs = refs[21], refs[22:26], refs[26:31], refs[31:]
     (s_nf, s_nb, s_ef, s_eb, s_cf, s_cb), refs = refs[:6], refs[6:]
     well_rows, wells, boxes, refs = refs[:8], refs[8], refs[9:13], refs[13:]
     load_sem, send_sem, recv_sem, sum_send, sum_recv = refs
@@ -564,8 +564,6 @@
     col = iota(wide, 1)
     closed_col = ((col == cols - 1) & (me_e == n_east - 1)) | ((col == ext_cols - 1) & (me_e == 0))
     open_east = jnp.where(closed_col, 0.0, 2.0)
-    open_low = jnp.where((sub == 7) & (me_n == 0), 0.0, 2.0)
-    open_high = jnp.where((sub == 7) & (me_n == n_north - 1), 0.0, 2.0)
 
     def east(v):
         return roll(v, ext_cols - 1, 1)
@@ -582,19 +580,6 @@
     fu[0] = jnp.zeros((ext_rows, ext_cols), F32)
     fu[layers] = jnp.zeros((ext_rows, ext_cols), F32)
 
-    def row_chunks(begin, end, unit, body, carry):
-        if end - begin == unit:
-            for j in range(begin, end):
-                carry = body(j, carry)
-            return carry
-
-        def several(k, carry):
-            for i in range(unit):
-                carry = body(begin + k * unit + i, carry)
-            return carry
-
-        return lax.fori_loop(0, (end - begin) // unit, several, carry)
-
     def at(j):
         return pl.ds(8 * j if isinstance(j, int) else pl.multiple_of(8 * j, 8), 8)
 
@@ -604,46 +589,66 @@
     def layer_of(k):
         return jnp.where(me_l == 0, k, layers - 1 - k)
 
-    def start(k, carry, with_wells):
-        z = layer_of(k)
-        up = layer_of(jnp.minimum(k + 1, layers - 1))
-        down = layer_of(jnp.maximum(k - 1, 0))
-        open_up = jnp.where(k < layers - 1, 2.0, 0.0)
+    def start(first, count, with_wells):
+        zs = [layer_of(first + i) for i in range(count)]
+        above = layer_of(jnp.minimum(first + count, layers - 1))
+        below = layer_of(jnp.maximum(first - 1, 0))
+        opens = [jnp.where(first + i < layers - 1, 2.0, 0.0) for i in range(count)]
 
         def chunk(j, carry):
-            fn_prior, gn_prior, k_n, h = carry
-            k_e, k_u, k_u2 = ke[z, at(j)], kv[z, at(j)], kv[up, at(j)]
-            k_e2 = east(k_e)
-            k_after, h_after = kn[z, at(next_of(j))], hx[z, at(next_of(j))]
-            k_n2 = north(k_n, k_after)
-            f_e = open_east * k_e * k_e2 * reciprocal(k_e + k_e2)
-            if isinstance(j, int):
-                opened = open_low if j == 0 else open_high if j == chunks_of_rows - 2 else 2.0
-            else:
-                edge = ((j == 0) & (me_n == 0)) | ((j == chunks_of_rows - 2) & (me_n == n_north - 1))
-                opened = jnp.where((sub == 7) & edge, 0.0, 2.0)
-            f_n = opened * k_n * k_n2 * reciprocal(k_n + k_n2)
-            f_u = open_up * k_u * k_u2 * reciprocal(k_u + k_u2)
-            f_d = fu[z + me_l, at(j)]
-            fe[z, at(j)] = f_e
-            fn[z, at(j)] = f_n
-            fu[z + 1 - me_l, at(j)] = f_u
-            diagonal = st[z, at(j)] + f_e + west(f_e) + f_n + south(f_n, fn_prior) + f_u + f_d
-            inverse = reciprocal(diagonal)
-            inv[z, at(j)] = inverse
-            g_e = f_e * (east(h) - h)
-            g_n = f_n * (north(h, h_after) - h)
-            g_u = f_u * (hx[up, at(j)] - h)
-            g_d = f_d * (h - hx[down, at(j)])
-            residual = (g_e - west(g_e)) + (g_n - south(g_n, gn_prior)) + (g_u - g_d)
-            if with_wells:
-                residual = residual - src[z, at(j)]
-            d0[z, at(j)] = inverse * residual
-            return f_n, g_n, k_after, h_after
-
-        none = jnp.zeros(wide, F32)
-        row_chunks(0, chunks_of_rows, START_UNIT, chunk, (none, none, kn[z, at(0)], hx[z, at(0)]))
-        return carry
+            f_priors, g_priors, k_now, h_now = carry
+            k_ups = [kv[z, at(j)] for z in zs] + [kv[above, at(j)]]
+            heads = h_now + [hx[above, at(j)]]
+            edge = ((j == 0) & (me_n == 0)) | ((j == chunks_of_rows - 2) & (me_n == n_north - 1))
+            opened = jnp.where((sub == 7) & edge, 0.0, 2.0)
+            f_d = fu[zs[0] + me_l, at(j)]
+            g_d = f_d * (h_now[0] - hx[below, at(j)])
+            faces, flows, k_after, h_after = [], [], [], []
+            for i, z in enumerate(zs):
+                k_e, k_n, h = ke[z, at(j)], k_now[i], h_now[i]
+                k_after.append(kn[z, at(next_of(j))])
+                h_after.append(hx[z, at(next_of(j))])
+                k_e2 = east(k_e)
+                k_n2 = north(k_n, k_after[i])
+                f_e = open_east * k_e * k_e2 * reciprocal(k_e + k_e2)
+                f_n = opened * k_n * k_n2 * reciprocal(k_n + k_n2)
+                f_u = opens[i] * k_ups[i] * k_ups[i + 1] * reciprocal(k_ups[i] + k_ups[i + 1])
+                fe[z, at(j)] = f_e
+                fn[z, at(j)] = f_n
+                fu[z + 1 - me_l, at(j)] = f_u
+                diagonal = st[z, at(j)] + f_e + west(f_e) + f_n + south(f_n, f_priors[i]) + f_u + f_d
+                inverse = reciprocal(diagonal)
+                inv[z, at(j)] = inverse
+                g_e = f_e * (east(h) - h)
+                g_n = f_n * (north(h, h_after[i]) - h)
+                g_u = f_u * (heads[i + 1] - h)
+                residual = (g_e - west(g_e)) + (g_n - south(g_n, g_priors[i])) + (g_u - g_d)
+                if with_wells:
+                    residual = residual - src[z, at(j)]
+                d0[z, at(j)] = inverse * residual
+                faces.append(f_n)
+                flows.append(g_n)
+                f_d, g_d = f_u, g_u
+            return faces, flows, k_after, h_after
+
+        def several(i, carry):
+            for m in range(START_UNIT):
+                carry = chunk(i * START_UNIT + m, carry)
+            return carry
+
+        none = [jnp.zeros(wide, F32)] * count
+        carry = (none, none, [kn[z, at(0)] for z in zs], [hx[z, at(0)] for z in zs])
+        lax.fori_loop(0, chunks_of_rows // START_UNIT, several, carry)
+
+    def start_layers(begin, end, with_wells):
+        def some(i, carry):
+            start(begin + START_LAYERS * i, START_LAYERS, with_wells)
+            return carry
+
+        whole = (end - begin) // START_LAYERS
+        lax.fori_loop(0, whole, some, 0)
+        if begin + whole * START_LAYERS < end:
+            start(begin + whole * START_LAYERS, end - begin - whole * START_LAYERS, with_wells)
 
     def pump(k, carry):
         z = layer_of(k)
@@ -667,7 +672,7 @@
     forwards.append(send(cbs.at[0], cbs.at[1], partner))
     fill_north(0, own)
     fill_corners(0, own)
-    lax.fori_loop(0, depth - 1, functools.partial(start, with_wells=False), 0)
+    start_layers(0, depth - 1, False)
     for copy in blocks:
         copy.wait_recv()
     fill_inner(other)
@@ -704,7 +709,7 @@
         lw[z] = field[ext_rows:]
 
     lax.fori_loop(0, depth - 1, pump, 0)
-    lax.fori_loop(depth - 1, layers, functools.partial(start, with_wells=True), 0)
+    start_layers(depth - 1, layers, True)
 
     def sweep(field, margin, finish, chunk_from, chunk_to):
         first = (depth - margin) * me_l
@@ -838,8 +843,7 @@
         width = min(LANES, n_wells - LANES * k)
         out_slope[:, pl.ds(LANES * k, width)] = total[k:k + 1, :width]
     sums = jnp.sum(total[groups:], axis=1, keepdims=True)
-    out_cost[...] = sums[0:1]
-    out_misfit[...] = sums[1:2]
+    out_sums[...] = jnp.broadcast_to(sums, out_sums.shape)
     out_crowded[...] = sums[2:3]
 
 
@@ -850,7 +854,6 @@
     groups = -(-n_wells // LANES)
     n_east, n_x, n_z = sizes
     block = pltpu.VMEM((depth, rows, cols), F32)
-    one = pltpu.VMEM((1, 1), F32)
     ext = pltpu.VMEM((layers, ext_rows, ext_cols), F32)
     operands = (*fields, *wells)
     copies = 4 + 4 + 8 + 6 + 7
@@ -858,11 +861,11 @@
     return pl.pallas_call(
         functools.partial(kernel, sizes),
         out_shape=[
-            block, block, pltpu.VMEM((1, n_wells), F32), one, one,
+            block, block, pltpu.VMEM((1, n_wells), F32), pltpu.VMEM((8, LANES), F32),
             jax.ShapeDtypeStruct((1, 1), F32),
         ],
         in_specs=[pl.BlockSpec(memory_space=pltpu.HBM)] * len(operands),
-        out_specs=[pl.BlockSpec(memory_space=pltpu.VMEM)] * 6,
+        out_specs=[pl.BlockSpec(memory_space=pltpu.VMEM)] * 5,
         scratch_shapes=[ext] * 8
         + [pltpu.VMEM((layers + 1, ext_rows, ext_cols), F32)]
         + [ext] * 6
@@ -895,10 +898,14 @@
     )(*operands)
 
 
-def hand_over(*refs):
-    count = len(refs) // 2
+def hand_over(new, adjoint, slope, sums, o_new, o_adjoint, o_slope, o_cost, o_misfit, cost, misfit, sem):
+    cost[...] = sums[0:1, 0:1]
+    misfit[...] = sums[1:2, 0:1]
     copies = [
-        pltpu.make_async_copy(refs[k], refs[count + k], refs[-1].at[k]) for k in range(count)
+        pltpu.make_async_copy(src_ref, dst_ref, sem.at[k])
+        for k, (src_ref, dst_ref) in enumerate((
+            (new, o_new), (adjoint, o_adjoint), (slope, o_slope), (cost, o_cost), (misfit, o_misfit),
+        ))
     ]
     for copy in copies:
         copy.start()
@@ -906,16 +913,18 @@
         copy.wait()
 
 
-def run_hand_over(values):
+def run_hand_over(new, adjoint, slope, sums):
+    block = jax.ShapeDtypeStruct(new.shape, F32)
+    one = jax.ShapeDtypeStruct((1, 1), F32)
     return pl.pallas_call(
         hand_over,
-        out_shape=[jax.ShapeDtypeStruct(v.shape, v.dtype) for v in values],
-        in_specs=[pl.BlockSpec(memory_space=pltpu.VMEM)] * len(values),
-        out_specs=[pl.BlockSpec(memory_space=pltpu.HBM)] * len(values),
-        scratch_shapes=[pltpu.SemaphoreType.DMA((len(values),))],
+        out_shape=[block, block, jax.ShapeDtypeStruct(slope.shape, F32), one, one],
+        in_specs=[pl.BlockSpec(memory_space=pltpu.VMEM)] * 4,
+        out_specs=[pl.BlockSpec(memory_space=pltpu.HBM)] * 5,
+        scratch_shapes=[pltpu.VMEM((1, 1), F32)] * 2 + [pltpu.SemaphoreType.DMA((5,))],
         compiler_params=pltpu.CompilerParams(vmem_limit_bytes=8 * 1024 * 1024),
         name="hand_over",
-    )(*values)
+    )(new, adjoint, slope, sums)
 
 
 def in_order(value):
@@ -926,8 +935,8 @@
     fields = arguments[:6]
     e, n, top, bottom, tariff, rates, ground, prices = arguments[6:]
     wells = [w.reshape(1, -1) for w in (e, n, top, bottom, rates, tariff, ground, prices)]
-    new, adjoint, slope, cost, misfit, crowded = run_kernel(sizes, fields, wells)
-    found = tuple(run_hand_over((new, adjoint, slope, cost, misfit)))
+    *results, crowded = run_kernel(sizes, fields, wells)
+    found = tuple(run_hand_over(*results))
 
     def again(state):
         blocks = [in_order(x) for x in fields]

time: 45.2 us -> 43.8 us (0.969)
  Pallas kernels: 43.4 us -> 42 us
    pallas_call x1, Pallas kernels: 2.33 us -> 1.02 us  [run_hand_over(): pl.pallas_call(hand_over, out_shape=[block, block, jax.ShapeDtypeStruct(s...]
where the time goes in v9:
time: 43.8 us; the launch traced here: 43.6 us
  Pallas kernels  42 us (96%)
  between operations  0.89 us (2%)
  loops' own time  0.73 us (2%)
    pallas_call x1, Pallas kernels, run_kernel(): pl.pallas_call(functools.partial(kernel, sizes), out_shape=[block, block,...  41 us
    pallas_call x1, Pallas kernels, run_hand_over(): pl.pallas_call(hand_over, out_shape=[block, block, jax.ShapeDtypeStruct(s...  1.02 us

profile of v9, /device:TPU:0, one launch (start us, length us, event | category | flops | bytes accessed | tf_op | source)
XLA Modules:
  0.0 43.6 jit_solution(6807997553857364762)
XLA Ops:
  0.6 0.0 copy-start.26
  0.6 0.0 copy-start.15
  0.7 0.0 copy-start.13
  0.7 0.0 copy-start.9
  0.7 0.0 copy-start
  0.7 41.0 %whole_step.1 = (f32[4,128,256]{2,1,0:T(8,128)S(1)}, f32[4,128,256]{2,1,0:T(8,128)S(1)}, f32[1,3000]{1,0:T(1,128)S(1)}, f32[8,128]{1,0:T(8,128)S(1)}, f32[1,1]{1,0:T(1,128)}) custom-call(f32[4,128,256]{2,1,0:T(8,128)} %refs_0_.1, f32[4,128,256]{2,1,0:T(8,128)} %refs_1_.1, bf16[4,128,256]{2,1,0:T(8,128)(2,1)} %refs_2_.1, bf16[4,128,256]{2,1,0:T(8,128)(2,1)} %refs_3_.1, ...), custom_call_target="tpu_custom_call" | custom-call | tf_op jit(solution)/shard_map/whole_step/pallas_call | solution.py:861
  41.7 1.0 %hand_over.1 = (f32[4,128,256]{2,1,0:T(8,128)}, f32[4,128,256]{2,1,0:T(8,128)}, f32[1,3000]{1,0:T(1,128)}, f32[1,1]{1,0:T(1,128)}, f32[1,1]{1,0:T(1,128)}) custom-call(f32[4,128,256]{2,1,0:T(8,128)S(1)} %get-tuple-element.116.new, f32[4,128,256]{2,1,0:T(8,128)S(1)} %get-tuple-element.117.adjoint, f32[1,3000]{1,0:T(1,128)S(1)} %get-tuple-element.118.slope, ...), custom_call_target="tpu_custom_call" | custom-call | tf_op jit(solution)/shard_map/hand_over/pallas_call | solution.py:919
  42.7 0.0 copy-done.26
  42.7 0.0 copy-done.15
  42.7 0.0 copy-done.13
  42.7 0.0 copy-done.9
  42.7 0.0 copy-done
  42.8 0.7 %while.17 = (f32[]{:T(128)}, f32[4,128,256]{2,1,0:T(8,128)}, f32[4,128,256]{2,1,0:T(8,128)}, f32[1,3000]{1,0:T(1,128)}, f32[1,1]{1,0:T(1,128)}, /*index=5*/f32[1...) while((f32[]{:T(128)}, f32[4,128,256]{2,1,0:T(8,128)}, ...), condition=%region_13.14_spmd, body=%region_0.13_spmd | while | flops 59988996 | bytes 132797736 | solution.py:947
Async XLA Ops:
  0.6 42.1 %copy-start.26 = (f32[3000]{0:T(1024)S(1)}, f32[3000]{0:T(1024)}, u32[]{:S(2)}) copy-start(f32[3000]{0:T(1024)} %param.27) | copy-start | bytes 36004
  0.6 42.1 %copy-start.15 = (bf16[4,128,256]{2,1,0:T(8,128)(2,1)S(1)}, bf16[4,128,256]{2,1,0:T(8,128)(2,1)}, u32[]{:S(2)}) copy-start(bf16[4,128,256]{2,1,0:T(8,128)(2,1)} %refs_4_.1) | copy-start | bytes 786436
  0.7 42.1 %copy-start.13 = (bf16[4,128,256]{2,1,0:T(8,128)(2,1)S(1)}, bf16[4,128,256]{2,1,0:T(8,128)(2,1)}, u32[]{:S(2)}) copy-start(bf16[4,128,256]{2,1,0:T(8,128)(2,1)} %refs_3_.1) | copy-start | bytes 786436
  0.7 42.1 %copy-start.9 = (bf16[4,128,256]{2,1,0:T(8,128)(2,1)S(1)}, bf16[4,128,256]{2,1,0:T(8,128)(2,1)}, u32[]{:S(2)}) copy-start(bf16[4,128,256]{2,1,0:T(8,128)(2,1)} %refs_2_.1) | copy-start | bytes 786436
  0.7 42.1 %copy-start = (f32[4,128,256]{2,1,0:T(8,128)S(1)}, f32[4,128,256]{2,1,0:T(8,128)}, u32[]{:S(2)}) copy-start(f32[4,128,256]{2,1,0:T(8,128)} %refs_0_.1) | copy-start | bytes 1572868

commit v10 on v9

--- a/solution.py
+++ b/solution.py
@@ -256,8 +256,8 @@
     fields, well_refs, refs = refs[:6], refs[6:14], refs[14:]
     head_new, adjoint, out_slope, out_sums, out_crowded = refs[:5]
     hx, tx, ke, kn, kv, st, fe, fn, fu, inv, src, lw, d0, d1, s1, pt = refs[5:21]
-    parts, staged, (nbs, efs, ebs, cfs, cbs), refs = refs[21], refs[22:26], refs[26:31], refs[31:]
-    (s_nf, s_nb, s_ef, s_eb, s_cf, s_cb), refs = refs[:6], refs[6:]
+    parts, staged, (nbs, efs, ebs, cfs), refs = refs[21], refs[22:26], refs[26:30], refs[30:]
+    (s_nf, s_nb, s_ef, s_eb, s_cf), refs = refs[:5], refs[5:]
     well_rows, wells, boxes, refs = refs[:8], refs[8], refs[9:13], refs[13:]
     load_sem, send_sem, recv_sem, sum_send, sum_recv = refs
     depth, rows, cols = head_new.shape
@@ -288,9 +288,8 @@
     ):
         phases.append((box, mine, [device(lax.rem(mine + k, size)) for k in range(1, size)]))
 
-    greeted = [partner] + to_north + to_east + to_corner
-    for _, _, peers in phases:
-        greeted = greeted + peers
+    z_peers, east_peers, x_peers = (peers for _, _, peers in phases[1:])
+    greeted = to_corner + to_north + x_peers + z_peers + east_peers[1:-1] + to_east + [partner]
     barrier = pltpu.get_barrier_semaphore()
     for device in greeted:
         pl.semaphore_signal(barrier, inc=1, device_id=device, device_id_type=MESH)
@@ -385,8 +384,7 @@
                         pieces[8 * half:8 * half + 8], HALO * slot - (LANES - HALO) * c, 1
                     )
                     mixed = jnp.where(group == slot, moved, mixed)
-            s_cf[2 * r + c] = kept
-            s_cb[2 * r + c] = jnp.concatenate([mixed, mixed], axis=0).astype(BF16)
+            s_cf[2 * r + c] = jnp.concatenate([kept, mixed], axis=0)
 
     pl.semaphore_wait(barrier, len(greeted))
 
@@ -411,12 +409,11 @@
         norths.append(
             send(s_nf.at[side], hx.at[own_layers, edge_rows[side], inside_cols], to_north[side])
         )
+    for d in range(4):
+        corners.append(send(s_cf.at[d], cfs.at[0, d], to_corner[d]))
     for side in (0, 1):
         easts.append(send(s_eb.at[side], ebs.at[0, side], to_east[side]))
         easts.append(send(s_ef.at[side], efs.at[0, side], to_east[side]))
-    for d in range(4):
-        corners.append(send(s_cb.at[d], cbs.at[0, d], to_corner[d]))
-        corners.append(send(s_cf.at[d], cfs.at[0, d], to_corner[d]))
     two = (depth - 2) * (1 - me_l)
     blocks = [send(fields[2 + a], staged[a].at[own_layers], partner) for a in range(4)]
     blocks.append(send(fields[0], hx.at[own_layers, inner, inside_cols], partner))
@@ -542,9 +539,8 @@
 
     def fill_corners(who, base):
         for side, at_rows in enumerate(edge_rows):
-            right, left = cfs[who, 2 * side], cfs[who, 2 * side + 1]
-            rights = cbs[who, 2 * side].astype(F32)[:8]
-            lefts = cbs[who, 2 * side + 1].astype(F32)[:8]
+            right, rights = cfs[who, 2 * side, :8], cfs[who, 2 * side, 8:]
+            left, lefts = cfs[who, 2 * side + 1, :8], cfs[who, 2 * side + 1, 8:]
 
             def taken(a, b, slot):
                 return jnp.where(
@@ -669,7 +665,6 @@
     for copy in corners:
         copy.wait_recv()
     forwards.append(send(cfs.at[0], cfs.at[1], partner))
-    forwards.append(send(cbs.at[0], cbs.at[1], partner))
     fill_north(0, own)
     fill_corners(0, own)
     start_layers(0, depth - 1, False)
@@ -856,7 +851,7 @@
     block = pltpu.VMEM((depth, rows, cols), F32)
     ext = pltpu.VMEM((layers, ext_rows, ext_cols), F32)
     operands = (*fields, *wells)
-    copies = 4 + 4 + 8 + 6 + 7
+    copies = 4 + 4 + 4 + 6 + 6
     peers = 1 + n_z + n_east + n_x - 3
     return pl.pallas_call(
         functools.partial(kernel, sizes),
@@ -876,14 +871,12 @@
             pltpu.VMEM((2, 2, depth, 16, cols), BF16),
             pltpu.VMEM((2, 2, depth, 8, LANES), F32),
             pltpu.VMEM((2, 2, depth, 32, LANES), BF16),
-            pltpu.VMEM((2, 4, 8, LANES), F32),
-            pltpu.VMEM((2, 4, 16, LANES), BF16),
+            pltpu.VMEM((2, 4, 16, LANES), F32),
             pltpu.VMEM((2, depth, 8, cols), F32),
             pltpu.VMEM((2, depth, 16, cols), BF16),
             pltpu.VMEM((2, depth, 8, LANES), F32),
             pltpu.VMEM((2, depth, 32, LANES), BF16),
-            pltpu.VMEM((4, 8, LANES), F32),
-            pltpu.VMEM((4, 16, LANES), BF16),
+            pltpu.VMEM((4, 16, LANES), F32),
         ]
         + [pltpu.VMEM(w.shape, w.dtype) for w in wells]
         + [pltpu.VMEM((8, groups * LANES), F32)]

time: 43.8 us -> 43.7 us (level)
  no operation moved by 1% of the time
where the time goes in v10:
time: 43.7 us; the launch traced here: 43.5 us
  Pallas kernels  41.9 us (96%)
  between operations  0.89 us (2%)
  loops' own time  0.73 us (2%)
    pallas_call x1, Pallas kernels, run_kernel(): pl.pallas_call(functools.partial(kernel, sizes), out_shape=[block, block,...  40.9 us
    pallas_call x1, Pallas kernels, run_hand_over(): pl.pallas_call(hand_over, out_shape=[block, block, jax.ShapeDtypeStruct(s...  1.02 us

profile of v10, /device:TPU:0, one launch (start us, length us, event | category | flops | bytes accessed | tf_op | source)
XLA Modules:
  0.0 43.5 jit_solution(12783359140321812426)
XLA Ops:
  0.6 0.0 copy-start.26
  0.6 0.0 copy-start.15
  0.7 0.0 copy-start.13
  0.7 0.0 copy-start.9
  0.7 0.0 copy-start
  0.7 40.9 %whole_step.1 = (f32[4,128,256]{2,1,0:T(8,128)S(1)}, f32[4,128,256]{2,1,0:T(8,128)S(1)}, f32[1,3000]{1,0:T(1,128)S(1)}, f32[8,128]{1,0:T(8,128)S(1)}, f32[1,1]{1,0:T(1,128)}) custom-call(f32[4,128,256]{2,1,0:T(8,128)} %refs_0_.1, f32[4,128,256]{2,1,0:T(8,128)} %refs_1_.1, bf16[4,128,256]{2,1,0:T(8,128)(2,1)} %refs_2_.1, bf16[4,128,256]{2,1,0:T(8,128)(2,1)} %refs_3_.1, ...), custom_call_target="tpu_custom_call" | custom-call | tf_op jit(solution)/shard_map/whole_step/pallas_call | solution.py:856
  41.5 1.0 %hand_over.1 = (f32[4,128,256]{2,1,0:T(8,128)}, f32[4,128,256]{2,1,0:T(8,128)}, f32[1,3000]{1,0:T(1,128)}, f32[1,1]{1,0:T(1,128)}, f32[1,1]{1,0:T(1,128)}) custom-call(f32[4,128,256]{2,1,0:T(8,128)S(1)} %get-tuple-element.116.new, f32[4,128,256]{2,1,0:T(8,128)S(1)} %get-tuple-element.117.adjoint, f32[1,3000]{1,0:T(1,128)S(1)} %get-tuple-element.118.slope, ...), custom_call_target="tpu_custom_call" | custom-call | tf_op jit(solution)/shard_map/hand_over/pallas_call | solution.py:912
  42.6 0.0 copy-done.26
  42.6 0.0 copy-done.15
  42.6 0.0 copy-done.13
  42.6 0.0 copy-done.9
  42.6 0.0 copy-done
  42.6 0.7 %while.17 = (f32[]{:T(128)}, f32[4,128,256]{2,1,0:T(8,128)}, f32[4,128,256]{2,1,0:T(8,128)}, f32[1,3000]{1,0:T(1,128)}, f32[1,1]{1,0:T(1,128)}, /*index=5*/f32[1...) while((f32[]{:T(128)}, f32[4,128,256]{2,1,0:T(8,128)}, ...), condition=%region_13.14_spmd, body=%region_0.13_spmd | while | flops 59988996 | bytes 132797736 | solution.py:940
Async XLA Ops:
  0.6 41.9 %copy-start.26 = (f32[3000]{0:T(1024)S(1)}, f32[3000]{0:T(1024)}, u32[]{:S(2)}) copy-start(f32[3000]{0:T(1024)} %param.27) | copy-start | bytes 36004
  0.6 41.9 %copy-start.15 = (bf16[4,128,256]{2,1,0:T(8,128)(2,1)S(1)}, bf16[4,128,256]{2,1,0:T(8,128)(2,1)}, u32[]{:S(2)}) copy-start(bf16[4,128,256]{2,1,0:T(8,128)(2,1)} %refs_4_.1) | copy-start | bytes 786436
  0.7 41.9 %copy-start.13 = (bf16[4,128,256]{2,1,0:T(8,128)(2,1)S(1)}, bf16[4,128,256]{2,1,0:T(8,128)(2,1)}, u32[]{:S(2)}) copy-start(bf16[4,128,256]{2,1,0:T(8,128)(2,1)} %refs_3_.1) | copy-start | bytes 786436
  0.7 41.9 %copy-start.9 = (bf16[4,128,256]{2,1,0:T(8,128)(2,1)S(1)}, bf16[4,128,256]{2,1,0:T(8,128)(2,1)}, u32[]{:S(2)}) copy-start(bf16[4,128,256]{2,1,0:T(8,128)(2,1)} %refs_2_.1) | copy-start | bytes 786436
  0.7 41.9 %copy-start = (f32[4,128,256]{2,1,0:T(8,128)S(1)}, f32[4,128,256]{2,1,0:T(8,128)}, u32[]{:S(2)}) copy-start(f32[4,128,256]{2,1,0:T(8,128)} %refs_0_.1) | copy-start | bytes 1572868

commit v11 on v10

--- a/solution.py
+++ b/solution.py
@@ -656,6 +656,9 @@
         copy.wait_recv()
     forwards = [send(efs.at[0], efs.at[1], partner), send(ebs.at[0], ebs.at[1], partner)]
     fill_east(0, own)
+    for copy in blocks:
+        copy.wait_recv()
+    fill_inner(other)
     for copy in norths:
         copy.wait_recv()
     forwards.append(send(nbs.at[0], nbs.at[1], partner))
@@ -668,9 +671,6 @@
     fill_north(0, own)
     fill_corners(0, own)
     start_layers(0, depth - 1, False)
-    for copy in blocks:
-        copy.wait_recv()
-    fill_inner(other)
     for copy in forwards:
         copy.wait_recv()
     fill_east(1, other)

time: 43.7 us -> 43.5 us (level)
  no operation moved by 1% of the time
where the time goes in v11:
time: 43.5 us; the launch traced here: 43.4 us
  Pallas kernels  41.7 us (96%)
  between operations  0.89 us (2%)
  loops' own time  0.73 us (2%)
    pallas_call x1, Pallas kernels, run_kernel(): pl.pallas_call(functools.partial(kernel, sizes), out_shape=[block, block,...  40.7 us
    pallas_call x1, Pallas kernels, run_hand_over(): pl.pallas_call(hand_over, out_shape=[block, block, jax.ShapeDtypeStruct(s...  1.02 us

profile of v11, /device:TPU:0, one launch (start us, length us, event | category | flops | bytes accessed | tf_op | source)
XLA Modules:
  0.0 43.4 jit_solution(12146517739389563200)
XLA Ops:
  0.6 0.0 copy-start.26
  0.6 0.0 copy-start.15
  0.7 0.0 copy-start.13
  0.7 0.0 copy-start.9
  0.7 0.0 copy-start
  0.7 40.7 %whole_step.1 = (f32[4,128,256]{2,1,0:T(8,128)S(1)}, f32[4,128,256]{2,1,0:T(8,128)S(1)}, f32[1,3000]{1,0:T(1,128)S(1)}, f32[8,128]{1,0:T(8,128)S(1)}, f32[1,1]{1,0:T(1,128)}) custom-call(f32[4,128,256]{2,1,0:T(8,128)} %refs_0_.1, f32[4,128,256]{2,1,0:T(8,128)} %refs_1_.1, bf16[4,128,256]{2,1,0:T(8,128)(2,1)} %refs_2_.1, bf16[4,128,256]{2,1,0:T(8,128)(2,1)} %refs_3_.1, ...), custom_call_target="tpu_custom_call" | custom-call | tf_op jit(solution)/shard_map/whole_step/pallas_call | solution.py:856
  41.4 1.0 %hand_over.1 = (f32[4,128,256]{2,1,0:T(8,128)}, f32[4,128,256]{2,1,0:T(8,128)}, f32[1,3000]{1,0:T(1,128)}, f32[1,1]{1,0:T(1,128)}, f32[1,1]{1,0:T(1,128)}) custom-call(f32[4,128,256]{2,1,0:T(8,128)S(1)} %get-tuple-element.116.new, f32[4,128,256]{2,1,0:T(8,128)S(1)} %get-tuple-element.117.adjoint, f32[1,3000]{1,0:T(1,128)S(1)} %get-tuple-element.118.slope, ...), custom_call_target="tpu_custom_call" | custom-call | tf_op jit(solution)/shard_map/hand_over/pallas_call | solution.py:912
  42.4 0.0 copy-done.26
  42.4 0.0 copy-done.15
  42.4 0.0 copy-done.13
  42.4 0.0 copy-done.9
  42.5 0.0 copy-done
  42.5 0.7 %while.17 = (f32[]{:T(128)}, f32[4,128,256]{2,1,0:T(8,128)}, f32[4,128,256]{2,1,0:T(8,128)}, f32[1,3000]{1,0:T(1,128)}, f32[1,1]{1,0:T(1,128)}, /*index=5*/f32[1...) while((f32[]{:T(128)}, f32[4,128,256]{2,1,0:T(8,128)}, ...), condition=%region_13.14_spmd, body=%region_0.13_spmd | while | flops 59988996 | bytes 132797736 | solution.py:940
Async XLA Ops:
  0.6 41.8 %copy-start.26 = (f32[3000]{0:T(1024)S(1)}, f32[3000]{0:T(1024)}, u32[]{:S(2)}) copy-start(f32[3000]{0:T(1024)} %param.27) | copy-start | bytes 36004
  0.6 41.8 %copy-start.15 = (bf16[4,128,256]{2,1,0:T(8,128)(2,1)S(1)}, bf16[4,128,256]{2,1,0:T(8,128)(2,1)}, u32[]{:S(2)}) copy-start(bf16[4,128,256]{2,1,0:T(8,128)(2,1)} %refs_4_.1) | copy-start | bytes 786436
  0.7 41.8 %copy-start.13 = (bf16[4,128,256]{2,1,0:T(8,128)(2,1)S(1)}, bf16[4,128,256]{2,1,0:T(8,128)(2,1)}, u32[]{:S(2)}) copy-start(bf16[4,128,256]{2,1,0:T(8,128)(2,1)} %refs_3_.1) | copy-start | bytes 786436
  0.7 41.8 %copy-start.9 = (bf16[4,128,256]{2,1,0:T(8,128)(2,1)S(1)}, bf16[4,128,256]{2,1,0:T(8,128)(2,1)}, u32[]{:S(2)}) copy-start(bf16[4,128,256]{2,1,0:T(8,128)(2,1)} %refs_2_.1) | copy-start | bytes 786436
  0.7 41.8 %copy-start = (f32[4,128,256]{2,1,0:T(8,128)S(1)}, f32[4,128,256]{2,1,0:T(8,128)}, u32[]{:S(2)}) copy-start(f32[4,128,256]{2,1,0:T(8,128)} %refs_0_.1) | copy-start | bytes 1572868
